TPU v7x, 512 devices: a whole 4x8x8 slice. The times are simulated.
512 devices in a mesh: chan: 8 (over x, z_hi), tile: 64 (over y, z_lo, core).
Axes of the slice: x: 4, y: 8, z: 8 (z_hi: 2, z_lo: 4; z = z_hi * 4 + z_lo), core: 2. Of those that a mesh axis runs over, the one named last changes fastest.
Arguments:
- latent: bfloat16 [2, 256, 512, 128], P(None, 'tile', 'chan'), may hold values from -6 to 6
- kernel: bfloat16 [3, 3, 3, 512, 2048], P(None, None, None, 'chan', 'tile'), may hold values from -0.0546875 to 0.0546875
- bias: float32 [2048], replicated, may hold values from -3 to 3
Outputs:
- upsampled: bfloat16 [2, 512, 512, 256], P(None, ('tile', 'chan'))
All inputs are finite; a program needn't handle non-finite values.
Results may differ from a plain program's by a relative error of at most 0.015.
Values may be sent and summed in bfloat16 or wider, within the bound.
No kernel may reach another device: no remote copies, remote signals or barrier semaphores. Data moves between devices by JAX's collectives and lax.ppermute only.
A program may use at most 128 MiB of HBM per device.

v0:
```python
import jax
import jax.numpy as jnp
from jax import lax
from jax.sharding import PartitionSpec as P


def extended_2(shard, sides, width):
    for axis, dim in sides:
        count, length = (lax.axis_size(axis), shard.shape[dim])
        up = [(i, (i + 1) % count) for i in range(count - 1)]
        down = [(j, i) for i, j in up]
        last = lax.slice_in_dim(shard, length - width, length, axis=dim)
        leading = lax.slice_in_dim(shard, 0, width, axis=dim)
        before = lax.ppermute(last, axis, up)
        after = lax.ppermute(leading, axis, down)
        shard = jnp.concatenate([before, shard, after], axis=dim)
    return shard


def extend_local(padded):
    first = padded[:1]
    timed = jnp.concatenate([first, first, padded], axis=0)
    return jnp.pad(timed, ((0, 0), (0, 0), (0, 0), (1, 1)))


def stack_windows(extended):
    frames = extended.shape[0] - 2
    rows = extended.shape[1] - 2
    cols = extended.shape[3] - 2
    windows = []
    for tap_t in range(3):
        for tap_h in range(3):
            for tap_w in range(3):
                windows.append(
                    extended[tap_t : tap_t + frames, tap_h : tap_h + rows, :, tap_w : tap_w + cols]
                )
    return jnp.concatenate(windows, axis=2)


def conv_taps(stacked, kernel):
    flat_kernel = kernel.reshape(-1, kernel.shape[-1])
    return jnp.einsum("thkw,ko->thow", stacked, flat_kernel, preferred_element_type=jnp.float32)


def shuffle(conv):
    frames, rows, chans, cols = conv.shape
    split = conv.reshape(frames, rows, chans // 4, 2, 2, cols)
    moved = jnp.transpose(split, (0, 1, 3, 2, 5, 4))
    return moved.reshape(frames, rows * 2, chans // 4, cols * 2)


def local(latent, kernel, bias):
    padded = extended_2(latent, (("tile", 1),), 1)
    chan_index = lax.axis_index("chan")
    stacked = stack_windows(extend_local(padded))
    terms = conv_taps(stacked, lax.all_gather(kernel, "tile", axis=4, tiled=True))
    summed = lax.psum_scatter(
        terms.astype(jnp.bfloat16), "chan", scatter_dimension=2, tiled=True
    ).astype(jnp.float32)
    block = summed.shape[2]
    bias_part = lax.dynamic_slice_in_dim(bias, chan_index * block, block)
    conv = (summed + bias_part[None, None, :, None]).astype(jnp.bfloat16)
    shuffled = shuffle(conv)
    strips = lax.all_to_all(shuffled, "chan", split_axis=1, concat_axis=2, tiled=True)
    return strips


def solution(mesh):
    placed = (P(None, "tile", "chan", None), P(None, None, None, "chan", "tile"), P())
    return jax.shard_map(
        local,
        mesh=mesh,
        in_specs=placed,
        out_specs=P(None, ("tile", "chan"), None, None),
        check_vma=False,
    )
```

profile of v0, /device:TPU:1, one launch (start us, length us, event | category | flops | bytes accessed | tf_op | source)
XLA Modules:
  0.0 328.5 jit_solution(10013070709011095792)
XLA Ops:
  6.5 0.7 all-gather.2.cloned.1.call-update
  7.3 0.8 fusion.18
  8.1 5.5 %collective-permute-start = (bf16[2,1,64,128]{3,2,1,0:T(8,128)(2,1)S(1)}, bf16[2,1,64,128]{3,2,1,0:T(8,128)(2,1)S(1)}, u32[]{:S(2)}, u32[]{:S(2)}) collective-permute-start(bf16[2,1,64,128]{3,2,1,0:T(8,128)(2,1)S(1)} %get-tuple-element.6), channel_id=1, source_target_pairs={{0,1},{1,2},{2,3},{3,4},{4,5},{5,6},{6,7},{7,8},{8,9},{9,10},{10,1... | collective-permute-start | bytes 98312 | tf_op jit(solution)/shard_map/ppermute | solution.py:14
  13.6 4.7 %collective-permute-start.1 = (bf16[2,1,64,128]{3,2,1,0:T(8,128)(2,1)S(1)}, bf16[2,1,64,128]{3,2,1,0:T(8,128)(2,1)S(1)}, u32[]{:S(2)}, u32[]{:S(2)}) collective-permute-start(bf16[2,1,64,128]{3,2,1,0:T(8,128)(2,1)S(1)} %get-tuple-element.5), channel_id=1, source_target_pairs={{1,0},{2,1},{3,2},{4,3},{5,4},{6,5},{7,6},{8,7},{9,8},{10,9},{11,1... | collective-permute-start | bytes 98312 | tf_op jit(solution)/shard_map/ppermute | solution.py:15
  18.3 0.9 constant_dynamic-update-slice_fusion.1
  19.3 0.3 fusion.5
  19.7 0.1 slice_dynamic-update-slice_fusion.16
  19.9 0.1 slice_dynamic-update-slice_fusion.14
  20.1 0.1 slice_dynamic-update-slice_fusion.12
  20.3 0.1 slice_dynamic-update-slice_fusion.10
  20.5 0.1 slice_dynamic-update-slice_fusion.8
  20.7 0.1 slice_dynamic-update-slice_fusion.6
  21.3 0.1 slice_dynamic-update-slice_fusion
  21.5 127.7 %all-gather.2.cloned.1.call-done = bf16[3,3,3,64,2048]{3,4,2,1,0:T(8,128)(2,1)} async-done(((bf16[3,3,3,64,32]{3,4,2,1,0:T(8,128)(2,1)}), bf16[3,3,3,64,2048]{3,4,2,1,0:T(8,128)(2,1)}) %all-gather.2.cloned.1.call-update) | async-done | bytes 7077904 | tf_op jit(solution)/shard_map/all_gather | solution.py:56
  149.1 14.9 %copy.13 = bf16[3,3,3,64,2048]{4,3,2,1,0:T(8,128)(2,1)} copy(bf16[3,3,3,64,2048]{3,4,2,1,0:T(8,128)(2,1)} %all-gather.2.cloned.1.call-done) | data formatting | bytes 14155776 | tf_op jit(solution)/shard_map/all_gather | solution.py:56
  164.1 11.4 %convert_bitcast_fusion = bf16[2,4,2048,128]{2,3,1,0:T(8,128)(2,1)} fusion(bf16[2,4,1728,128]{3,2,1,0:T(8,128)(2,1)S(1)} %slice_dynamic-update-slice_fusion, bf16[1728,2048,1,1]{1,0,3,2:T(8,128)(2,1)} %bitcast.16), kind=kOutput, calls=%fused_computation | convolution fusion | flops 7249854464 | bytes 14811136 | tf_op jit(solution)/shard_map/thkw,ko->thow/dot_general | solution.py:42
  175.5 0.8 dynamic_slice.3
  176.2 128.0 %reduce-scatter.2.cloned.1.call-done = bf16[2,4,256,128]{2,3,1,0:T(8,128)(2,1)} async-done(((bf16[2,4,2048,128]{2,3,1,0:T(8,128)(2,1)}), bf16[2,4,256,128]{2,3,1,0:T(8,128)(2,1)}) %reduce-scatter.2.cloned.1.call-update) | async-done | bytes 524304 | tf_op jit(solution)/shard_map/reduce_scatter | solution.py:57
  304.3 1.1 add_convert_fusion
  305.4 0.3 copy.14
  305.7 0.8 copy.15
  306.5 0.3 copy.16
  306.8 14.0 %all_to_all.12 = bf16[2,8,64,256]{3,2,0,1:T(8,128)(2,1)S(1)} all-to-all(bf16[2,8,64,256]{3,2,0,1:T(8,128)(2,1)S(1)} %copy.16), channel_id=1, replica_groups=mesh['chan'=8,'tile'=64] {'chan'}, dimensions={1} | all-to-all | bytes 1048576 | tf_op jit(solution)/shard_map/all_to_all | solution.py:64
  320.8 0.8 copy.17
  (30 shorter events, 0.8 us)
Async XLA Ops:
  6.5 142.6 %all-gather.2.cloned.1.call-start = ((), (), s32[]{:S(2)}) async-start(), calls=%async_computation.2 | async-start | bytes 14376960 | tf_op jit(solution)/shard_map/all_gather | solution.py:56
  7.3 297.0 %reduce-scatter.2.cloned.1.call-start = ((), (), s32[]{:S(2)}) async-start(), calls=%async_computation.3 | async-start | bytes 4718592 | tf_op jit(solution)/shard_map/reduce_scatter | solution.py:57
  8.1 12.8 %copy-start = (bf16[2,4,64,128]{3,2,1,0:T(8,128)(2,1)S(1)}, bf16[2,4,64,128]{3,2,1,0:T(8,128)(2,1)}, u32[]{:S(2)}) copy-start(bf16[2,4,64,128]{3,2,1,0:T(8,128)(2,1)} %param.3) | copy-start | bytes 393220
  8.1 10.2 %collective-permute-start = (bf16[2,1,64,128]{3,2,1,0:T(8,128)(2,1)S(1)}, bf16[2,1,64,128]{3,2,1,0:T(8,128)(2,1)S(1)}, u32[]{:S(2)}, u32[]{:S(2)}) collective-permute-start(bf16[2,1,64,128]{3,2,1,0:T(8,128)(2,1)S(1)} %get-tuple-element.6), channel_id=1, source_target_pairs={{0,1},{1,2},{2,3},{3,4},{4,5},{5,6},{6,7},{7,8},{8,9},{9,10},{10,1... | collective-permute-start | bytes 98312 | tf_op jit(solution)/shard_map/ppermute | solution.py:14
  13.6 5.6 %collective-permute-start.1 = (bf16[2,1,64,128]{3,2,1,0:T(8,128)(2,1)S(1)}, bf16[2,1,64,128]{3,2,1,0:T(8,128)(2,1)S(1)}, u32[]{:S(2)}, u32[]{:S(2)}) collective-permute-start(bf16[2,1,64,128]{3,2,1,0:T(8,128)(2,1)S(1)} %get-tuple-element.5), channel_id=1, source_target_pairs={{1,0},{2,1},{3,2},{4,3},{5,4},{6,5},{7,6},{8,7},{9,8},{10,9},{11,1... | collective-permute-start | bytes 98312 | tf_op jit(solution)/shard_map/ppermute | solution.py:15
Sparse Core Ops, SparseCore 0:
  9.5 139.5 all-gather.1
  175.6 128.6 reduce-scatter.1
where the time goes:
time: 335 us; the launch traced here: 328 us
  waiting for transfers between devices  256 us (76%)
  local copies, waits for them, and re-layouts  21.1 us (6%)
  blocking collectives  14 us (4%)
  between operations  13.7 us (4%)
  matrix products  11.4 us (3%)
  starting transfers between devices  10.2 us (3%)
    reduce_scatter x1, waiting for transfers between devices, local(): lax.psum_scatter(terms.astype(jnp.bfloat16), 'chan', scatter_dimension=2,...  128 us
    all_gather x1, waiting for transfers between devices, local(): lax.all_gather(kernel, 'tile', axis=4, tiled=True)  128 us
    all_gather x1, local copies, waits for them, and re-layouts, local(): lax.all_gather(kernel, 'tile', axis=4, tiled=True)  14.9 us
    all_to_all x1, blocking collectives, local(): lax.all_to_all(shuffled, 'chan', split_axis=1, concat_axis=2, tiled=True)  14 us
    dot_general x1, matrix products, conv_taps(): jnp.einsum('thkw,ko->thow', stacked, flat_kernel, preferred_element_type=...  11.4 us
  transfers between devices with their start and end apart: 4, of which 2 were waited for; matrix products, arithmetic and copies ran while one was open for 1% of the time, Pallas kernels for 0%

commit v1 on v0

v1 whole, which is shorter than its diff:
```python
import functools

import jax
import jax.numpy as jnp
from jax import lax
from jax.experimental import pallas as pl
from jax.experimental.pallas import tpu as pltpu
from jax.sharding import Mesh, PartitionSpec as P

AXES = ("x", "zh", "y", "zl", "k")
SIZES = (4, 2, 8, 4, 2)
NX, NH, NY, NL, NK = SIZES


def ring(size, step):
    return [(i, (i + step) % size) for i in range(size)]


def spread_kernel(kernel):
    k01 = (kernel[0].astype(jnp.float32) + kernel[1].astype(jnp.float32)).astype(kernel.dtype)
    both = jnp.stack([k01, kernel[2]])
    split = both.reshape(2, 3, 3, 64, NX, 2, 2, 2)
    moved = jnp.transpose(split, (4, 6, 1, 2, 7, 5, 0, 3))
    flat = moved.reshape(NX, NH, 1, 3, 3, 2, 2, 128)
    return jnp.broadcast_to(flat, (NX, NH, NL, 3, 3, 2, 2, 128))


def own_chunk(kernel):
    pieces = spread_kernel(kernel).reshape(NX * NH * NL, 3, 3, 2, 2, 128)
    got = lax.all_to_all(pieces, ("x", "zh", "zl"), 0, 0, tiled=True)
    got = got.reshape(NX * NH, NL, 3, 3, 2, 2, 128)
    return jnp.transpose(got, (2, 3, 4, 1, 5, 0, 6)).reshape(3, 3, 16, 1024)


def own_rows(latent):
    core = lax.axis_index("k")
    rows = jnp.transpose(latent, (1, 0, 2, 3))
    edge = jnp.where(core == 0, rows[:1], rows[3:])
    pairs = [(2 * i + 1, 2 * i + 2) for i in range(31)]
    halo = lax.ppermute(edge, ("y", "zl", "k"), pairs + [(b, a) for a, b in pairs])
    return jnp.concatenate([rows, halo], axis=0)


def conv_kernel(
    at_ref, own, u1, u2, u3, u4, d1, d2, d3, d4, ab, r1, l1, r2, l2, other, bias_ref, perm_ref, out_ref,
    w_ref, x_ref, w_sem, x_sem,
):
    x, zh, y, core = at_ref[0], at_ref[1], at_ref[2], at_ref[3]
    copies = []

    def start(src, dst, sem):
        copy = pltpu.make_async_copy(src, dst, sem.at[len(copies)])
        copy.start()
        copies.append(copy)

    def rows_in(piece, chan, at):
        first = jnp.where(at == 0, 1, 5)
        beyond = jnp.where(at == 0, 0, 9)
        start(piece.at[pl.ds(0, 4)], x_ref.at[pl.ds(first, 4), :, chan], x_sem)
        start(piece.at[pl.ds(4, 1)], x_ref.at[pl.ds(beyond, 1), :, chan], x_sem)

    left, right, far = lax.rem(x + 3, 4), lax.rem(x + 1, 4), lax.rem(x + 2, 4)
    same, cross = zh, 1 - zh
    mine = [
        (ab.at[0], 2 * x + same), (ab.at[1], 2 * x + cross),
        (r1.at[0], 2 * left + same), (r1.at[1], 2 * left + cross),
        (l1.at[0], 2 * right + same), (l1.at[1], 2 * right + cross),
        (r2, 2 * far + same), (l2, 2 * far + cross),
    ]
    for n, (piece, chan) in enumerate(mine):
        rows_in(piece, chan, core)
        rows_in(other.at[n], chan, 1 - core)
    n_x = len(copies)
    for step, chunk in ((0, own), (7, u1), (6, u2), (5, u3), (1, d1), (2, d2), (3, d3)):
        start(chunk, w_ref.at[:, :, lax.rem(y + step, 8)], w_sem)
    opposite = lax.rem(y + 4, 8)
    start(u4, w_ref.at[:, :, opposite, :, pl.ds(0, 512)], w_sem)
    start(d4, w_ref.at[:, :, opposite, :, pl.ds(512, 512)], w_sem)
    for copy in copies:
        copy.wait()

    lane = lax.broadcasted_iota(jnp.int32, (128, 128), 1)

    def step(n, carry):
        pair, frame = n // 2, lax.rem(n, 2)
        total = jnp.zeros((384, 256), jnp.float32)
        for b in range(3):
            sides = []
            for q in range(2):
                row = 2 * pair + q + b
                parts = []
                for chan in range(8):
                    parts.append(x_ref[row, 0, chan])
                    parts.append(x_ref[row, frame, chan])
                sides.append(jnp.concatenate(parts, axis=0))
            taps = w_ref[b].reshape(384, 1024)
            total += jnp.dot(taps, jnp.concatenate(sides, axis=1), preferred_element_type=jnp.float32)
        for q in range(2):
            half = total[:, q * 128 : (q + 1) * 128]
            before = jnp.where(lane == 0, 0.0, pltpu.roll(half[:128], 1, 1))
            after = jnp.where(lane == 127, 0.0, pltpu.roll(half[256:], 127, 1))
            conv = before + half[128:256] + after + bias_ref[...]
            conv = conv.reshape(8, 2, 8, 128)
            both = jnp.concatenate([conv[:, 0].reshape(64, 128), conv[:, 1].reshape(64, 128)], axis=1)
            mixed = jnp.dot(both.astype(jnp.bfloat16), perm_ref[...], preferred_element_type=jnp.float32)
            out_ref[2 * pair + q, frame] = mixed.astype(jnp.bfloat16)
        return carry

    lax.fori_loop(0, 8, step, 0)


def convolve(at, chunks, pieces, bias, perm):
    n_any = len(chunks) + len(pieces)
    return pl.pallas_call(
        conv_kernel,
        out_shape=jax.ShapeDtypeStruct((8, 2, 64, 256), jnp.bfloat16),
        in_specs=[pl.BlockSpec(memory_space=pltpu.SMEM)]
        + [pl.BlockSpec(memory_space=pl.ANY)] * n_any
        + [pl.BlockSpec(memory_space=pltpu.VMEM)] * 2,
        out_specs=pl.BlockSpec(memory_space=pltpu.VMEM),
        scratch_shapes=[
            pltpu.VMEM((3, 3, 8, 16, 1024), jnp.bfloat16),
            pltpu.VMEM((10, 2, 8, 64, 128), jnp.bfloat16),
            pltpu.SemaphoreType.DMA((48,)),
            pltpu.SemaphoreType.DMA((48,)),
        ],
        compiler_params=pltpu.CompilerParams(vmem_limit_bytes=40 * 1024 * 1024),
        cost_estimate=pl.CostEstimate(flops=4_900_000_000, bytes_accessed=6_000_000, transcendentals=0),
        name="conv",
    )(at, *chunks, *pieces, bias, perm)


def local(latent, kernel, bias):
    x, zh, y, core = (lax.axis_index(a) for a in ("x", "zh", "y", "k"))
    own = own_chunk(kernel)
    up, down = ring(NY, 1), ring(NY, -1)
    u1 = lax.ppermute(own, "y", up)
    d1 = lax.ppermute(own, "y", down)
    u2 = lax.ppermute(u1, "y", up)
    d2 = lax.ppermute(d1, "y", down)
    u3 = lax.ppermute(u2, "y", up)
    d3 = lax.ppermute(d2, "y", down)
    u4 = lax.ppermute(u3[..., :512], "y", up)
    d4 = lax.ppermute(d3[..., 512:], "y", down)

    rows = own_rows(latent)
    ab = jnp.stack([rows, lax.ppermute(rows, "zh", ring(NH, 1))])
    r1 = lax.ppermute(ab, "x", ring(NX, 1))
    l1 = lax.ppermute(ab, "x", ring(NX, -1))
    r2 = lax.ppermute(r1[0], "x", ring(NX, 1))
    l2 = lax.ppermute(l1[1], "x", ring(NX, -1))
    other = lax.ppermute(jnp.concatenate([ab, r1, l1, r2[None], l2[None]]), "k", ring(NK, 1))

    split = bias.reshape(NY, NL, NK, NX, 2, NH, 2)
    picked = split[:, :, core, x, :, zh, :]
    column = jnp.transpose(picked, (0, 3, 1, 2)).reshape(128, 1)
    column = jnp.broadcast_to(column, (128, 128))
    place = jnp.arange(256)
    perm = (2 * (place % 128) + place // 128)[:, None] == place[None, :]
    at = jnp.stack([x, zh, y, core]).astype(jnp.int32)
    out = convolve(
        at, (own, u1, u2, u3, u4, d1, d2, d3, d4), (ab, r1, l1, r2, l2, other), column, perm.astype(jnp.bfloat16)
    )
    got = lax.all_to_all(out, ("k", "x"), 0, 0, tiled=True)
    got = got.reshape(NK, NX, 2, 32, 2, 256)
    return jnp.transpose(got, (2, 3, 0, 1, 4, 5)).reshape(2, 1, 512, 256)


def solution(mesh):
    fine = Mesh(mesh.devices.reshape(SIZES), AXES)
    tile = ("y", "zl", "k")
    chan = ("x", "zh")
    return jax.shard_map(
        local,
        mesh=fine,
        in_specs=(P(None, tile, chan, None), P(None, None, None, chan, tile), P()),
        out_specs=P(None, tile + chan, None, None),
        check_vma=False,
    )
```

time: 335 us -> 136 us (0.41)
  the two profiles are of different devices: /device:TPU:1 before, /device:TPU:25 now
where the time goes in v1:
time: 136 us; the launch traced here: 135 us
  starting transfers between devices  70 us (51%)
  waiting for transfers between devices  20.1 us (15%)
  blocking collectives  18.2 us (13%)
  local copies, waits for them, and re-layouts  13.2 us (10%)
  Pallas kernels  11.3 us (8%)
  other arithmetic  2.28 us (2%)
    all_to_all x1, blocking collectives, local(): got = lax.all_to_all(out, ('k', 'x'), 0, 0, tiled=True)  18.2 us
    pallas_call x1, Pallas kernels, convolve(): pl.pallas_call(conv_kernel, out_shape=jax.ShapeDtypeStruct((8, 2, 64, 256...  11.3 us
    all_to_all x1, starting transfers between devices, own_chunk(): got = lax.all_to_all(pieces, ('x', 'zh', 'zl'), 0, 0, tiled=True)  11.2 us
    ppermute x1, starting transfers between devices, local(): ab = jnp.stack([rows, lax.ppermute(rows, 'zh', ring(NH, 1))])  9.74 us
    ppermute x1, starting transfers between devices, local(): u1 = lax.ppermute(own, 'y', up)  5.85 us
    ppermute x1, starting transfers between devices, local(): u4 = lax.ppermute(u3[..., :512], 'y', up)  5.31 us
    ppermute x1, starting transfers between devices, local(): u2 = lax.ppermute(u1, 'y', up)  5.31 us
    ppermute x1, starting transfers between devices, local(): u3 = lax.ppermute(u2, 'y', up)  5.31 us
  transfers between devices with their start and end apart: 16, of which 8 were waited for; matrix products, arithmetic and copies ran while one was open for 10% of the time, Pallas kernels for 0%

profile of v1, /device:TPU:25, one launch (start us, length us, event | category | flops | bytes accessed | tf_op | source)
XLA Modules:
  0.0 135.4 jit_solution(2539466912771362956)
XLA Ops:
  1.0 4.6 %collective-permute-start.8 = (bf16[1,2,64,128]{3,2,1,0:T(8,128)(2,1)S(1)}, bf16[1,2,64,128]{3,2,1,0:T(8,128)(2,1)S(1)}, u32[]{:S(2)}, u32[]{:S(2)}) collective-permute-start(bf16[1,2,64,128]{3,2,1,0:T(8,128)(2,1)S(1)} %slice_select_fusion), channel_id=1, source_target_pairs={{1,2},{3,4},{5,6},{7,8},{9,10},{11,12},{13,14},{15,16},{17,18},{19... | collective-permute-start | bytes 98312 | tf_op jit(solution)/shard_map/ppermute | solution.py:40
  7.2 9.7 %collective-permute-start.9 = (bf16[5,2,64,128]{3,2,1,0:T(8,128)(2,1)S(1)}, bf16[5,2,64,128]{3,2,1,0:T(8,128)(2,1)S(1)}, u32[]{:S(2)}, u32[]{:S(2)}) collective-permute-start(bf16[5,2,64,128]{3,2,1,0:T(8,128)(2,1)S(1)} %get-tuple-element.6), channel_id=1, source_target_pairs={{0,64},{64,0},{1,65},{65,1},{2,66},{66,2},{3,67},{67,3},{4,68},{68... | collective-permute-start | bytes 491528 | tf_op jit(solution)/shard_map/ppermute | solution.py:147
  19.5 11.2 %all-to-all-start = ((bf16[32,3,3,2,2,128]{5,4,3,2,1,0:T(2,128)(2,1)}), bf16[32,3,3,2,2,128]{5,4,3,2,1,0:T(2,128)(2,1)S(1)}, u32[]{:S(2)}, u32[]{:S(2)}) async-start(bf16[32,3,3,2,2,128]{5,4,3,2,1,0:T(2,128)(2,1)} %bitcast.7), calls=%async_computation | async-start | bytes 589824 | tf_op jit(solution)/shard_map/all_to_all | solution.py:30
  30.8 3.1 %collective-permute-start.10 = (bf16[2,5,2,64,128]{4,3,2,1,0:T(8,128)(2,1)S(1)}, bf16[2,5,2,64,128]{4,3,2,1,0:T(8,128)(2,1)S(1)}, u32[]{:S(2)}, u32[]{:S(2)}) collective-permute-start(bf16[2,5,2,64,128]{4,3,2,1,0:T(8,128)(2,1)S(1)} %pad_maximum_fusion.ab), channel_id=1, source_target_pairs={{0,128},{128,256},{256,384},{384,0},{1,129},{129,257},{257,385},{3... | collective-permute-start | bytes 983048 | tf_op jit(solution)/shard_map/ppermute | solution.py:148
  34.6 3.3 %collective-permute-start.11 = (bf16[2,5,2,64,128]{4,3,2,1,0:T(8,128)(2,1)S(1)}, bf16[2,5,2,64,128]{4,3,2,1,0:T(8,128)(2,1)S(1)}, u32[]{:S(2)}, u32[]{:S(2)}) collective-permute-start(bf16[2,5,2,64,128]{4,3,2,1,0:T(8,128)(2,1)S(1)} %pad_maximum_fusion.ab), channel_id=1, source_target_pairs={{0,384},{128,0},{256,128},{384,256},{1,385},{129,1},{257,129},{385... | collective-permute-start | bytes 983048 | tf_op jit(solution)/shard_map/ppermute | solution.py:149
  38.6 5.1 %collective-permute-done.10.r1 = bf16[2,5,2,64,128]{4,3,2,1,0:T(8,128)(2,1)S(1)} collective-permute-done((bf16[2,5,2,64,128]{4,3,2,1,0:T(8,128)(2,1)S(1)}, bf16[2,5,2,64,128]{4,3,2,1,0:T(8,128)(2,1)S(1)}, u32[]{:S(2)}, u32[]{:S(2)}) %collective-permute-start.10) | collective-permute-done | bytes 327712 | tf_op jit(solution)/shard_map/ppermute | solution.py:148
  43.8 1.9 %collective-permute-start.12 = (bf16[5,2,64,128]{3,2,1,0:T(8,128)(2,1)S(1)}, bf16[5,2,64,128]{3,2,1,0:T(8,128)(2,1)S(1)}, u32[]{:S(2)}, u32[]{:S(2)}) collective-permute-start(bf16[5,2,64,128]{3,2,1,0:T(8,128)(2,1)S(1)} %slice_bitcast_fusion.1), channel_id=1, source_target_pairs={{0,128},{128,256},{256,384},{384,0},{1,129},{129,257},{257,385},{3... | collective-permute-start | bytes 491528 | tf_op jit(solution)/shard_map/ppermute | solution.py:150
  45.7 4.6 %collective-permute-start.13 = (bf16[5,2,64,128]{3,2,1,0:T(8,128)(2,1)S(1)}, bf16[5,2,64,128]{3,2,1,0:T(8,128)(2,1)S(1)}, u32[]{:S(2)}, u32[]{:S(2)}) collective-permute-start(bf16[5,2,64,128]{3,2,1,0:T(8,128)(2,1)S(1)} %slice_bitcast_fusion), channel_id=1, source_target_pairs={{0,384},{128,0},{256,128},{384,256},{1,385},{129,1},{257,129},{385... | collective-permute-start | bytes 491528 | tf_op jit(solution)/shard_map/ppermute | solution.py:151
  54.8 2.1 %collective-permute-start.14 = (bf16[8,5,2,64,128]{4,3,2,1,0:T(8,128)(2,1)}, bf16[8,5,2,64,128]{4,3,2,1,0:T(8,128)(2,1)}, u32[]{:S(2)}, u32[]{:S(2)}) collective-permute-start(bf16[8,5,2,64,128]{4,3,2,1,0:T(8,128)(2,1)} %bitcast_dynamic-update-slice_fusion), channel_id=1, source_target_pairs={{0,1},{1,0},{2,3},{3,2},{4,5},{5,4},{6,7},{7,6},{8,9},{9,8},{10,11... | collective-permute-start | bytes 3932168 | tf_op jit(solution)/shard_map/ppermute | solution.py:152
  57.2 5.8 %collective-permute-start = (bf16[3,3,16,1024]{3,2,1,0:T(8,128)(2,1)S(1)}, bf16[3,3,16,1024]{3,2,1,0:T(8,128)(2,1)S(1)}, u32[]{:S(2)}, u32[]{:S(2)}) collective-permute-start(bf16[3,3,16,1024]{3,2,1,0:T(8,128)(2,1)S(1)} %reshape.49.own), channel_id=1, source_target_pairs={{0,8},{8,16},{16,24},{24,32},{32,40},{40,48},{48,56},{56,0},{1,9},... | collective-permute-start | bytes 884744 | tf_op jit(solution)/shard_map/ppermute | solution.py:137
  63.1 1.9 %collective-permute-start.4 = (bf16[3,3,16,1024]{3,2,1,0:T(8,128)(2,1)S(1)}, bf16[3,3,16,1024]{3,2,1,0:T(8,128)(2,1)S(1)}, u32[]{:S(2)}, u32[]{:S(2)}) collective-permute-start(bf16[3,3,16,1024]{3,2,1,0:T(8,128)(2,1)S(1)} %reshape.49.own), channel_id=1, source_target_pairs={{0,56},{8,0},{16,8},{24,16},{32,24},{40,32},{48,40},{56,48},{1,57}... | collective-permute-start | bytes 884744 | tf_op jit(solution)/shard_map/ppermute | solution.py:138
  65.0 4.5 %collective-permute-done.u1 = bf16[3,3,16,1024]{3,2,1,0:T(8,128)(2,1)S(1)} collective-permute-done((bf16[3,3,16,1024]{3,2,1,0:T(8,128)(2,1)S(1)}, bf16[3,3,16,1024]{3,2,1,0:T(8,128)(2,1)S(1)}, u32[]{:S(2)}, u32[]{:S(2)}) %collective-permute-start) | collective-permute-done | bytes 294944 | tf_op jit(solution)/shard_map/ppermute | solution.py:137
  69.5 5.3 %collective-permute-start.1 = (bf16[3,3,16,1024]{3,2,1,0:T(8,128)(2,1)S(1)}, bf16[3,3,16,1024]{3,2,1,0:T(8,128)(2,1)S(1)}, u32[]{:S(2)}, u32[]{:S(2)}) collective-permute-start(bf16[3,3,16,1024]{3,2,1,0:T(8,128)(2,1)S(1)} %collective-permute-done.u1), channel_id=1, source_target_pairs={{0,8},{8,16},{16,24},{24,32},{32,40},{40,48},{48,56},{56,0},{1,9},... | collective-permute-start | bytes 884744 | tf_op jit(solution)/shard_map/ppermute | solution.py:139
  74.8 1.9 %collective-permute-start.5 = (bf16[3,3,16,1024]{3,2,1,0:T(8,128)(2,1)S(1)}, bf16[3,3,16,1024]{3,2,1,0:T(8,128)(2,1)S(1)}, u32[]{:S(2)}, u32[]{:S(2)}) collective-permute-start(bf16[3,3,16,1024]{3,2,1,0:T(8,128)(2,1)S(1)} %collective-permute-done.4.d1), channel_id=1, source_target_pairs={{0,56},{8,0},{16,8},{24,16},{32,24},{40,32},{48,40},{56,48},{1,57}... | collective-permute-start | bytes 884744 | tf_op jit(solution)/shard_map/ppermute | solution.py:140
  76.7 1.6 %reshape.50 = f32[8,4,2,4,2,2,2]{6,5,4,3,2,1,0:T(2,128)} reshape(f32[2048]{0:T(1024)S(1)} %copy-done) | data formatting | bytes 16384 | tf_op jit(solution)/shard_map/reshape | solution.py:154
  78.3 2.0 %collective-permute-done.1.u2 = bf16[3,3,16,1024]{3,2,1,0:T(8,128)(2,1)S(1)} collective-permute-done((bf16[3,3,16,1024]{3,2,1,0:T(8,128)(2,1)S(1)}, bf16[3,3,16,1024]{3,2,1,0:T(8,128)(2,1)S(1)}, u32[]{:S(2)}, u32[]{:S(2)}) %collective-permute-start.1) | collective-permute-done | bytes 294944 | tf_op jit(solution)/shard_map/ppermute | solution.py:139
  80.3 5.3 %collective-permute-start.2 = (bf16[3,3,16,1024]{3,2,1,0:T(8,128)(2,1)S(1)}, bf16[3,3,16,1024]{3,2,1,0:T(8,128)(2,1)S(1)}, u32[]{:S(2)}, u32[]{:S(2)}) collective-permute-start(bf16[3,3,16,1024]{3,2,1,0:T(8,128)(2,1)S(1)} %collective-permute-done.1.u2), channel_id=1, source_target_pairs={{0,8},{8,16},{16,24},{24,32},{32,40},{40,48},{48,56},{56,0},{1,9},... | collective-permute-start | bytes 884744 | tf_op jit(solution)/shard_map/ppermute | solution.py:141
  85.6 1.9 %collective-permute-start.6 = (bf16[3,3,16,1024]{3,2,1,0:T(8,128)(2,1)S(1)}, bf16[3,3,16,1024]{3,2,1,0:T(8,128)(2,1)S(1)}, u32[]{:S(2)}, u32[]{:S(2)}) collective-permute-start(bf16[3,3,16,1024]{3,2,1,0:T(8,128)(2,1)S(1)} %collective-permute-done.5.d2), channel_id=1, source_target_pairs={{0,56},{8,0},{16,8},{24,16},{32,24},{40,32},{48,40},{56,48},{1,57}... | collective-permute-start | bytes 884744 | tf_op jit(solution)/shard_map/ppermute | solution.py:142
  87.7 2.5 %collective-permute-done.2.u3 = bf16[3,3,16,1024]{3,2,1,0:T(8,128)(2,1)S(1)} collective-permute-done((bf16[3,3,16,1024]{3,2,1,0:T(8,128)(2,1)S(1)}, bf16[3,3,16,1024]{3,2,1,0:T(8,128)(2,1)S(1)}, u32[]{:S(2)}, u32[]{:S(2)}) %collective-permute-start.2) | collective-permute-done | bytes 294944 | tf_op jit(solution)/shard_map/ppermute | solution.py:141
  90.9 5.3 %collective-permute-start.3 = (bf16[3,3,16,512]{3,2,1,0:T(8,128)(2,1)}, bf16[3,3,16,512]{3,2,1,0:T(8,128)(2,1)}, u32[]{:S(2)}, u32[]{:S(2)}) collective-permute-start(bf16[3,3,16,512]{3,2,1,0:T(8,128)(2,1)} %slice.36), channel_id=1, source_target_pairs={{0,8},{8,16},{16,24},{24,32},{32,40},{40,48},{48,56},{56,0},{1,9},... | collective-permute-start | bytes 442376 | tf_op jit(solution)/shard_map/ppermute | solution.py:143
  96.9 1.9 %collective-permute-start.7 = (bf16[3,3,16,512]{3,2,1,0:T(8,128)(2,1)}, bf16[3,3,16,512]{3,2,1,0:T(8,128)(2,1)}, u32[]{:S(2)}, u32[]{:S(2)}) collective-permute-start(bf16[3,3,16,512]{3,2,1,0:T(8,128)(2,1)} %slice.37), channel_id=1, source_target_pairs={{0,56},{8,0},{16,8},{24,16},{32,24},{40,32},{48,40},{56,48},{1,57}... | collective-permute-start | bytes 442376 | tf_op jit(solution)/shard_map/ppermute | solution.py:144
  101.6 2.7 %collective-permute-done.7.d4 = bf16[3,3,16,512]{3,2,1,0:T(8,128)(2,1)} collective-permute-done((bf16[3,3,16,512]{3,2,1,0:T(8,128)(2,1)}, bf16[3,3,16,512]{3,2,1,0:T(8,128)(2,1)}, u32[]{:S(2)}, u32[]{:S(2)}) %collective-permute-start.7) | collective-permute-done | bytes 147488 | tf_op jit(solution)/shard_map/ppermute | solution.py:144
  104.4 11.3 %conv.1 = bf16[8,2,64,256]{3,2,1,0:T(8,128)(2,1)S(1)} custom-call(s32[4]{0:T(128)S(1)} %pad_add_fusion.at_ref, bf16[3,3,16,1024]{3,2,1,0:T(8,128)(2,1)S(1)} %reshape.49.own, bf16[3,3,16,1024]{3,2,1,0:T(8,128)(2,1)S(1)} %collective-permute-done.u1, bf16[3,3,16,1024]{3,2,1,0:T(8,128)(2,1)S(1)} %collective-permute-done.1.u2, ...), custom_call_target="tpu_custom_call" | custom-call | flops 4899999744 | bytes 6000000 | tf_op jit(solution)/shard_map/conv/pallas_call | solution.py:114
  115.7 18.2 %all_to_all.10 = bf16[8,2,64,256]{3,2,1,0:T(8,128)(2,1)S(1)} all-to-all(bf16[8,2,64,256]{3,2,1,0:T(8,128)(2,1)S(1)} %conv.1), channel_id=1, replica_groups=mesh['x'=4,'zh'=2,'y'=8,'zl'=4,'k'=2] {'k','x'}, dimensions={0} | all-to-all | bytes 1048576 | tf_op jit(solution)/shard_map/all_to_all | solution.py:164
  (48 shorter events, 17.2 us)
Async XLA Ops:
  0.0 18.0 %slice-start = ((bf16[3,3,3,64,32]{3,4,2,1,0:T(8,128)(2,1)}), bf16[1,3,3,64,32]{3,4,2,1,0:T(8,128)(2,1)S(1)}, s32[]{:S(2)}) async-start(bf16[3,3,3,64,32]{3,4,2,1,0:T(8,128)(2,1)} %param.4), calls=%async_computation.2 | async-start | bytes 147456 | tf_op jit(solution)/shard_map/slice | solution.py:21
  1.0 6.2 %collective-permute-start.8 = (bf16[1,2,64,128]{3,2,1,0:T(8,128)(2,1)S(1)}, bf16[1,2,64,128]{3,2,1,0:T(8,128)(2,1)S(1)}, u32[]{:S(2)}, u32[]{:S(2)}) collective-permute-start(bf16[1,2,64,128]{3,2,1,0:T(8,128)(2,1)S(1)} %slice_select_fusion), channel_id=1, source_target_pairs={{1,2},{3,4},{5,6},{7,8},{9,10},{11,12},{13,14},{15,16},{17,18},{19... | collective-permute-start | bytes 98312 | tf_op jit(solution)/shard_map/ppermute | solution.py:40
  7.2 23.6 %collective-permute-start.9 = (bf16[5,2,64,128]{3,2,1,0:T(8,128)(2,1)S(1)}, bf16[5,2,64,128]{3,2,1,0:T(8,128)(2,1)S(1)}, u32[]{:S(2)}, u32[]{:S(2)}) collective-permute-start(bf16[5,2,64,128]{3,2,1,0:T(8,128)(2,1)S(1)} %get-tuple-element.6), channel_id=1, source_target_pairs={{0,64},{64,0},{1,65},{65,1},{2,66},{66,2},{3,67},{67,3},{4,68},{68... | collective-permute-start | bytes 491528 | tf_op jit(solution)/shard_map/ppermute | solution.py:147
  19.5 37.4 %all-to-all-start = ((bf16[32,3,3,2,2,128]{5,4,3,2,1,0:T(2,128)(2,1)}), bf16[32,3,3,2,2,128]{5,4,3,2,1,0:T(2,128)(2,1)S(1)}, u32[]{:S(2)}, u32[]{:S(2)}) async-start(bf16[32,3,3,2,2,128]{5,4,3,2,1,0:T(2,128)(2,1)} %bitcast.7), calls=%async_computation | async-start | bytes 589824 | tf_op jit(solution)/shard_map/all_to_all | solution.py:30
  30.8 13.0 %collective-permute-start.10 = (bf16[2,5,2,64,128]{4,3,2,1,0:T(8,128)(2,1)S(1)}, bf16[2,5,2,64,128]{4,3,2,1,0:T(8,128)(2,1)S(1)}, u32[]{:S(2)}, u32[]{:S(2)}) collective-permute-start(bf16[2,5,2,64,128]{4,3,2,1,0:T(8,128)(2,1)S(1)} %pad_maximum_fusion.ab), channel_id=1, source_target_pairs={{0,128},{128,256},{256,384},{384,0},{1,129},{129,257},{257,385},{3... | collective-permute-start | bytes 983048 | tf_op jit(solution)/shard_map/ppermute | solution.py:148
  34.6 11.1 %collective-permute-start.11 = (bf16[2,5,2,64,128]{4,3,2,1,0:T(8,128)(2,1)S(1)}, bf16[2,5,2,64,128]{4,3,2,1,0:T(8,128)(2,1)S(1)}, u32[]{:S(2)}, u32[]{:S(2)}) collective-permute-start(bf16[2,5,2,64,128]{4,3,2,1,0:T(8,128)(2,1)S(1)} %pad_maximum_fusion.ab), channel_id=1, source_target_pairs={{0,384},{128,0},{256,128},{384,256},{1,385},{129,1},{257,129},{385... | collective-permute-start | bytes 983048 | tf_op jit(solution)/shard_map/ppermute | solution.py:149
  43.8 8.6 %collective-permute-start.12 = (bf16[5,2,64,128]{3,2,1,0:T(8,128)(2,1)S(1)}, bf16[5,2,64,128]{3,2,1,0:T(8,128)(2,1)S(1)}, u32[]{:S(2)}, u32[]{:S(2)}) collective-permute-start(bf16[5,2,64,128]{3,2,1,0:T(8,128)(2,1)S(1)} %slice_bitcast_fusion.1), channel_id=1, source_target_pairs={{0,128},{128,256},{256,384},{384,0},{1,129},{129,257},{257,385},{3... | collective-permute-start | bytes 491528 | tf_op jit(solution)/shard_map/ppermute | solution.py:150
  45.7 8.5 %collective-permute-start.13 = (bf16[5,2,64,128]{3,2,1,0:T(8,128)(2,1)S(1)}, bf16[5,2,64,128]{3,2,1,0:T(8,128)(2,1)S(1)}, u32[]{:S(2)}, u32[]{:S(2)}) collective-permute-start(bf16[5,2,64,128]{3,2,1,0:T(8,128)(2,1)S(1)} %slice_bitcast_fusion), channel_id=1, source_target_pairs={{0,384},{128,0},{256,128},{384,256},{1,385},{129,1},{257,129},{385... | collective-permute-start | bytes 491528 | tf_op jit(solution)/shard_map/ppermute | solution.py:151
  51.9 24.9 %copy-start = (f32[2048]{0:T(1024)S(1)}, f32[2048]{0:T(1024)}, u32[]{:S(2)}) copy-start(f32[2048]{0:T(1024)} %param.5) | copy-start | bytes 24580
  54.8 49.5 %collective-permute-start.14 = (bf16[8,5,2,64,128]{4,3,2,1,0:T(8,128)(2,1)}, bf16[8,5,2,64,128]{4,3,2,1,0:T(8,128)(2,1)}, u32[]{:S(2)}, u32[]{:S(2)}) collective-permute-start(bf16[8,5,2,64,128]{4,3,2,1,0:T(8,128)(2,1)} %bitcast_dynamic-update-slice_fusion), channel_id=1, source_target_pairs={{0,1},{1,0},{2,3},{3,2},{4,5},{5,4},{6,7},{7,6},{8,9},{9,8},{10,11... | collective-permute-start | bytes 3932168 | tf_op jit(solution)/shard_map/ppermute | solution.py:152
  57.2 12.3 %collective-permute-start = (bf16[3,3,16,1024]{3,2,1,0:T(8,128)(2,1)S(1)}, bf16[3,3,16,1024]{3,2,1,0:T(8,128)(2,1)S(1)}, u32[]{:S(2)}, u32[]{:S(2)}) collective-permute-start(bf16[3,3,16,1024]{3,2,1,0:T(8,128)(2,1)S(1)} %reshape.49.own), channel_id=1, source_target_pairs={{0,8},{8,16},{16,24},{24,32},{32,40},{40,48},{48,56},{56,0},{1,9},... | collective-permute-start | bytes 884744 | tf_op jit(solution)/shard_map/ppermute | solution.py:137
  63.1 11.7 %collective-permute-start.4 = (bf16[3,3,16,1024]{3,2,1,0:T(8,128)(2,1)S(1)}, bf16[3,3,16,1024]{3,2,1,0:T(8,128)(2,1)S(1)}, u32[]{:S(2)}, u32[]{:S(2)}) collective-permute-start(bf16[3,3,16,1024]{3,2,1,0:T(8,128)(2,1)S(1)} %reshape.49.own), channel_id=1, source_target_pairs={{0,56},{8,0},{16,8},{24,16},{32,24},{40,32},{48,40},{56,48},{1,57}... | collective-permute-start | bytes 884744 | tf_op jit(solution)/shard_map/ppermute | solution.py:138
  69.5 10.8 %collective-permute-start.1 = (bf16[3,3,16,1024]{3,2,1,0:T(8,128)(2,1)S(1)}, bf16[3,3,16,1024]{3,2,1,0:T(8,128)(2,1)S(1)}, u32[]{:S(2)}, u32[]{:S(2)}) collective-permute-start(bf16[3,3,16,1024]{3,2,1,0:T(8,128)(2,1)S(1)} %collective-permute-done.u1), channel_id=1, source_target_pairs={{0,8},{8,16},{16,24},{24,32},{32,40},{40,48},{48,56},{56,0},{1,9},... | collective-permute-start | bytes 884744 | tf_op jit(solution)/shard_map/ppermute | solution.py:139
  74.8 10.8 %collective-permute-start.5 = (bf16[3,3,16,1024]{3,2,1,0:T(8,128)(2,1)S(1)}, bf16[3,3,16,1024]{3,2,1,0:T(8,128)(2,1)S(1)}, u32[]{:S(2)}, u32[]{:S(2)}) collective-permute-start(bf16[3,3,16,1024]{3,2,1,0:T(8,128)(2,1)S(1)} %collective-permute-done.4.d1), channel_id=1, source_target_pairs={{0,56},{8,0},{16,8},{24,16},{32,24},{40,32},{48,40},{56,48},{1,57}... | collective-permute-start | bytes 884744 | tf_op jit(solution)/shard_map/ppermute | solution.py:140
  80.3 9.9 %collective-permute-start.2 = (bf16[3,3,16,1024]{3,2,1,0:T(8,128)(2,1)S(1)}, bf16[3,3,16,1024]{3,2,1,0:T(8,128)(2,1)S(1)}, u32[]{:S(2)}, u32[]{:S(2)}) collective-permute-start(bf16[3,3,16,1024]{3,2,1,0:T(8,128)(2,1)S(1)} %collective-permute-done.1.u2), channel_id=1, source_target_pairs={{0,8},{8,16},{16,24},{24,32},{32,40},{40,48},{48,56},{56,0},{1,9},... | collective-permute-start | bytes 884744 | tf_op jit(solution)/shard_map/ppermute | solution.py:141
  85.6 10.6 %collective-permute-start.6 = (bf16[3,3,16,1024]{3,2,1,0:T(8,128)(2,1)S(1)}, bf16[3,3,16,1024]{3,2,1,0:T(8,128)(2,1)S(1)}, u32[]{:S(2)}, u32[]{:S(2)}) collective-permute-start(bf16[3,3,16,1024]{3,2,1,0:T(8,128)(2,1)S(1)} %collective-permute-done.5.d2), channel_id=1, source_target_pairs={{0,56},{8,0},{16,8},{24,16},{32,24},{40,32},{48,40},{56,48},{1,57}... | collective-permute-start | bytes 884744 | tf_op jit(solution)/shard_map/ppermute | solution.py:142
  90.9 10.7 %collective-permute-start.3 = (bf16[3,3,16,512]{3,2,1,0:T(8,128)(2,1)}, bf16[3,3,16,512]{3,2,1,0:T(8,128)(2,1)}, u32[]{:S(2)}, u32[]{:S(2)}) collective-permute-start(bf16[3,3,16,512]{3,2,1,0:T(8,128)(2,1)} %slice.36), channel_id=1, source_target_pairs={{0,8},{8,16},{16,24},{24,32},{32,40},{40,48},{48,56},{56,0},{1,9},... | collective-permute-start | bytes 442376 | tf_op jit(solution)/shard_map/ppermute | solution.py:143
  96.9 7.4 %collective-permute-start.7 = (bf16[3,3,16,512]{3,2,1,0:T(8,128)(2,1)}, bf16[3,3,16,512]{3,2,1,0:T(8,128)(2,1)}, u32[]{:S(2)}, u32[]{:S(2)}) collective-permute-start(bf16[3,3,16,512]{3,2,1,0:T(8,128)(2,1)} %slice.37), channel_id=1, source_target_pairs={{0,56},{8,0},{16,8},{24,16},{32,24},{40,32},{48,40},{56,48},{1,57}... | collective-permute-start | bytes 442376 | tf_op jit(solution)/shard_map/ppermute | solution.py:144

commit v2 on v1

--- a/solution.py
+++ b/solution.py
@@ -41,41 +41,50 @@
     return jnp.concatenate([rows, halo], axis=0)
 
 
+def two_way(size):
+    return [(2 * i + k, 2 * ((i + 1 - 2 * k) % size) + k) for i in range(size) for k in range(NK)]
+
+
+def swap_cores(array):
+    return lax.ppermute(array, "k", ring(NK, 1))
+
+
 def conv_kernel(
-    at_ref, own, u1, u2, u3, u4, d1, d2, d3, d4, ab, r1, l1, r2, l2, other, bias_ref, perm_ref, out_ref,
-    w_ref, x_ref, w_sem, x_sem,
+    at_ref, both, c1, s1, c2, s2, c3, s3, c4, ab, e1, e1s, e2, e2s, bias_ref, perm_ref, out_ref,
+    w_ref, x_ref, sems,
 ):
     x, zh, y, core = at_ref[0], at_ref[1], at_ref[2], at_ref[3]
     copies = []
 
-    def start(src, dst, sem):
-        copy = pltpu.make_async_copy(src, dst, sem.at[len(copies)])
+    def start(src, dst):
+        copy = pltpu.make_async_copy(src, dst, sems.at[len(copies)])
         copy.start()
         copies.append(copy)
 
-    def rows_in(piece, chan, at):
-        first = jnp.where(at == 0, 1, 5)
-        beyond = jnp.where(at == 0, 0, 9)
-        start(piece.at[pl.ds(0, 4)], x_ref.at[pl.ds(first, 4), :, chan], x_sem)
-        start(piece.at[pl.ds(4, 1)], x_ref.at[pl.ds(beyond, 1), :, chan], x_sem)
+    def rows_in(piece, x_from, owner):
+        first = jnp.where(owner == 0, 1, 5)
+        beyond = jnp.where(owner == 0, 0, 9)
+        for j, chan in enumerate((2 * x_from + zh, 2 * x_from + 1 - zh)):
+            start(piece.at[j, pl.ds(0, 4)], x_ref.at[pl.ds(first, 4), :, chan])
+            start(piece.at[j, pl.ds(4, 1)], x_ref.at[pl.ds(beyond, 1), :, chan])
 
-    left, right, far = lax.rem(x + 3, 4), lax.rem(x + 1, 4), lax.rem(x + 2, 4)
-    same, cross = zh, 1 - zh
-    mine = [
-        (ab.at[0], 2 * x + same), (ab.at[1], 2 * x + cross),
-        (r1.at[0], 2 * left + same), (r1.at[1], 2 * left + cross),
-        (l1.at[0], 2 * right + same), (l1.at[1], 2 * right + cross),
-        (r2, 2 * far + same), (l2, 2 * far + cross),
-    ]
-    for n, (piece, chan) in enumerate(mine):
-        rows_in(piece, chan, core)
-        rows_in(other.at[n], chan, 1 - core)
-    n_x = len(copies)
-    for step, chunk in ((0, own), (7, u1), (6, u2), (5, u3), (1, d1), (2, d2), (3, d3)):
-        start(chunk, w_ref.at[:, :, lax.rem(y + step, 8)], w_sem)
-    opposite = lax.rem(y + 4, 8)
-    start(u4, w_ref.at[:, :, opposite, :, pl.ds(0, 512)], w_sem)
-    start(d4, w_ref.at[:, :, opposite, :, pl.ds(512, 512)], w_sem)
+    there = 1 - core
+    near, back = lax.rem(x + 3 + 2 * core, 4), lax.rem(x + 1 + 2 * core, 4)
+    far = lax.rem(x + 2, 4)
+    rows_in(ab.at[0], x, core)
+    rows_in(ab.at[1], x, there)
+    rows_in(e1.at[0], near, core)
+    rows_in(e1.at[1], near, there)
+    rows_in(e1s.at[0], back, there)
+    rows_in(e1s.at[1], back, core)
+    rows_in(e2, far, core)
+    rows_in(e2s, far, there)
+    sign = 1 - 2 * core
+    start(both.at[0], w_ref.at[:, :, y])
+    for n, (chunk, swapped) in enumerate(((c1, s1), (c2, s2), (c3, s3))):
+        start(chunk.at[0], w_ref.at[:, :, lax.rem(y + 8 - (n + 1) * sign, 8)])
+        start(swapped, w_ref.at[:, :, lax.rem(y + 8 + (n + 1) * sign, 8)])
+    start(c4, w_ref.at[:, :, lax.rem(y + 4, 8)])
     for copy in copies:
         copy.wait()
 
@@ -121,8 +130,7 @@
         scratch_shapes=[
             pltpu.VMEM((3, 3, 8, 16, 1024), jnp.bfloat16),
             pltpu.VMEM((10, 2, 8, 64, 128), jnp.bfloat16),
-            pltpu.SemaphoreType.DMA((48,)),
-            pltpu.SemaphoreType.DMA((48,)),
+            pltpu.SemaphoreType.DMA((40,)),
         ],
         compiler_params=pltpu.CompilerParams(vmem_limit_bytes=40 * 1024 * 1024),
         cost_estimate=pl.CostEstimate(flops=4_900_000_000, bytes_accessed=6_000_000, transcendentals=0),
@@ -132,24 +140,22 @@
 
 def local(latent, kernel, bias):
     x, zh, y, core = (lax.axis_index(a) for a in ("x", "zh", "y", "k"))
+    rows = own_rows(latent)
     own = own_chunk(kernel)
-    up, down = ring(NY, 1), ring(NY, -1)
-    u1 = lax.ppermute(own, "y", up)
-    d1 = lax.ppermute(own, "y", down)
-    u2 = lax.ppermute(u1, "y", up)
-    d2 = lax.ppermute(d1, "y", down)
-    u3 = lax.ppermute(u2, "y", up)
-    d3 = lax.ppermute(d2, "y", down)
-    u4 = lax.ppermute(u3[..., :512], "y", up)
-    d4 = lax.ppermute(d3[..., 512:], "y", down)
+    own, rows = lax.optimization_barrier((own, rows))
 
-    rows = own_rows(latent)
-    ab = jnp.stack([rows, lax.ppermute(rows, "zh", ring(NH, 1))])
-    r1 = lax.ppermute(ab, "x", ring(NX, 1))
-    l1 = lax.ppermute(ab, "x", ring(NX, -1))
-    r2 = lax.ppermute(r1[0], "x", ring(NX, 1))
-    l2 = lax.ppermute(l1[1], "x", ring(NX, -1))
-    other = lax.ppermute(jnp.concatenate([ab, r1, l1, r2[None], l2[None]]), "k", ring(NK, 1))
+    both = jnp.stack([own, swap_cores(own)])
+    c1 = lax.ppermute(both, ("y", "k"), two_way(NY))
+    c2 = lax.ppermute(c1, ("y", "k"), two_way(NY))
+    c3 = lax.ppermute(c2, ("y", "k"), two_way(NY))
+    c4 = lax.ppermute(c3[0], ("y", "k"), two_way(NY))
+    s1, s2, s3 = swap_cores(c1[1]), swap_cores(c2[1]), swap_cores(c3[1])
+
+    rows = jnp.stack([rows, lax.ppermute(rows, "zh", ring(NH, 1))])
+    ab = jnp.stack([rows, swap_cores(rows)])
+    e1 = lax.ppermute(ab, ("x", "k"), two_way(NX))
+    e2 = lax.ppermute(e1[0], ("x", "k"), two_way(NX))
+    e1s, e2s = swap_cores(e1), swap_cores(e2)
 
     split = bias.reshape(NY, NL, NK, NX, 2, NH, 2)
     picked = split[:, :, core, x, :, zh, :]
@@ -159,7 +165,7 @@
     perm = (2 * (place % 128) + place // 128)[:, None] == place[None, :]
     at = jnp.stack([x, zh, y, core]).astype(jnp.int32)
     out = convolve(
-        at, (own, u1, u2, u3, u4, d1, d2, d3, d4), (ab, r1, l1, r2, l2, other), column, perm.astype(jnp.bfloat16)
+        at, (both, c1, s1, c2, s2, c3, s3, c4), (ab, e1, e1s, e2, e2s), column, perm.astype(jnp.bfloat16)
     )
     got = lax.all_to_all(out, ("k", "x"), 0, 0, tiled=True)
     got = got.reshape(NK, NX, 2, 32, 2, 256)

time: 136 us -> 120 us (0.88)
  the two profiles are of different devices: /device:TPU:25 before, /device:TPU:1 now
where the time goes in v2:
time: 120 us
  starting transfers between devices  71.5 us (60%)
  blocking collectives  15.9 us (13%)
  waiting for transfers between devices  13.1 us (11%)
  Pallas kernels  10.2 us (8%)
  local copies, waits for them, and re-layouts  6.8 us (6%)
  other arithmetic  1.75 us (1%)
    ppermute x7, starting transfers between devices, swap_cores(): return lax.ppermute(array, 'k', ring(NK, 1))  25.4 us
    all_to_all x1, blocking collectives, local(): got = lax.all_to_all(out, ('k', 'x'), 0, 0, tiled=True)  15.9 us
    all_to_all x1, starting transfers between devices, own_chunk(): got = lax.all_to_all(pieces, ('x', 'zh', 'zl'), 0, 0, tiled=True)  13.8 us
    pallas_call x1, Pallas kernels, convolve(): pl.pallas_call(conv_kernel, out_shape=jax.ShapeDtypeStruct((8, 2, 64, 256...  10.2 us
    ppermute x1, starting transfers between devices, local(): rows = jnp.stack([rows, lax.ppermute(rows, 'zh', ring(NH, 1))])  5.56 us
    ppermute x1, starting transfers between devices, local(): c2 = lax.ppermute(c1, ('y', 'k'), two_way(NY))  5.31 us
    ppermute x1, starting transfers between devices, local(): c3 = lax.ppermute(c2, ('y', 'k'), two_way(NY))  5.01 us
    ppermute x1, waiting for transfers between devices, own_rows(): lax.ppermute(edge, ('y', 'zl', 'k'), pairs + [(b, a) for a, b in pairs])  4.92 us
  transfers between devices with their start and end apart: 16, of which 5 were waited for; matrix products, arithmetic and copies ran while one was open for 3% of the time, Pallas kernels for 0%

profile of v2, /device:TPU:1, one launch (start us, length us, event | category | flops | bytes accessed | tf_op | source)
XLA Modules:
  0.0 119.6 jit_solution(4642946991591154874)
XLA Ops:
  2.6 13.8 %all-to-all-start = ((bf16[32,3,3,2,2,128]{5,4,3,2,1,0:T(2,128)(2,1)}), bf16[32,3,3,2,2,128]{5,4,3,2,1,0:T(2,128)(2,1)S(1)}, u32[]{:S(2)}, u32[]{:S(2)}) async-start(bf16[32,3,3,2,2,128]{5,4,3,2,1,0:T(2,128)(2,1)} %bitcast.7), calls=%async_computation | async-start | bytes 589824 | tf_op jit(solution)/shard_map/all_to_all | solution.py:30
  16.6 4.3 %collective-permute-start = (bf16[1,2,64,128]{3,2,1,0:T(8,128)(2,1)S(1)}, bf16[1,2,64,128]{3,2,1,0:T(8,128)(2,1)S(1)}, u32[]{:S(2)}, u32[]{:S(2)}) collective-permute-start(bf16[1,2,64,128]{3,2,1,0:T(8,128)(2,1)S(1)} %slice_select_fusion), channel_id=1, source_target_pairs={{1,2},{3,4},{5,6},{7,8},{9,10},{11,12},{13,14},{15,16},{17,18},{19... | collective-permute-start | bytes 98312 | tf_op jit(solution)/shard_map/ppermute | solution.py:40
  20.8 4.9 %collective-permute-done = bf16[1,2,64,128]{3,2,1,0:T(8,128)(2,1)S(1)} collective-permute-done((bf16[1,2,64,128]{3,2,1,0:T(8,128)(2,1)S(1)}, bf16[1,2,64,128]{3,2,1,0:T(8,128)(2,1)S(1)}, u32[]{:S(2)}, u32[]{:S(2)}) %collective-permute-start) | collective-permute-done | bytes 32800 | tf_op jit(solution)/shard_map/ppermute | solution.py:40
  26.7 5.6 %collective-permute-start.9 = (bf16[5,2,64,128]{3,2,1,0:T(8,128)(2,1)S(1)}, bf16[5,2,64,128]{3,2,1,0:T(8,128)(2,1)S(1)}, u32[]{:S(2)}, u32[]{:S(2)}) collective-permute-start(bf16[5,2,64,128]{3,2,1,0:T(8,128)(2,1)S(1)} %pad_maximum_fusion.3), channel_id=1, source_target_pairs={{0,64},{64,0},{1,65},{65,1},{2,66},{66,2},{3,67},{67,3},{4,68},{68... | collective-permute-start | bytes 491528 | tf_op jit(solution)/shard_map/ppermute | solution.py:154
  32.3 4.8 %collective-permute-start.1 = (bf16[3,3,16,1024]{3,2,1,0:T(8,128)(2,1)S(1)}, bf16[3,3,16,1024]{3,2,1,0:T(8,128)(2,1)S(1)}, u32[]{:S(2)}, u32[]{:S(2)}) collective-permute-start(bf16[3,3,16,1024]{3,2,1,0:T(8,128)(2,1)S(1)} %reshape.49), channel_id=1, source_target_pairs={{0,1},{1,0},{2,3},{3,2},{4,5},{5,4},{6,7},{7,6},{8,9},{9,8},{10,11... | collective-permute-start | bytes 884744 | tf_op jit(solution)/shard_map/ppermute | solution.py:49
  37.1 10.0 %collective-permute-start.10 = (bf16[2,5,2,64,128]{4,3,2,1,0:T(8,128)(2,1)S(1)}, bf16[2,5,2,64,128]{4,3,2,1,0:T(8,128)(2,1)S(1)}, u32[]{:S(2)}, u32[]{:S(2)}) collective-permute-start(bf16[2,5,2,64,128]{4,3,2,1,0:T(8,128)(2,1)S(1)} %get-tuple-element.12), channel_id=1, source_target_pairs={{0,1},{1,0},{2,3},{3,2},{4,5},{5,4},{6,7},{7,6},{8,9},{9,8},{10,11... | collective-permute-start | bytes 983048 | tf_op jit(solution)/shard_map/ppermute | solution.py:49
  47.2 4.4 %collective-permute-start.2 = (bf16[2,3,3,16,1024]{4,3,2,1,0:T(8,128)(2,1)S(1)}, bf16[2,3,3,16,1024]{4,3,2,1,0:T(8,128)(2,1)S(1)}, u32[]{:S(2)}, u32[]{:S(2)}) collective-permute-start(bf16[2,3,3,16,1024]{4,3,2,1,0:T(8,128)(2,1)S(1)} %pad_maximum_fusion.1.both), channel_id=1, source_target_pairs={{0,8},{1,57},{8,16},{9,1},{16,24},{17,9},{24,32},{25,17},{32,40},{... | collective-permute-start | bytes 1769480 | tf_op jit(solution)/shard_map/ppermute | solution.py:148
  51.7 1.9 %collective-permute-start.11 = (bf16[2,2,5,2,64,128]{5,4,3,2,1,0:T(8,128)(2,1)S(1)}, bf16[2,2,5,2,64,128]{5,4,3,2,1,0:T(8,128)(2,1)S(1)}, u32[]{:S(2)}, u32[]{:S(2)}) collective-permute-start(bf16[2,2,5,2,64,128]{5,4,3,2,1,0:T(8,128)(2,1)S(1)} %pad_maximum_fusion.ab), channel_id=1, source_target_pairs={{0,128},{1,385},{128,256},{129,1},{256,384},{257,129},{384,0},{385... | collective-permute-start | bytes 1966088 | tf_op jit(solution)/shard_map/ppermute | solution.py:156
  53.6 4.8 %collective-permute-done.2.c1 = bf16[2,3,3,16,1024]{4,3,2,1,0:T(8,128)(2,1)S(1)} collective-permute-done((bf16[2,3,3,16,1024]{4,3,2,1,0:T(8,128)(2,1)S(1)}, bf16[2,3,3,16,1024]{4,3,2,1,0:T(8,128)(2,1)S(1)}, u32[]{:S(2)}, u32[]{:S(2)}) %collective-permute-start.2) | collective-permute-done | bytes 589856 | tf_op jit(solution)/shard_map/ppermute | solution.py:148
  58.4 5.3 %collective-permute-start.4 = (bf16[2,3,3,16,1024]{4,3,2,1,0:T(8,128)(2,1)S(1)}, bf16[2,3,3,16,1024]{4,3,2,1,0:T(8,128)(2,1)S(1)}, u32[]{:S(2)}, u32[]{:S(2)}) collective-permute-start(bf16[2,3,3,16,1024]{4,3,2,1,0:T(8,128)(2,1)S(1)} %collective-permute-done.2.c1), channel_id=1, source_target_pairs={{0,8},{1,57},{8,16},{9,1},{16,24},{17,9},{24,32},{25,17},{32,40},{... | collective-permute-start | bytes 1769480 | tf_op jit(solution)/shard_map/ppermute | solution.py:149
  64.4 1.6 %reshape.50 = f32[8,4,2,4,2,2,2]{6,5,4,3,2,1,0:T(2,128)} reshape(f32[2048]{0:T(1024)S(1)} %copy-done.1) | data formatting | bytes 16384 | tf_op jit(solution)/shard_map/reshape | solution.py:160
  67.4 1.9 %collective-permute-start.13 = (bf16[2,5,2,64,128]{4,3,2,1,0:T(8,128)(2,1)S(1)}, bf16[2,5,2,64,128]{4,3,2,1,0:T(8,128)(2,1)S(1)}, u32[]{:S(2)}, u32[]{:S(2)}) collective-permute-start(bf16[2,5,2,64,128]{4,3,2,1,0:T(8,128)(2,1)S(1)} %slice_bitcast_fusion), channel_id=1, source_target_pairs={{0,128},{1,385},{128,256},{129,1},{256,384},{257,129},{384,0},{385... | collective-permute-start | bytes 983048 | tf_op jit(solution)/shard_map/ppermute | solution.py:157
  69.3 1.2 %collective-permute-done.4.c2 = bf16[2,3,3,16,1024]{4,3,2,1,0:T(8,128)(2,1)S(1)} collective-permute-done((bf16[2,3,3,16,1024]{4,3,2,1,0:T(8,128)(2,1)S(1)}, bf16[2,3,3,16,1024]{4,3,2,1,0:T(8,128)(2,1)S(1)}, u32[]{:S(2)}, u32[]{:S(2)}) %collective-permute-start.4) | collective-permute-done | bytes 589856 | tf_op jit(solution)/shard_map/ppermute | solution.py:149
  70.5 5.0 %collective-permute-start.6 = (bf16[2,3,3,16,1024]{4,3,2,1,0:T(8,128)(2,1)S(1)}, bf16[2,3,3,16,1024]{4,3,2,1,0:T(8,128)(2,1)S(1)}, u32[]{:S(2)}, u32[]{:S(2)}) collective-permute-start(bf16[2,3,3,16,1024]{4,3,2,1,0:T(8,128)(2,1)S(1)} %collective-permute-done.4.c2), channel_id=1, source_target_pairs={{0,8},{1,57},{8,16},{9,1},{16,24},{17,9},{24,32},{25,17},{32,40},{... | collective-permute-start | bytes 1769480 | tf_op jit(solution)/shard_map/ppermute | solution.py:150
  75.6 1.9 %collective-permute-start.3 = (bf16[3,3,16,1024]{3,2,1,0:T(8,128)(2,1)S(1)}, bf16[3,3,16,1024]{3,2,1,0:T(8,128)(2,1)S(1)}, u32[]{:S(2)}, u32[]{:S(2)}) collective-permute-start(bf16[3,3,16,1024]{3,2,1,0:T(8,128)(2,1)S(1)} %slice_bitcast_fusion.4), channel_id=1, source_target_pairs={{0,1},{1,0},{2,3},{3,2},{4,5},{5,4},{6,7},{7,6},{8,9},{9,8},{10,11... | collective-permute-start | bytes 884744 | tf_op jit(solution)/shard_map/ppermute | solution.py:49
  77.5 2.4 %collective-permute-start.12 = (bf16[2,2,5,2,64,128]{5,4,3,2,1,0:T(8,128)(2,1)S(1)}, bf16[2,2,5,2,64,128]{5,4,3,2,1,0:T(8,128)(2,1)S(1)}, u32[]{:S(2)}, u32[]{:S(2)}) collective-permute-start(bf16[2,2,5,2,64,128]{5,4,3,2,1,0:T(8,128)(2,1)S(1)} %collective-permute-done.11.e1), channel_id=1, source_target_pairs={{0,1},{1,0},{2,3},{3,2},{4,5},{5,4},{6,7},{7,6},{8,9},{9,8},{10,11... | collective-permute-start | bytes 1966088 | tf_op jit(solution)/shard_map/ppermute | solution.py:49
  80.0 1.9 %collective-permute-start.14 = (bf16[2,5,2,64,128]{4,3,2,1,0:T(8,128)(2,1)S(1)}, bf16[2,5,2,64,128]{4,3,2,1,0:T(8,128)(2,1)S(1)}, u32[]{:S(2)}, u32[]{:S(2)}) collective-permute-start(bf16[2,5,2,64,128]{4,3,2,1,0:T(8,128)(2,1)S(1)} %collective-permute-done.13.e2), channel_id=1, source_target_pairs={{0,1},{1,0},{2,3},{3,2},{4,5},{5,4},{6,7},{7,6},{8,9},{9,8},{10,11... | collective-permute-start | bytes 983048 | tf_op jit(solution)/shard_map/ppermute | solution.py:49
  81.9 2.4 %collective-permute-start.5 = (bf16[3,3,16,1024]{3,2,1,0:T(8,128)(2,1)S(1)}, bf16[3,3,16,1024]{3,2,1,0:T(8,128)(2,1)S(1)}, u32[]{:S(2)}, u32[]{:S(2)}) collective-permute-start(bf16[3,3,16,1024]{3,2,1,0:T(8,128)(2,1)S(1)} %slice_bitcast_fusion.3), channel_id=1, source_target_pairs={{0,1},{1,0},{2,3},{3,2},{4,5},{5,4},{6,7},{7,6},{8,9},{9,8},{10,11... | collective-permute-start | bytes 884744 | tf_op jit(solution)/shard_map/ppermute | solution.py:49
  84.4 3.9 %collective-permute-start.8 = (bf16[3,3,16,1024]{3,2,1,0:T(8,128)(2,1)S(1)}, bf16[3,3,16,1024]{3,2,1,0:T(8,128)(2,1)S(1)}, u32[]{:S(2)}, u32[]{:S(2)}) collective-permute-start(bf16[3,3,16,1024]{3,2,1,0:T(8,128)(2,1)S(1)} %get-tuple-element.9), channel_id=1, source_target_pairs={{0,8},{1,57},{8,16},{9,1},{16,24},{17,9},{24,32},{25,17},{32,40},{... | collective-permute-start | bytes 884744 | tf_op jit(solution)/shard_map/ppermute | solution.py:151
  88.3 1.9 %collective-permute-start.7 = (bf16[3,3,16,1024]{3,2,1,0:T(8,128)(2,1)S(1)}, bf16[3,3,16,1024]{3,2,1,0:T(8,128)(2,1)S(1)}, u32[]{:S(2)}, u32[]{:S(2)}) collective-permute-start(bf16[3,3,16,1024]{3,2,1,0:T(8,128)(2,1)S(1)} %get-tuple-element.10), channel_id=1, source_target_pairs={{0,1},{1,0},{2,3},{3,2},{4,5},{5,4},{6,7},{7,6},{8,9},{9,8},{10,11... | collective-permute-start | bytes 884744 | tf_op jit(solution)/shard_map/ppermute | solution.py:49
  90.4 1.5 %collective-permute-done.8.c4 = bf16[3,3,16,1024]{3,2,1,0:T(8,128)(2,1)S(1)} collective-permute-done((bf16[3,3,16,1024]{3,2,1,0:T(8,128)(2,1)S(1)}, bf16[3,3,16,1024]{3,2,1,0:T(8,128)(2,1)S(1)}, u32[]{:S(2)}, u32[]{:S(2)}) %collective-permute-start.8) | collective-permute-done | bytes 294944 | tf_op jit(solution)/shard_map/ppermute | solution.py:151
  92.0 10.2 %conv.1 = bf16[8,2,64,256]{3,2,1,0:T(8,128)(2,1)S(1)} custom-call(s32[4]{0:T(128)S(1)} %pad_add_fusion.at_ref, bf16[2,3,3,16,1024]{4,3,2,1,0:T(8,128)(2,1)S(1)} %pad_maximum_fusion.1.both, bf16[2,3,3,16,1024]{4,3,2,1,0:T(8,128)(2,1)S(1)} %collective-permute-done.2.c1, bf16[3,3,16,1024]{3,2,1,0:T(8,128)(2,1)S(1)} %collective-permute-done.3.s1, ...), custom_call_target="tpu_custom_call" | custom-call | flops 4899999744 | bytes 6000000 | tf_op jit(solution)/shard_map/conv/pallas_call | solution.py:123
  102.2 15.9 %all_to_all.10 = bf16[8,2,64,256]{3,2,1,0:T(8,128)(2,1)S(1)} all-to-all(bf16[8,2,64,256]{3,2,1,0:T(8,128)(2,1)S(1)} %conv.1), channel_id=1, replica_groups=mesh['x'=4,'zh'=2,'y'=8,'zl'=4,'k'=2] {'k','x'}, dimensions={0} | all-to-all | bytes 1048576 | tf_op jit(solution)/shard_map/all_to_all | solution.py:170
  118.6 1.0 reshape.52
  (46 shorter events, 6.7 us)
Async XLA Ops:
  0.0 1.0 slice-start
  2.6 13.9 %copy-start = (bf16[2,4,64,128]{3,2,1,0:T(8,128)(2,1)S(1)}, bf16[2,4,64,128]{3,2,1,0:T(8,128)(2,1)}, u32[]{:S(2)}) copy-start(bf16[2,4,64,128]{3,2,1,0:T(8,128)(2,1)} %param.3) | copy-start | bytes 393220
  2.6 23.8 %all-to-all-start = ((bf16[32,3,3,2,2,128]{5,4,3,2,1,0:T(2,128)(2,1)}), bf16[32,3,3,2,2,128]{5,4,3,2,1,0:T(2,128)(2,1)S(1)}, u32[]{:S(2)}, u32[]{:S(2)}) async-start(bf16[32,3,3,2,2,128]{5,4,3,2,1,0:T(2,128)(2,1)} %bitcast.7), calls=%async_computation | async-start | bytes 589824 | tf_op jit(solution)/shard_map/all_to_all | solution.py:30
  16.6 9.2 %collective-permute-start = (bf16[1,2,64,128]{3,2,1,0:T(8,128)(2,1)S(1)}, bf16[1,2,64,128]{3,2,1,0:T(8,128)(2,1)S(1)}, u32[]{:S(2)}, u32[]{:S(2)}) collective-permute-start(bf16[1,2,64,128]{3,2,1,0:T(8,128)(2,1)S(1)} %slice_select_fusion), channel_id=1, source_target_pairs={{1,2},{3,4},{5,6},{7,8},{9,10},{11,12},{13,14},{15,16},{17,18},{19... | collective-permute-start | bytes 98312 | tf_op jit(solution)/shard_map/ppermute | solution.py:40
  26.7 10.3 %collective-permute-start.9 = (bf16[5,2,64,128]{3,2,1,0:T(8,128)(2,1)S(1)}, bf16[5,2,64,128]{3,2,1,0:T(8,128)(2,1)S(1)}, u32[]{:S(2)}, u32[]{:S(2)}) collective-permute-start(bf16[5,2,64,128]{3,2,1,0:T(8,128)(2,1)S(1)} %pad_maximum_fusion.3), channel_id=1, source_target_pairs={{0,64},{64,0},{1,65},{65,1},{2,66},{66,2},{3,67},{67,3},{4,68},{68... | collective-permute-start | bytes 491528 | tf_op jit(solution)/shard_map/ppermute | solution.py:154
  32.3 14.9 %collective-permute-start.1 = (bf16[3,3,16,1024]{3,2,1,0:T(8,128)(2,1)S(1)}, bf16[3,3,16,1024]{3,2,1,0:T(8,128)(2,1)S(1)}, u32[]{:S(2)}, u32[]{:S(2)}) collective-permute-start(bf16[3,3,16,1024]{3,2,1,0:T(8,128)(2,1)S(1)} %reshape.49), channel_id=1, source_target_pairs={{0,1},{1,0},{2,3},{3,2},{4,5},{5,4},{6,7},{7,6},{8,9},{9,8},{10,11... | collective-permute-start | bytes 884744 | tf_op jit(solution)/shard_map/ppermute | solution.py:49
  37.1 14.5 %collective-permute-start.10 = (bf16[2,5,2,64,128]{4,3,2,1,0:T(8,128)(2,1)S(1)}, bf16[2,5,2,64,128]{4,3,2,1,0:T(8,128)(2,1)S(1)}, u32[]{:S(2)}, u32[]{:S(2)}) collective-permute-start(bf16[2,5,2,64,128]{4,3,2,1,0:T(8,128)(2,1)S(1)} %get-tuple-element.12), channel_id=1, source_target_pairs={{0,1},{1,0},{2,3},{3,2},{4,5},{5,4},{6,7},{7,6},{8,9},{9,8},{10,11... | collective-permute-start | bytes 983048 | tf_op jit(solution)/shard_map/ppermute | solution.py:49
  47.2 11.2 %collective-permute-start.2 = (bf16[2,3,3,16,1024]{4,3,2,1,0:T(8,128)(2,1)S(1)}, bf16[2,3,3,16,1024]{4,3,2,1,0:T(8,128)(2,1)S(1)}, u32[]{:S(2)}, u32[]{:S(2)}) collective-permute-start(bf16[2,3,3,16,1024]{4,3,2,1,0:T(8,128)(2,1)S(1)} %pad_maximum_fusion.1.both), channel_id=1, source_target_pairs={{0,8},{1,57},{8,16},{9,1},{16,24},{17,9},{24,32},{25,17},{32,40},{... | collective-permute-start | bytes 1769480 | tf_op jit(solution)/shard_map/ppermute | solution.py:148
  51.7 15.7 %collective-permute-start.11 = (bf16[2,2,5,2,64,128]{5,4,3,2,1,0:T(8,128)(2,1)S(1)}, bf16[2,2,5,2,64,128]{5,4,3,2,1,0:T(8,128)(2,1)S(1)}, u32[]{:S(2)}, u32[]{:S(2)}) collective-permute-start(bf16[2,2,5,2,64,128]{5,4,3,2,1,0:T(8,128)(2,1)S(1)} %pad_maximum_fusion.ab), channel_id=1, source_target_pairs={{0,128},{1,385},{128,256},{129,1},{256,384},{257,129},{384,0},{385... | collective-permute-start | bytes 1966088 | tf_op jit(solution)/shard_map/ppermute | solution.py:156
  58.4 12.1 %collective-permute-start.4 = (bf16[2,3,3,16,1024]{4,3,2,1,0:T(8,128)(2,1)S(1)}, bf16[2,3,3,16,1024]{4,3,2,1,0:T(8,128)(2,1)S(1)}, u32[]{:S(2)}, u32[]{:S(2)}) collective-permute-start(bf16[2,3,3,16,1024]{4,3,2,1,0:T(8,128)(2,1)S(1)} %collective-permute-done.2.c1), channel_id=1, source_target_pairs={{0,8},{1,57},{8,16},{9,1},{16,24},{17,9},{24,32},{25,17},{32,40},{... | collective-permute-start | bytes 1769480 | tf_op jit(solution)/shard_map/ppermute | solution.py:149
  63.7 0.7 copy-start.1
  67.4 12.6 %collective-permute-start.13 = (bf16[2,5,2,64,128]{4,3,2,1,0:T(8,128)(2,1)S(1)}, bf16[2,5,2,64,128]{4,3,2,1,0:T(8,128)(2,1)S(1)}, u32[]{:S(2)}, u32[]{:S(2)}) collective-permute-start(bf16[2,5,2,64,128]{4,3,2,1,0:T(8,128)(2,1)S(1)} %slice_bitcast_fusion), channel_id=1, source_target_pairs={{0,128},{1,385},{128,256},{129,1},{256,384},{257,129},{384,0},{385... | collective-permute-start | bytes 983048 | tf_op jit(solution)/shard_map/ppermute | solution.py:157
  70.5 13.8 %collective-permute-start.6 = (bf16[2,3,3,16,1024]{4,3,2,1,0:T(8,128)(2,1)S(1)}, bf16[2,3,3,16,1024]{4,3,2,1,0:T(8,128)(2,1)S(1)}, u32[]{:S(2)}, u32[]{:S(2)}) collective-permute-start(bf16[2,3,3,16,1024]{4,3,2,1,0:T(8,128)(2,1)S(1)} %collective-permute-done.4.c2), channel_id=1, source_target_pairs={{0,8},{1,57},{8,16},{9,1},{16,24},{17,9},{24,32},{25,17},{32,40},{... | collective-permute-start | bytes 1769480 | tf_op jit(solution)/shard_map/ppermute | solution.py:150
  75.6 12.7 %collective-permute-start.3 = (bf16[3,3,16,1024]{3,2,1,0:T(8,128)(2,1)S(1)}, bf16[3,3,16,1024]{3,2,1,0:T(8,128)(2,1)S(1)}, u32[]{:S(2)}, u32[]{:S(2)}) collective-permute-start(bf16[3,3,16,1024]{3,2,1,0:T(8,128)(2,1)S(1)} %slice_bitcast_fusion.4), channel_id=1, source_target_pairs={{0,1},{1,0},{2,3},{3,2},{4,5},{5,4},{6,7},{7,6},{8,9},{9,8},{10,11... | collective-permute-start | bytes 884744 | tf_op jit(solution)/shard_map/ppermute | solution.py:49
  77.5 12.9 %collective-permute-start.12 = (bf16[2,2,5,2,64,128]{5,4,3,2,1,0:T(8,128)(2,1)S(1)}, bf16[2,2,5,2,64,128]{5,4,3,2,1,0:T(8,128)(2,1)S(1)}, u32[]{:S(2)}, u32[]{:S(2)}) collective-permute-start(bf16[2,2,5,2,64,128]{5,4,3,2,1,0:T(8,128)(2,1)S(1)} %collective-permute-done.11.e1), channel_id=1, source_target_pairs={{0,1},{1,0},{2,3},{3,2},{4,5},{5,4},{6,7},{7,6},{8,9},{9,8},{10,11... | collective-permute-start | bytes 1966088 | tf_op jit(solution)/shard_map/ppermute | solution.py:49
  80.0 10.5 %collective-permute-start.14 = (bf16[2,5,2,64,128]{4,3,2,1,0:T(8,128)(2,1)S(1)}, bf16[2,5,2,64,128]{4,3,2,1,0:T(8,128)(2,1)S(1)}, u32[]{:S(2)}, u32[]{:S(2)}) collective-permute-start(bf16[2,5,2,64,128]{4,3,2,1,0:T(8,128)(2,1)S(1)} %collective-permute-done.13.e2), channel_id=1, source_target_pairs={{0,1},{1,0},{2,3},{3,2},{4,5},{5,4},{6,7},{7,6},{8,9},{9,8},{10,11... | collective-permute-start | bytes 983048 | tf_op jit(solution)/shard_map/ppermute | solution.py:49
  81.9 8.5 %collective-permute-start.5 = (bf16[3,3,16,1024]{3,2,1,0:T(8,128)(2,1)S(1)}, bf16[3,3,16,1024]{3,2,1,0:T(8,128)(2,1)S(1)}, u32[]{:S(2)}, u32[]{:S(2)}) collective-permute-start(bf16[3,3,16,1024]{3,2,1,0:T(8,128)(2,1)S(1)} %slice_bitcast_fusion.3), channel_id=1, source_target_pairs={{0,1},{1,0},{2,3},{3,2},{4,5},{5,4},{6,7},{7,6},{8,9},{9,8},{10,11... | collective-permute-start | bytes 884744 | tf_op jit(solution)/shard_map/ppermute | solution.py:49
  84.4 7.5 %collective-permute-start.8 = (bf16[3,3,16,1024]{3,2,1,0:T(8,128)(2,1)S(1)}, bf16[3,3,16,1024]{3,2,1,0:T(8,128)(2,1)S(1)}, u32[]{:S(2)}, u32[]{:S(2)}) collective-permute-start(bf16[3,3,16,1024]{3,2,1,0:T(8,128)(2,1)S(1)} %get-tuple-element.9), channel_id=1, source_target_pairs={{0,8},{1,57},{8,16},{9,1},{16,24},{17,9},{24,32},{25,17},{32,40},{... | collective-permute-start | bytes 884744 | tf_op jit(solution)/shard_map/ppermute | solution.py:151
  88.3 3.6 %collective-permute-start.7 = (bf16[3,3,16,1024]{3,2,1,0:T(8,128)(2,1)S(1)}, bf16[3,3,16,1024]{3,2,1,0:T(8,128)(2,1)S(1)}, u32[]{:S(2)}, u32[]{:S(2)}) collective-permute-start(bf16[3,3,16,1024]{3,2,1,0:T(8,128)(2,1)S(1)} %get-tuple-element.10), channel_id=1, source_target_pairs={{0,1},{1,0},{2,3},{3,2},{4,5},{5,4},{6,7},{7,6},{8,9},{9,8},{10,11... | collective-permute-start | bytes 884744 | tf_op jit(solution)/shard_map/ppermute | solution.py:49

commit v3 on v2

--- a/solution.py
+++ b/solution.py
@@ -1,5 +1,3 @@
-import functools
-
 import jax
 import jax.numpy as jnp
 from jax import lax
@@ -14,6 +12,14 @@
 
 def ring(size, step):
     return [(i, (i + step) % size) for i in range(size)]
+
+
+def two_way(size):
+    return [(2 * i + k, 2 * ((i + 1 - 2 * k) % size) + k) for i in range(size) for k in range(NK)]
+
+
+def swap_cores(array):
+    return lax.ppermute(array, "k", ring(NK, 1))
 
 
 def spread_kernel(kernel):
@@ -33,27 +39,17 @@
 
 
 def own_rows(latent):
-    core = lax.axis_index("k")
     rows = jnp.transpose(latent, (1, 0, 2, 3))
-    edge = jnp.where(core == 0, rows[:1], rows[3:])
+    edge = jnp.where(lax.axis_index("k") == 0, rows[:1], rows[3:])
     pairs = [(2 * i + 1, 2 * i + 2) for i in range(31)]
     halo = lax.ppermute(edge, ("y", "zl", "k"), pairs + [(b, a) for a, b in pairs])
     return jnp.concatenate([rows, halo], axis=0)
 
 
-def two_way(size):
-    return [(2 * i + k, 2 * ((i + 1 - 2 * k) % size) + k) for i in range(size) for k in range(NK)]
-
-
-def swap_cores(array):
-    return lax.ppermute(array, "k", ring(NK, 1))
-
-
 def conv_kernel(
-    at_ref, both, c1, s1, c2, s2, c3, s3, c4, ab, e1, e1s, e2, e2s, bias_ref, perm_ref, out_ref,
-    w_ref, x_ref, sems,
+    at_ref, mine, other, both, c1, s1, c2, s2, c3, s3, c4, bias_ref, perm_ref, out_ref, w_ref, x_ref, sems
 ):
-    x, zh, y, core = at_ref[0], at_ref[1], at_ref[2], at_ref[3]
+    zh, core, y = at_ref[0], at_ref[1], at_ref[2]
     copies = []
 
     def start(src, dst):
@@ -61,24 +57,14 @@
         copy.start()
         copies.append(copy)
 
-    def rows_in(piece, x_from, owner):
-        first = jnp.where(owner == 0, 1, 5)
-        beyond = jnp.where(owner == 0, 0, 9)
-        for j, chan in enumerate((2 * x_from + zh, 2 * x_from + 1 - zh)):
-            start(piece.at[j, pl.ds(0, 4)], x_ref.at[pl.ds(first, 4), :, chan])
-            start(piece.at[j, pl.ds(4, 1)], x_ref.at[pl.ds(beyond, 1), :, chan])
-
-    there = 1 - core
-    near, back = lax.rem(x + 3 + 2 * core, 4), lax.rem(x + 1 + 2 * core, 4)
-    far = lax.rem(x + 2, 4)
-    rows_in(ab.at[0], x, core)
-    rows_in(ab.at[1], x, there)
-    rows_in(e1.at[0], near, core)
-    rows_in(e1.at[1], near, there)
-    rows_in(e1s.at[0], back, there)
-    rows_in(e1s.at[1], back, core)
-    rows_in(e2, far, core)
-    rows_in(e2s, far, there)
+    for piece, owner in ((mine, core), (other, 1 - core)):
+        top = jnp.where(owner == 0, 1, 5)
+        edge = jnp.where(owner == 0, 0, 9)
+        for x in range(NX):
+            for j in range(2):
+                chan = 2 * x + (zh if j == 0 else 1 - zh)
+                start(piece.at[x, j, pl.ds(0, 4)], x_ref.at[pl.ds(top, 4), :, chan])
+                start(piece.at[x, j, pl.ds(4, 1)], x_ref.at[pl.ds(edge, 1), :, chan])
     sign = 1 - 2 * core
     start(both.at[0], w_ref.at[:, :, y])
     for n, (chunk, swapped) in enumerate(((c1, s1), (c2, s2), (c3, s3))):
@@ -118,57 +104,53 @@
     lax.fori_loop(0, 8, step, 0)
 
 
-def convolve(at, chunks, pieces, bias, perm):
-    n_any = len(chunks) + len(pieces)
+def convolve(at, rows, chunks, bias, perm):
     return pl.pallas_call(
         conv_kernel,
         out_shape=jax.ShapeDtypeStruct((8, 2, 64, 256), jnp.bfloat16),
         in_specs=[pl.BlockSpec(memory_space=pltpu.SMEM)]
-        + [pl.BlockSpec(memory_space=pl.ANY)] * n_any
+        + [pl.BlockSpec(memory_space=pl.ANY)] * 10
         + [pl.BlockSpec(memory_space=pltpu.VMEM)] * 2,
         out_specs=pl.BlockSpec(memory_space=pltpu.VMEM),
         scratch_shapes=[
-            pltpu.VMEM((3, 3, 8, 16, 1024), jnp.bfloat16),
+            pltpu.VMEM((3, 3, NY, 16, 1024), jnp.bfloat16),
             pltpu.VMEM((10, 2, 8, 64, 128), jnp.bfloat16),
             pltpu.SemaphoreType.DMA((40,)),
         ],
-        compiler_params=pltpu.CompilerParams(vmem_limit_bytes=40 * 1024 * 1024),
+        compiler_params=pltpu.CompilerParams(vmem_limit_bytes=32 * 1024 * 1024),
         cost_estimate=pl.CostEstimate(flops=4_900_000_000, bytes_accessed=6_000_000, transcendentals=0),
         name="conv",
-    )(at, *chunks, *pieces, bias, perm)
+    )(at, *rows, *chunks, bias, perm)
 
 
 def local(latent, kernel, bias):
     x, zh, y, core = (lax.axis_index(a) for a in ("x", "zh", "y", "k"))
+    picked = bias.reshape(NY, NL, NK, NX, 2, NH, 2)[:, :, core, x, :, zh, :]
+    column = jnp.transpose(picked, (0, 3, 1, 2)).reshape(128, 1)
+    column = jnp.broadcast_to(column, (128, 128))
     rows = own_rows(latent)
     own = own_chunk(kernel)
-    own, rows = lax.optimization_barrier((own, rows))
+    own, rows, column = lax.optimization_barrier((own, rows, column))
 
     both = jnp.stack([own, swap_cores(own)])
     c1 = lax.ppermute(both, ("y", "k"), two_way(NY))
+    rows = jnp.stack([rows, lax.ppermute(rows, "zh", ring(NH, 1))])
+    c1, rows = lax.optimization_barrier((c1, rows))
     c2 = lax.ppermute(c1, ("y", "k"), two_way(NY))
+    mine = lax.all_to_all(jnp.broadcast_to(rows, (NX, *rows.shape)), "x", 0, 0, tiled=True)
+    s1 = swap_cores(c1[1])
     c3 = lax.ppermute(c2, ("y", "k"), two_way(NY))
+    s2 = swap_cores(c2[1])
+    c3, mine, s1, s2 = lax.optimization_barrier((c3, mine, s1, s2))
     c4 = lax.ppermute(c3[0], ("y", "k"), two_way(NY))
-    s1, s2, s3 = swap_cores(c1[1]), swap_cores(c2[1]), swap_cores(c3[1])
+    other = swap_cores(mine)
+    s3 = swap_cores(c3[1])
 
-    rows = jnp.stack([rows, lax.ppermute(rows, "zh", ring(NH, 1))])
-    ab = jnp.stack([rows, swap_cores(rows)])
-    e1 = lax.ppermute(ab, ("x", "k"), two_way(NX))
-    e2 = lax.ppermute(e1[0], ("x", "k"), two_way(NX))
-    e1s, e2s = swap_cores(e1), swap_cores(e2)
-
-    split = bias.reshape(NY, NL, NK, NX, 2, NH, 2)
-    picked = split[:, :, core, x, :, zh, :]
-    column = jnp.transpose(picked, (0, 3, 1, 2)).reshape(128, 1)
-    column = jnp.broadcast_to(column, (128, 128))
     place = jnp.arange(256)
-    perm = (2 * (place % 128) + place // 128)[:, None] == place[None, :]
-    at = jnp.stack([x, zh, y, core]).astype(jnp.int32)
-    out = convolve(
-        at, (both, c1, s1, c2, s2, c3, s3, c4), (ab, e1, e1s, e2, e2s), column, perm.astype(jnp.bfloat16)
-    )
-    got = lax.all_to_all(out, ("k", "x"), 0, 0, tiled=True)
-    got = got.reshape(NK, NX, 2, 32, 2, 256)
+    perm = ((2 * (place % 128) + place // 128)[:, None] == place[None, :]).astype(jnp.bfloat16)
+    at = jnp.stack([zh, core, y]).astype(jnp.int32)
+    out = convolve(at, (mine, other), (both, c1, s1, c2, s2, c3, s3, c4), column, perm)
+    got = lax.all_to_all(out, ("k", "x"), 0, 0, tiled=True).reshape(NK, NX, 2, NY * NL, 2, 256)
     return jnp.transpose(got, (2, 3, 0, 1, 4, 5)).reshape(2, 1, 512, 256)
 
 

time: 120 us -> 117 us (0.975)
  starting transfers between devices: 71.5 us -> 58.6 us
  waiting for transfers between devices: 13.1 us -> 22.6 us
  blocking collectives: 15.9 us -> 13.8 us
  local copies, waits for them, and re-layouts: 6.8 us -> 8.5 us
    ppermute x7 -> x5, starting transfers between devices: 25.4 us -> 16.9 us  [swap_cores(): return lax.ppermute(array, 'k', ring(NK, 1))]
    ppermute x1, waiting for transfers between devices: 0.01 us -> 7.95 us  [local(): rows = jnp.stack([rows, lax.ppermute(rows, 'zh', ring(NH, 1))])]
    ppermute x1, waiting for transfers between devices: 4.8 us -> 0.01 us  [local(): c1 = lax.ppermute(both, ('y', 'k'), two_way(NY))]
    all_to_all x0 -> x1, starting transfers between devices: none -> 4.39 us  [local(): lax.all_to_all(jnp.broadcast_to(rows, (NX, *rows.shape)), 'x', 0, 0, tile...]
    ppermute x2 -> x0, starting transfers between devices: 3.84 us -> none  [the longest x1 1.92 us: local(): e1 = lax.ppermute(ab, ('x', 'k'), two_way(NX))]
    all_to_all x0 -> x1, waiting for transfers between devices: none -> 3.54 us  [local(): lax.all_to_all(jnp.broadcast_to(rows, (NX, *rows.shape)), 'x', 0, 0, tile...]
    ppermute x7 -> x5, waiting for transfers between devices: 0.02 us -> 2.73 us  [swap_cores(): return lax.ppermute(array, 'k', ring(NK, 1))]
    all_to_all x1, blocking collectives: 15.9 us -> 13.8 us  [local(): lax.all_to_all(out, ('k', 'x'), 0, 0, tiled=True)]
  transfers between devices with their start and end apart: 16 -> 13, of which waited for: 5 -> 8; matrix products, arithmetic and copies ran while one was open for 3% -> 3% of each run, Pallas kernels for 0% -> 0%
where the time goes in v3:
time: 117 us; the launch traced here: 116 us
  starting transfers between devices  58.6 us (50%)
  waiting for transfers between devices  22.6 us (19%)
  blocking collectives  13.8 us (12%)
  Pallas kernels  11 us (9%)
  local copies, waits for them, and re-layouts  8.5 us (7%)
  other arithmetic  1.64 us (1%)
    ppermute x5, starting transfers between devices, swap_cores(): return lax.ppermute(array, 'k', ring(NK, 1))  16.9 us
    all_to_all x1, blocking collectives, local(): lax.all_to_all(out, ('k', 'x'), 0, 0, tiled=True)  13.8 us
    all_to_all x1, starting transfers between devices, own_chunk(): got = lax.all_to_all(pieces, ('x', 'zh', 'zl'), 0, 0, tiled=True)  13.7 us
    pallas_call x1, Pallas kernels, convolve(): pl.pallas_call(conv_kernel, out_shape=jax.ShapeDtypeStruct((8, 2, 64, 256...  11 us
    ppermute x1, waiting for transfers between devices, local(): rows = jnp.stack([rows, lax.ppermute(rows, 'zh', ring(NH, 1))])  7.95 us
    ppermute x1, starting transfers between devices, local(): c3 = lax.ppermute(c2, ('y', 'k'), two_way(NY))  4.6 us
    all_to_all x1, starting transfers between devices, local(): lax.all_to_all(jnp.broadcast_to(rows, (NX, *rows.shape)), 'x', 0, 0, tile...  4.39 us
    ppermute x1, starting transfers between devices, own_rows(): lax.ppermute(edge, ('y', 'zl', 'k'), pairs + [(b, a) for a, b in pairs])  4.26 us
  transfers between devices with their start and end apart: 13, of which 8 were waited for; matrix products, arithmetic and copies ran while one was open for 3% of the time, Pallas kernels for 0%

profile of v3, /device:TPU:1, one launch (start us, length us, event | category | flops | bytes accessed | tf_op | source)
XLA Modules:
  0.0 116.4 jit_solution(12118875919478543057)
XLA Ops:
  3.5 13.7 %all-to-all-start = ((bf16[32,3,3,2,2,128]{5,4,3,2,1,0:T(2,128)(2,1)}), bf16[32,3,3,2,2,128]{5,4,3,2,1,0:T(2,128)(2,1)S(1)}, u32[]{:S(2)}, u32[]{:S(2)}) async-start(bf16[32,3,3,2,2,128]{5,4,3,2,1,0:T(2,128)(2,1)} %bitcast.6), calls=%async_computation | async-start | bytes 589824 | tf_op jit(solution)/shard_map/all_to_all | solution.py:36
  17.3 4.3 %collective-permute-start = (bf16[1,2,64,128]{3,2,0,1:T(8,128)(2,1)S(1)}, bf16[1,2,64,128]{3,2,0,1:T(8,128)(2,1)S(1)}, u32[]{:S(2)}, u32[]{:S(2)}) collective-permute-start(bf16[1,2,64,128]{3,2,0,1:T(8,128)(2,1)S(1)} %slice_select_fusion), channel_id=1, source_target_pairs={{1,2},{3,4},{5,6},{7,8},{9,10},{11,12},{13,14},{15,16},{17,18},{19... | collective-permute-start | bytes 98312 | tf_op jit(solution)/shard_map/ppermute | solution.py:45
  22.9 3.6 %collective-permute-done = bf16[1,2,64,128]{3,2,0,1:T(8,128)(2,1)S(1)} collective-permute-done((bf16[1,2,64,128]{3,2,0,1:T(8,128)(2,1)S(1)}, bf16[1,2,64,128]{3,2,0,1:T(8,128)(2,1)S(1)}, u32[]{:S(2)}, u32[]{:S(2)}) %collective-permute-start) | collective-permute-done | bytes 32800 | tf_op jit(solution)/shard_map/ppermute | solution.py:45
  27.5 7.1 %collective-permute-start.1 = (bf16[3,3,16,1024]{3,2,1,0:T(8,128)(2,1)S(1)}, bf16[3,3,16,1024]{3,2,1,0:T(8,128)(2,1)S(1)}, u32[]{:S(2)}, u32[]{:S(2)}) collective-permute-start(bf16[3,3,16,1024]{3,2,1,0:T(8,128)(2,1)S(1)} %reshape.49), channel_id=1, source_target_pairs={{0,1},{1,0},{2,3},{3,2},{4,5},{5,4},{6,7},{7,6},{8,9},{9,8},{10,11... | collective-permute-start | bytes 884744 | tf_op jit(solution)/shard_map/ppermute | solution.py:22
  34.6 1.2 %collective-permute-done.1 = bf16[3,3,16,1024]{3,2,1,0:T(8,128)(2,1)S(1)} collective-permute-done((bf16[3,3,16,1024]{3,2,1,0:T(8,128)(2,1)S(1)}, bf16[3,3,16,1024]{3,2,1,0:T(8,128)(2,1)S(1)}, u32[]{:S(2)}, u32[]{:S(2)}) %collective-permute-start.1) | collective-permute-done | bytes 294944 | tf_op jit(solution)/shard_map/ppermute | solution.py:22
  35.9 3.9 %collective-permute-start.2 = (bf16[2,3,3,16,1024]{4,3,2,1,0:T(8,128)(2,1)S(1)}, bf16[2,3,3,16,1024]{4,3,2,1,0:T(8,128)(2,1)S(1)}, u32[]{:S(2)}, u32[]{:S(2)}) collective-permute-start(bf16[2,3,3,16,1024]{4,3,2,1,0:T(8,128)(2,1)S(1)} %pad_maximum_fusion.both), channel_id=1, source_target_pairs={{0,8},{1,57},{8,16},{9,1},{16,24},{17,9},{24,32},{25,17},{32,40},{... | collective-permute-start | bytes 1769480 | tf_op jit(solution)/shard_map/ppermute | solution.py:136
  39.8 3.9 %collective-permute-start.3 = (bf16[5,2,64,128]{3,2,0,1:T(8,128)(2,1)S(1)}, bf16[5,2,64,128]{3,2,0,1:T(8,128)(2,1)S(1)}, u32[]{:S(2)}, u32[]{:S(2)}) collective-permute-start(bf16[5,2,64,128]{3,2,0,1:T(8,128)(2,1)S(1)} %pad_maximum_fusion.2), channel_id=1, source_target_pairs={{0,64},{64,0},{1,65},{65,1},{2,66},{66,2},{3,67},{67,3},{4,68},{68... | collective-permute-start | bytes 491528 | tf_op jit(solution)/shard_map/ppermute | solution.py:137
  43.7 7.9 %collective-permute-done.3 = bf16[5,2,64,128]{3,2,0,1:T(8,128)(2,1)S(1)} collective-permute-done((bf16[5,2,64,128]{3,2,0,1:T(8,128)(2,1)S(1)}, bf16[5,2,64,128]{3,2,0,1:T(8,128)(2,1)S(1)}, u32[]{:S(2)}, u32[]{:S(2)}) %collective-permute-start.3) | collective-permute-done | bytes 163872 | tf_op jit(solution)/shard_map/ppermute | solution.py:137
  51.7 3.7 %collective-permute-start.4 = (bf16[2,3,3,16,1024]{4,3,2,1,0:T(8,128)(2,1)S(1)}, bf16[2,3,3,16,1024]{4,3,2,1,0:T(8,128)(2,1)}, u32[]{:S(2)}, u32[]{:S(2)}) collective-permute-start(bf16[2,3,3,16,1024]{4,3,2,1,0:T(8,128)(2,1)S(1)} %collective-permute-done.2.c1), channel_id=1, source_target_pairs={{0,8},{1,57},{8,16},{9,1},{16,24},{17,9},{24,32},{25,17},{32,40},{... | collective-permute-start | bytes 1769480 | tf_op jit(solution)/shard_map/ppermute | solution.py:139
  55.5 1.4 %broadcast_in_dim.23 = bf16[4,2,5,2,64,128]{5,4,3,2,1,0:T(8,128)(2,1)} broadcast(bf16[2,5,2,64,128]{4,3,2,1,0:T(8,128)(2,1)S(1)} %copy.21), dimensions={1,2,3,4,5} | broadcast | bytes 1638400 | tf_op jit(solution)/shard_map/broadcast_in_dim | solution.py:140
  56.9 4.4 %all-to-all-start.1 = ((bf16[4,2,5,2,64,128]{5,4,3,2,1,0:T(8,128)(2,1)}), bf16[4,2,5,2,64,128]{5,4,3,2,1,0:T(8,128)(2,1)S(1)}, u32[]{:S(2)}, u32[]{:S(2)}) async-start(bf16[4,2,5,2,64,128]{5,4,3,2,1,0:T(8,128)(2,1)} %broadcast_in_dim.23), calls=%async_computation.1 | async-start | bytes 2621440 | tf_op jit(solution)/shard_map/all_to_all | solution.py:140
  61.3 1.5 %collective-permute-done.4.c2 = bf16[2,3,3,16,1024]{4,3,2,1,0:T(8,128)(2,1)} collective-permute-done((bf16[2,3,3,16,1024]{4,3,2,1,0:T(8,128)(2,1)S(1)}, bf16[2,3,3,16,1024]{4,3,2,1,0:T(8,128)(2,1)}, u32[]{:S(2)}, u32[]{:S(2)}) %collective-permute-start.4) | collective-permute-done | bytes 589856 | tf_op jit(solution)/shard_map/ppermute | solution.py:139
  62.8 4.6 %collective-permute-start.5 = (bf16[2,3,3,16,1024]{4,3,2,1,0:T(8,128)(2,1)}, bf16[2,3,3,16,1024]{4,3,2,1,0:T(8,128)(2,1)S(1)}, u32[]{:S(2)}, u32[]{:S(2)}) collective-permute-start(bf16[2,3,3,16,1024]{4,3,2,1,0:T(8,128)(2,1)} %collective-permute-done.4.c2), channel_id=1, source_target_pairs={{0,8},{1,57},{8,16},{9,1},{16,24},{17,9},{24,32},{25,17},{32,40},{... | collective-permute-start | bytes 1769480 | tf_op jit(solution)/shard_map/ppermute | solution.py:142
  67.4 3.0 %collective-permute-start.6 = (bf16[3,3,16,1024]{3,2,1,0:T(8,128)(2,1)S(1)}, bf16[3,3,16,1024]{3,2,1,0:T(8,128)(2,1)S(1)}, u32[]{:S(2)}, u32[]{:S(2)}) collective-permute-start(bf16[3,3,16,1024]{3,2,1,0:T(8,128)(2,1)S(1)} %slice_bitcast_fusion.3), channel_id=1, source_target_pairs={{0,1},{1,0},{2,3},{3,2},{4,5},{5,4},{6,7},{7,6},{8,9},{9,8},{10,11... | collective-permute-start | bytes 884744 | tf_op jit(solution)/shard_map/ppermute | solution.py:22
  71.3 1.9 %collective-permute-start.7 = (bf16[3,3,16,1024]{3,2,1,0:T(8,128)(2,1)S(1)}, bf16[3,3,16,1024]{3,2,1,0:T(8,128)(2,1)S(1)}, u32[]{:S(2)}, u32[]{:S(2)}) collective-permute-start(bf16[3,3,16,1024]{3,2,1,0:T(8,128)(2,1)S(1)} %slice_bitcast_fusion), channel_id=1, source_target_pairs={{0,1},{1,0},{2,3},{3,2},{4,5},{5,4},{6,7},{7,6},{8,9},{9,8},{10,11... | collective-permute-start | bytes 884744 | tf_op jit(solution)/shard_map/ppermute | solution.py:22
  73.3 1.5 %collective-permute-done.7.s2 = bf16[3,3,16,1024]{3,2,1,0:T(8,128)(2,1)S(1)} collective-permute-done((bf16[3,3,16,1024]{3,2,1,0:T(8,128)(2,1)S(1)}, bf16[3,3,16,1024]{3,2,1,0:T(8,128)(2,1)S(1)}, u32[]{:S(2)}, u32[]{:S(2)}) %collective-permute-start.7) | collective-permute-done | bytes 294944 | tf_op jit(solution)/shard_map/ppermute | solution.py:22
  75.5 3.5 %all-to-all-done.1.mine = bf16[4,2,5,2,64,128]{5,4,3,2,1,0:T(8,128)(2,1)S(1)} async-done(((bf16[4,2,5,2,64,128]{5,4,3,2,1,0:T(8,128)(2,1)}), bf16[4,2,5,2,64,128]{5,4,3,2,1,0:T(8,128)(2,1)S(1)}, u32[]{:S(2)}, u32[]{:S(2)}) %all-to-all-start.1) | async-done | bytes 1310752 | tf_op jit(solution)/shard_map/all_to_all | solution.py:140
  79.1 2.9 %collective-permute-start.8 = (bf16[4,2,5,2,64,128]{5,4,3,2,1,0:T(8,128)(2,1)S(1)}, bf16[4,2,5,2,64,128]{5,4,3,2,1,0:T(8,128)(2,1)}, u32[]{:S(2)}, u32[]{:S(2)}) collective-permute-start(bf16[4,2,5,2,64,128]{5,4,3,2,1,0:T(8,128)(2,1)S(1)} %all-to-all-done.1.mine), channel_id=1, source_target_pairs={{0,1},{1,0},{2,3},{3,2},{4,5},{5,4},{6,7},{7,6},{8,9},{9,8},{10,11... | collective-permute-start | bytes 3932168 | tf_op jit(solution)/shard_map/ppermute | solution.py:22
  82.1 3.2 %collective-permute-start.10 = (bf16[3,3,16,1024]{3,2,1,0:T(8,128)(2,1)S(1)}, bf16[3,3,16,1024]{3,2,1,0:T(8,128)(2,1)S(1)}, u32[]{:S(2)}, u32[]{:S(2)}) collective-permute-start(bf16[3,3,16,1024]{3,2,1,0:T(8,128)(2,1)S(1)} %get-tuple-element.23), channel_id=1, source_target_pairs={{0,8},{1,57},{8,16},{9,1},{16,24},{17,9},{24,32},{25,17},{32,40},{... | collective-permute-start | bytes 884744 | tf_op jit(solution)/shard_map/ppermute | solution.py:145
  85.3 1.9 %collective-permute-start.9 = (bf16[3,3,16,1024]{3,2,1,0:T(8,128)(2,1)S(1)}, bf16[3,3,16,1024]{3,2,1,0:T(8,128)(2,1)S(1)}, u32[]{:S(2)}, u32[]{:S(2)}) collective-permute-start(bf16[3,3,16,1024]{3,2,1,0:T(8,128)(2,1)S(1)} %get-tuple-element.24), channel_id=1, source_target_pairs={{0,1},{1,0},{2,3},{3,2},{4,5},{5,4},{6,7},{7,6},{8,9},{9,8},{10,11... | collective-permute-start | bytes 884744 | tf_op jit(solution)/shard_map/ppermute | solution.py:22
  87.4 2.6 %collective-permute-done.10.c4 = bf16[3,3,16,1024]{3,2,1,0:T(8,128)(2,1)S(1)} collective-permute-done((bf16[3,3,16,1024]{3,2,1,0:T(8,128)(2,1)S(1)}, bf16[3,3,16,1024]{3,2,1,0:T(8,128)(2,1)S(1)}, u32[]{:S(2)}, u32[]{:S(2)}) %collective-permute-start.10) | collective-permute-done | bytes 294944 | tf_op jit(solution)/shard_map/ppermute | solution.py:145
  90.0 11.0 %conv.1 = bf16[8,2,64,256]{3,2,1,0:T(8,128)(2,1)S(1)} custom-call(s32[3]{0:T(128)S(1)} %pad_add_fusion.at_ref, bf16[4,2,5,2,64,128]{5,4,3,2,1,0:T(8,128)(2,1)S(1)} %all-to-all-done.1.mine, bf16[4,2,5,2,64,128]{5,4,3,2,1,0:T(8,128)(2,1)} %collective-permute-done.8.other, bf16[2,3,3,16,1024]{4,3,2,1,0:T(8,128)(2,1)S(1)} %pad_maximum_fusion.both, ...), custom_call_target="tpu_custom_call" | custom-call | flops 4899999744 | bytes 6000000 | tf_op jit(solution)/shard_map/conv/pallas_call | solution.py:108
  101.0 13.8 %all_to_all.15 = bf16[8,2,64,256]{3,2,1,0:T(8,128)(2,1)S(1)} all-to-all(bf16[8,2,64,256]{3,2,1,0:T(8,128)(2,1)S(1)} %conv.1), channel_id=1, replica_groups=mesh['x'=4,'zh'=2,'y'=8,'zl'=4,'k'=2] {'k','x'}, dimensions={0} | all-to-all | bytes 1048576 | tf_op jit(solution)/shard_map/all_to_all | solution.py:153
  115.5 1.0 reshape.52
  (42 shorter events, 8.4 us)
Async XLA Ops:
  0.0 17.3 %copy-start.2 = (bf16[2,4,64,128]{3,2,1,0:T(8,128)(2,1)S(1)}, bf16[2,4,64,128]{3,2,1,0:T(8,128)(2,1)}, u32[]{:S(2)}) copy-start(bf16[2,4,64,128]{3,2,1,0:T(8,128)(2,1)} %param.3) | copy-start | bytes 393220
  0.0 21.5 %copy-start.3 = (f32[2048]{0:T(1024)S(1)}, f32[2048]{0:T(1024)}, u32[]{:S(2)}) copy-start(f32[2048]{0:T(1024)} %param.5) | copy-start | bytes 24580
  3.5 23.7 %all-to-all-start = ((bf16[32,3,3,2,2,128]{5,4,3,2,1,0:T(2,128)(2,1)}), bf16[32,3,3,2,2,128]{5,4,3,2,1,0:T(2,128)(2,1)S(1)}, u32[]{:S(2)}, u32[]{:S(2)}) async-start(bf16[32,3,3,2,2,128]{5,4,3,2,1,0:T(2,128)(2,1)} %bitcast.6), calls=%async_computation | async-start | bytes 589824 | tf_op jit(solution)/shard_map/all_to_all | solution.py:36
  17.3 9.2 %collective-permute-start = (bf16[1,2,64,128]{3,2,0,1:T(8,128)(2,1)S(1)}, bf16[1,2,64,128]{3,2,0,1:T(8,128)(2,1)S(1)}, u32[]{:S(2)}, u32[]{:S(2)}) collective-permute-start(bf16[1,2,64,128]{3,2,0,1:T(8,128)(2,1)S(1)} %slice_select_fusion), channel_id=1, source_target_pairs={{1,2},{3,4},{5,6},{7,8},{9,10},{11,12},{13,14},{15,16},{17,18},{19... | collective-permute-start | bytes 98312 | tf_op jit(solution)/shard_map/ppermute | solution.py:45
  27.5 8.3 %collective-permute-start.1 = (bf16[3,3,16,1024]{3,2,1,0:T(8,128)(2,1)S(1)}, bf16[3,3,16,1024]{3,2,1,0:T(8,128)(2,1)S(1)}, u32[]{:S(2)}, u32[]{:S(2)}) collective-permute-start(bf16[3,3,16,1024]{3,2,1,0:T(8,128)(2,1)S(1)} %reshape.49), channel_id=1, source_target_pairs={{0,1},{1,0},{2,3},{3,2},{4,5},{5,4},{6,7},{7,6},{8,9},{9,8},{10,11... | collective-permute-start | bytes 884744 | tf_op jit(solution)/shard_map/ppermute | solution.py:22
  35.9 15.8 %collective-permute-start.2 = (bf16[2,3,3,16,1024]{4,3,2,1,0:T(8,128)(2,1)S(1)}, bf16[2,3,3,16,1024]{4,3,2,1,0:T(8,128)(2,1)S(1)}, u32[]{:S(2)}, u32[]{:S(2)}) collective-permute-start(bf16[2,3,3,16,1024]{4,3,2,1,0:T(8,128)(2,1)S(1)} %pad_maximum_fusion.both), channel_id=1, source_target_pairs={{0,8},{1,57},{8,16},{9,1},{16,24},{17,9},{24,32},{25,17},{32,40},{... | collective-permute-start | bytes 1769480 | tf_op jit(solution)/shard_map/ppermute | solution.py:136
  39.8 11.8 %collective-permute-start.3 = (bf16[5,2,64,128]{3,2,0,1:T(8,128)(2,1)S(1)}, bf16[5,2,64,128]{3,2,0,1:T(8,128)(2,1)S(1)}, u32[]{:S(2)}, u32[]{:S(2)}) collective-permute-start(bf16[5,2,64,128]{3,2,0,1:T(8,128)(2,1)S(1)} %pad_maximum_fusion.2), channel_id=1, source_target_pairs={{0,64},{64,0},{1,65},{65,1},{2,66},{66,2},{3,67},{67,3},{4,68},{68... | collective-permute-start | bytes 491528 | tf_op jit(solution)/shard_map/ppermute | solution.py:137
  51.7 11.0 %collective-permute-start.4 = (bf16[2,3,3,16,1024]{4,3,2,1,0:T(8,128)(2,1)S(1)}, bf16[2,3,3,16,1024]{4,3,2,1,0:T(8,128)(2,1)}, u32[]{:S(2)}, u32[]{:S(2)}) collective-permute-start(bf16[2,3,3,16,1024]{4,3,2,1,0:T(8,128)(2,1)S(1)} %collective-permute-done.2.c1), channel_id=1, source_target_pairs={{0,8},{1,57},{8,16},{9,1},{16,24},{17,9},{24,32},{25,17},{32,40},{... | collective-permute-start | bytes 1769480 | tf_op jit(solution)/shard_map/ppermute | solution.py:139
  56.9 22.2 %all-to-all-start.1 = ((bf16[4,2,5,2,64,128]{5,4,3,2,1,0:T(8,128)(2,1)}), bf16[4,2,5,2,64,128]{5,4,3,2,1,0:T(8,128)(2,1)S(1)}, u32[]{:S(2)}, u32[]{:S(2)}) async-start(bf16[4,2,5,2,64,128]{5,4,3,2,1,0:T(8,128)(2,1)} %broadcast_in_dim.23), calls=%async_computation.1 | async-start | bytes 2621440 | tf_op jit(solution)/shard_map/all_to_all | solution.py:140
  62.8 16.3 %collective-permute-start.5 = (bf16[2,3,3,16,1024]{4,3,2,1,0:T(8,128)(2,1)}, bf16[2,3,3,16,1024]{4,3,2,1,0:T(8,128)(2,1)S(1)}, u32[]{:S(2)}, u32[]{:S(2)}) collective-permute-start(bf16[2,3,3,16,1024]{4,3,2,1,0:T(8,128)(2,1)} %collective-permute-done.4.c2), channel_id=1, source_target_pairs={{0,8},{1,57},{8,16},{9,1},{16,24},{17,9},{24,32},{25,17},{32,40},{... | collective-permute-start | bytes 1769480 | tf_op jit(solution)/shard_map/ppermute | solution.py:142
  67.4 5.9 %collective-permute-start.6 = (bf16[3,3,16,1024]{3,2,1,0:T(8,128)(2,1)S(1)}, bf16[3,3,16,1024]{3,2,1,0:T(8,128)(2,1)S(1)}, u32[]{:S(2)}, u32[]{:S(2)}) collective-permute-start(bf16[3,3,16,1024]{3,2,1,0:T(8,128)(2,1)S(1)} %slice_bitcast_fusion.3), channel_id=1, source_target_pairs={{0,1},{1,0},{2,3},{3,2},{4,5},{5,4},{6,7},{7,6},{8,9},{9,8},{10,11... | collective-permute-start | bytes 884744 | tf_op jit(solution)/shard_map/ppermute | solution.py:22
  71.3 3.5 %collective-permute-start.7 = (bf16[3,3,16,1024]{3,2,1,0:T(8,128)(2,1)S(1)}, bf16[3,3,16,1024]{3,2,1,0:T(8,128)(2,1)S(1)}, u32[]{:S(2)}, u32[]{:S(2)}) collective-permute-start(bf16[3,3,16,1024]{3,2,1,0:T(8,128)(2,1)S(1)} %slice_bitcast_fusion), channel_id=1, source_target_pairs={{0,1},{1,0},{2,3},{3,2},{4,5},{5,4},{6,7},{7,6},{8,9},{9,8},{10,11... | collective-permute-start | bytes 884744 | tf_op jit(solution)/shard_map/ppermute | solution.py:22
  74.8 0.7 copy-start
  79.1 10.9 %collective-permute-start.8 = (bf16[4,2,5,2,64,128]{5,4,3,2,1,0:T(8,128)(2,1)S(1)}, bf16[4,2,5,2,64,128]{5,4,3,2,1,0:T(8,128)(2,1)}, u32[]{:S(2)}, u32[]{:S(2)}) collective-permute-start(bf16[4,2,5,2,64,128]{5,4,3,2,1,0:T(8,128)(2,1)S(1)} %all-to-all-done.1.mine), channel_id=1, source_target_pairs={{0,1},{1,0},{2,3},{3,2},{4,5},{5,4},{6,7},{7,6},{8,9},{9,8},{10,11... | collective-permute-start | bytes 3932168 | tf_op jit(solution)/shard_map/ppermute | solution.py:22
  82.0 8.0 %copy-start.1 = (bf16[3,3,16,1024]{3,2,1,0:T(8,128)(2,1)S(1)}, bf16[3,3,16,1024]{3,2,1,0:T(8,128)(2,1)}, u32[]{:S(2)}) copy-start(bf16[3,3,16,1024]{3,2,1,0:T(8,128)(2,1)} %copy-done) | copy-start | bytes 884740
  82.1 7.9 %collective-permute-start.10 = (bf16[3,3,16,1024]{3,2,1,0:T(8,128)(2,1)S(1)}, bf16[3,3,16,1024]{3,2,1,0:T(8,128)(2,1)S(1)}, u32[]{:S(2)}, u32[]{:S(2)}) collective-permute-start(bf16[3,3,16,1024]{3,2,1,0:T(8,128)(2,1)S(1)} %get-tuple-element.23), channel_id=1, source_target_pairs={{0,8},{1,57},{8,16},{9,1},{16,24},{17,9},{24,32},{25,17},{32,40},{... | collective-permute-start | bytes 884744 | tf_op jit(solution)/shard_map/ppermute | solution.py:145
  85.3 4.7 %collective-permute-start.9 = (bf16[3,3,16,1024]{3,2,1,0:T(8,128)(2,1)S(1)}, bf16[3,3,16,1024]{3,2,1,0:T(8,128)(2,1)S(1)}, u32[]{:S(2)}, u32[]{:S(2)}) collective-permute-start(bf16[3,3,16,1024]{3,2,1,0:T(8,128)(2,1)S(1)} %get-tuple-element.24), channel_id=1, source_target_pairs={{0,1},{1,0},{2,3},{3,2},{4,5},{5,4},{6,7},{7,6},{8,9},{9,8},{10,11... | collective-permute-start | bytes 884744 | tf_op jit(solution)/shard_map/ppermute | solution.py:22

commit v4 on v3

v4 whole, which is shorter than its diff:
```python
import jax
import jax.numpy as jnp
from jax import lax
from jax.experimental import pallas as pl
from jax.experimental.pallas import tpu as pltpu
from jax.sharding import Mesh, PartitionSpec as P

AXES = ("x1", "x0", "zh", "y", "zl1", "zl0", "k")
SIZES = (2, 2, 2, 8, 2, 2, 2)
NY = 8
ROWS = 4


def ring(size, step):
    return [(i, (i + step) % size) for i in range(size)]


def two_way(size):
    return [(2 * i + k, 2 * ((i + 1 - 2 * k) % size) + k) for i in range(size) for k in range(2)]


def swap(array, axis):
    return lax.ppermute(array, axis, ring(2, 1))


def spread_kernel(kernel):
    k01 = (kernel[0].astype(jnp.float32) + kernel[1].astype(jnp.float32)).astype(kernel.dtype)
    both = jnp.stack([k01, kernel[2]])
    split = both.reshape(2, 3, 3, 64, 2, 2, 2, 2, 2)
    moved = jnp.transpose(split, (4, 7, 5, 1, 2, 8, 6, 0, 3))
    flat = moved.reshape(2, 2, 1, 2, 3, 3, 2, 2, 128)
    return jnp.broadcast_to(flat, (2, 2, 2, 2, 3, 3, 2, 2, 128))


def own_chunk(kernel):
    pieces = spread_kernel(kernel).reshape(16, 3, 3, 2, 2, 128)
    got = lax.all_to_all(pieces, ("x0", "zh", "zl1", "zl0"), 0, 0, tiled=True)
    got = got.reshape(4, 4, 3, 3, 2, 2, 128)
    return jnp.transpose(got, (3, 4, 1, 5, 2, 0, 6)).reshape(3, 16, 1536)


def own_rows(latent):
    rows = jnp.transpose(latent, (1, 0, 2, 3))
    tile = ("y", "zl1", "zl0", "k")
    up = [(i, i + 1) for i in range(63)]
    above = lax.ppermute(rows[3:], tile, up)
    below = lax.ppermute(rows[:1], tile, [(b, a) for a, b in up])
    return jnp.concatenate([above, rows, below], axis=0)


def conv_kernel(
    at_ref, rows, both, c1, s1, c2, s2, c3, s3, c4, s4, bias_ref, perm_ref, out_ref,
    w_ref, x_ref, even_ref, odd_ref, sems,
):
    y, core = at_ref[0], at_ref[1]
    copies = []

    def start(src, dst):
        copy = pltpu.make_async_copy(src, dst, sems.at[len(copies)])
        copy.start()
        copies.append(copy)

    for x in range(2):
        for h in range(2):
            for z in range(2):
                start(rows.at[x, h, z], x_ref.at[z, :, :, 2 * x + h])
    sign = 1 - 2 * core
    for half, owner in enumerate((core, 1 - core)):
        start(both.at[half], w_ref.at[:, y, owner])
        for n, (chunk, swapped) in enumerate(((c1, s1), (c2, s2), (c3, s3))):
            start(chunk.at[half], w_ref.at[:, lax.rem(y + 8 - (n + 1) * sign, 8), owner])
            start(swapped.at[half], w_ref.at[:, lax.rem(y + 8 + (n + 1) * sign, 8), 1 - owner])
        start((c4, s4)[half], w_ref.at[:, lax.rem(y + 4, 8), owner])
    for copy in copies:
        copy.wait()

    lane = lax.broadcasted_iota(jnp.int32, (256, 128), 1)
    count = 8 // ROWS

    def place(n):
        part = lax.rem(n, count)
        return part * ROWS // 4, lax.rem(part * ROWS, 4), n // count

    def product(n):
        z, row, frame = place(n)
        sides = []
        for q in range(ROWS):
            parts = []
            for b in range(3):
                for chan in range(4):
                    parts.append(x_ref[z, row + q + b, 0, chan])
                    parts.append(x_ref[z, row + q + b, frame, chan])
            sides.append(jnp.concatenate(parts, axis=0))
        taps = w_ref[...].reshape(768, 1536)
        return jnp.dot(taps, jnp.concatenate(sides, axis=1), preferred_element_type=jnp.float32)

    def finish(total_ref, n):
        z, row, frame = place(n)
        mixed = []
        for q in range(ROWS):
            lanes = pl.ds(q * 128, 128)
            before = jnp.where(lane == 0, 0.0, pltpu.roll(total_ref[:256, lanes], 1, 1))
            after = jnp.where(lane == 127, 0.0, pltpu.roll(total_ref[512:, lanes], 127, 1))
            conv = before + total_ref[256:512, lanes] + after + bias_ref[...]
            conv = conv.reshape(16, 2, 8, 128)
            mixed.append(jnp.concatenate([conv[:, 0].reshape(128, 128), conv[:, 1].reshape(128, 128)], axis=1))
        mixed = jnp.concatenate(mixed, axis=0).astype(jnp.bfloat16)
        mixed = jnp.dot(mixed, perm_ref[...], preferred_element_type=jnp.float32).astype(jnp.bfloat16)
        for q in range(ROWS):
            out_ref[4 * z + row + q, frame] = mixed[128 * q : 128 * q + 128]

    def step(i, carry):
        n = 2 * i
        first = product(n)
        finish(odd_ref, jnp.maximum(n - 1, 0))
        even_ref[...] = first
        second = product(n + 1)
        finish(even_ref, n)
        odd_ref[...] = second
        return carry

    lax.fori_loop(0, count, step, 0)
    finish(odd_ref, 2 * count - 1)


def convolve(at, rows, chunks, bias, perm):
    return pl.pallas_call(
        conv_kernel,
        out_shape=jax.ShapeDtypeStruct((8, 2, 128, 256), jnp.bfloat16),
        in_specs=[pl.BlockSpec(memory_space=pltpu.SMEM)]
        + [pl.BlockSpec(memory_space=pl.ANY)] * 10
        + [pl.BlockSpec(memory_space=pltpu.VMEM)] * 2,
        out_specs=pl.BlockSpec(memory_space=pltpu.VMEM),
        scratch_shapes=[
            pltpu.VMEM((3, NY, 2, 16, 1536), jnp.bfloat16),
            pltpu.VMEM((2, 6, 2, 4, 64, 128), jnp.bfloat16),
            pltpu.VMEM((768, 128 * ROWS), jnp.float32),
            pltpu.VMEM((768, 128 * ROWS), jnp.float32),
            pltpu.SemaphoreType.DMA((24,)),
        ],
        compiler_params=pltpu.CompilerParams(vmem_limit_bytes=36 * 1024 * 1024),
        cost_estimate=pl.CostEstimate(flops=4_900_000_000, bytes_accessed=6_000_000, transcendentals=0),
        name="conv",
    )(at, rows, *chunks, bias, perm)


def local(latent, kernel, bias):
    x1, x0, zh, y, core = (lax.axis_index(a) for a in ("x1", "x0", "zh", "y", "k"))
    zl0 = lax.axis_index("zl0")
    picked = bias.reshape(NY, 4, 2, 2, 2, 2, 2, 2)[:, :, :, x0, zl0, :, zh, :]
    column = jnp.transpose(picked, (0, 2, 4, 1, 3)).reshape(256, 1)
    column = jnp.broadcast_to(jnp.where(x1 == 0, column, 0.0), (256, 128))
    rows = own_rows(latent)
    own = own_chunk(kernel)
    own, rows, column = lax.optimization_barrier((own, rows, column))

    both = jnp.stack([own, swap(own, "k")])
    both, rows = lax.optimization_barrier((both, rows))
    c1 = lax.ppermute(both, ("y", "k"), two_way(NY))
    rows = lax.all_to_all(jnp.broadcast_to(rows, (8, *rows.shape)), ("x0", "zh", "zl0"), 0, 0, tiled=True)
    rows = rows.reshape(2, 2, 2, *rows.shape[1:])
    c2 = lax.ppermute(c1, ("y", "k"), two_way(NY))
    s1 = swap(c1, "k")
    c3 = lax.ppermute(c2, ("y", "k"), two_way(NY))
    s2 = swap(c2, "k")
    c3, s1, s2 = lax.optimization_barrier((c3, s1, s2))
    c4 = lax.ppermute(c3[0], ("y", "k"), two_way(NY))
    s3 = swap(c3, "k")
    s4 = swap(c4, "k")

    place = jnp.arange(256)
    perm = ((2 * (place % 128) + place // 128)[:, None] == place[None, :]).astype(jnp.bfloat16)
    at = jnp.stack([y, core]).astype(jnp.int32)
    out = convolve(at, rows, (both, c1, s1, c2, s2, c3, s3, c4, s4), column, perm)
    got = lax.all_to_all(out, ("zl0", "x1", "x0"), 0, 0, tiled=True).reshape(2, 2, 2, 2, NY, 2, 4, 2, 256)
    total = (got[:, 0].astype(jnp.float32) + got[:, 1].astype(jnp.float32)).astype(jnp.bfloat16)
    return jnp.transpose(total, (2, 3, 5, 4, 1, 0, 6, 7)).reshape(2, 1, 512, 256)


def solution(mesh):
    fine = Mesh(mesh.devices.reshape(SIZES), AXES)
    tile = ("y", "zl1", "zl0", "k")
    chan = ("x1", "x0", "zh")
    return jax.shard_map(
        local,
        mesh=fine,
        in_specs=(P(None, tile, chan, None), P(None, None, None, chan, tile), P()),
        out_specs=P(None, tile + chan, None, None),
        check_vma=False,
    )
```

time: 117 us -> 115 us (0.983); the launches traced: 116 us -> 113 us
  waiting for transfers between devices: 22.6 us -> 9 us
  starting transfers between devices: 58.6 us -> 64.3 us
  blocking collectives: 13.8 us -> 19.4 us
  Pallas kernels: 11 us -> 8.8 us
    ppermute x7, waiting for transfers between devices: 14.3 us -> 1.93 us  [the longest x5 1.92 us: swap(): return lax.ppermute(array, axis, ring(2, 1))]
    all_to_all x1, blocking collectives: 13.8 us -> 19.4 us  [local(): lax.all_to_all(out, ('zl0', 'x1', 'x0'), 0, 0, tiled=True)]
    ppermute x1, starting transfers between devices: 3.94 us -> 8.57 us  [local(): c1 = lax.ppermute(both, ('y', 'k'), two_way(NY))]
    all_to_all x2, waiting for transfers between devices: 4.22 us -> 0.01 us  [the longest x1 0.01 us: own_chunk(): got = lax.all_to_all(pieces, ('x0', 'zh', 'zl1', 'zl0'), 0, 0, tiled=True)]
    ppermute x1, waiting for transfers between devices: 0.01 us -> 3.65 us  [local(): c1 = lax.ppermute(both, ('y', 'k'), two_way(NY))]
    ppermute x7, starting transfers between devices: 25 us -> 22.3 us  [the longest x5 16 us: swap(): return lax.ppermute(array, axis, ring(2, 1))]
    ppermute x1, waiting for transfers between devices: 2.57 us -> 0.01 us  [local(): c4 = lax.ppermute(c3[0], ('y', 'k'), two_way(NY))]
    pallas_call x1, Pallas kernels: 11 us -> 8.8 us  [convolve(): pl.pallas_call(conv_kernel, out_shape=jax.ShapeDtypeStruct((8, 2, 128, 25...]
  transfers between devices with their start and end apart: 13 -> 13, of which waited for: 8 -> 5; matrix products, arithmetic and copies ran while one was open for 3% -> 2% of each run, Pallas kernels for 0% -> 0%
where the time goes in v4:
time: 115 us; the launch traced here: 113 us
  starting transfers between devices  64.3 us (56%)
  blocking collectives  19.4 us (17%)
  waiting for transfers between devices  9 us (8%)
  local copies, waits for them, and re-layouts  8.84 us (8%)
  Pallas kernels  8.8 us (8%)
  other arithmetic  2.21 us (2%)
    all_to_all x1, blocking collectives, local(): lax.all_to_all(out, ('zl0', 'x1', 'x0'), 0, 0, tiled=True)  19.4 us
    ppermute x5, starting transfers between devices, swap(): return lax.ppermute(array, axis, ring(2, 1))  16 us
    all_to_all x1, starting transfers between devices, own_chunk(): got = lax.all_to_all(pieces, ('x0', 'zh', 'zl1', 'zl0'), 0, 0, tiled=True)  11.9 us
    pallas_call x1, Pallas kernels, convolve(): pl.pallas_call(conv_kernel, out_shape=jax.ShapeDtypeStruct((8, 2, 128, 25...  8.8 us
    ppermute x1, starting transfers between devices, local(): c1 = lax.ppermute(both, ('y', 'k'), two_way(NY))  8.57 us
    all_to_all x1, starting transfers between devices, local(): lax.all_to_all(jnp.broadcast_to(rows, (8, *rows.shape)), ('x0', 'zh', 'zl...  5.6 us
    ppermute x1, starting transfers between devices, local(): c4 = lax.ppermute(c3[0], ('y', 'k'), two_way(NY))  5.32 us
    ppermute x1, starting transfers between devices, local(): c2 = lax.ppermute(c1, ('y', 'k'), two_way(NY))  5.31 us
  transfers between devices with their start and end apart: 13, of which 5 were waited for; matrix products, arithmetic and copies ran while one was open for 2% of the time, Pallas kernels for 0%

profile of v4, /device:TPU:1, one launch (start us, length us, event | category | flops | bytes accessed | tf_op | source)
XLA Modules:
  0.0 112.9 jit_solution(16179829619507097057)
XLA Ops:
  0.9 0.9 add_convert_fusion.1
  3.4 11.9 %all-to-all-start = ((bf16[16,3,3,2,2,128]{5,4,3,2,1,0:T(2,128)(2,1)}), bf16[16,3,3,2,2,128]{5,4,3,2,1,0:T(2,128)(2,1)S(1)}, u32[]{:S(2)}, u32[]{:S(2)}) async-start(bf16[16,3,3,2,2,128]{5,4,3,2,1,0:T(2,128)(2,1)} %bitcast.5), calls=%async_computation | async-start | bytes 294912 | tf_op jit(solution)/shard_map/all_to_all | solution.py:37
  15.3 2.9 %collective-permute-start.1 = (bf16[1,2,64,128]{3,2,0,1:T(8,128)(2,1)S(1)}, bf16[1,2,64,128]{3,2,0,1:T(8,128)(2,1)S(1)}, u32[]{:S(2)}, u32[]{:S(2)}) collective-permute-start(bf16[1,2,64,128]{3,2,0,1:T(8,128)(2,1)S(1)} %get-tuple-element.22), channel_id=1, source_target_pairs={{1,0},{2,1},{3,2},{4,3},{5,4},{6,5},{7,6},{8,7},{9,8},{10,9},{11,1... | collective-permute-start | bytes 98312 | tf_op jit(solution)/shard_map/ppermute | solution.py:47
  18.2 3.4 %collective-permute-start = (bf16[1,2,64,128]{3,2,0,1:T(8,128)(2,1)S(1)}, bf16[1,2,64,128]{3,2,0,1:T(8,128)(2,1)S(1)}, u32[]{:S(2)}, u32[]{:S(2)}) collective-permute-start(bf16[1,2,64,128]{3,2,0,1:T(8,128)(2,1)S(1)} %get-tuple-element.21), channel_id=1, source_target_pairs={{0,1},{1,2},{2,3},{3,4},{4,5},{5,6},{6,7},{7,8},{8,9},{9,10},{10,1... | collective-permute-start | bytes 98312 | tf_op jit(solution)/shard_map/ppermute | solution.py:46
  23.5 3.7 %collective-permute-start.2 = (bf16[3,16,1536]{2,1,0:T(8,128)(2,1)S(1)}, bf16[3,16,1536]{2,1,0:T(8,128)(2,1)S(1)}, u32[]{:S(2)}, u32[]{:S(2)}) collective-permute-start(bf16[3,16,1536]{2,1,0:T(8,128)(2,1)S(1)} %reshape.68), channel_id=1, source_target_pairs={{0,1},{1,0},{2,3},{3,2},{4,5},{5,4},{6,7},{7,6},{8,9},{9,8},{10,11... | collective-permute-start | bytes 442376 | tf_op jit(solution)/shard_map/ppermute | solution.py:23
  27.2 1.0 collective-permute-done.2
  28.3 1.6 %broadcast_in_dim.25 = bf16[8,6,2,64,128]{4,3,2,1,0:T(8,128)(2,1)} broadcast(bf16[6,2,64,128]{3,2,1,0:T(8,128)(2,1)S(1)} %copy.18), dimensions={1,2,3,4} | broadcast | bytes 1769472 | tf_op jit(solution)/shard_map/broadcast_in_dim | solution.py:160
  29.8 5.6 %all-to-all-start.1 = ((bf16[8,6,2,64,128]{4,3,2,1,0:T(8,128)(2,1)}), bf16[8,6,2,64,128]{4,3,2,1,0:T(8,128)(2,1)S(1)}, u32[]{:S(2)}, u32[]{:S(2)}) async-start(bf16[8,6,2,64,128]{4,3,2,1,0:T(8,128)(2,1)} %broadcast_in_dim.25), calls=%async_computation.1 | async-start | bytes 3145728 | tf_op jit(solution)/shard_map/all_to_all | solution.py:160
  35.4 8.6 %collective-permute-start.3 = (bf16[2,3,16,1536]{3,2,1,0:T(8,128)(2,1)S(1)}, bf16[2,3,16,1536]{3,2,1,0:T(8,128)(2,1)S(1)}, u32[]{:S(2)}, u32[]{:S(2)}) collective-permute-start(bf16[2,3,16,1536]{3,2,1,0:T(8,128)(2,1)S(1)} %pad_maximum_fusion.both), channel_id=1, source_target_pairs={{0,8},{1,57},{8,16},{9,1},{16,24},{17,9},{24,32},{25,17},{32,40},{... | collective-permute-start | bytes 884744 | tf_op jit(solution)/shard_map/ppermute | solution.py:159
  44.0 3.6 %collective-permute-done.3.c1 = bf16[2,3,16,1536]{3,2,1,0:T(8,128)(2,1)S(1)} collective-permute-done((bf16[2,3,16,1536]{3,2,1,0:T(8,128)(2,1)S(1)}, bf16[2,3,16,1536]{3,2,1,0:T(8,128)(2,1)S(1)}, u32[]{:S(2)}, u32[]{:S(2)}) %collective-permute-start.3) | collective-permute-done | bytes 294944 | tf_op jit(solution)/shard_map/ppermute | solution.py:159
  47.7 5.3 %collective-permute-start.4 = (bf16[2,3,16,1536]{3,2,1,0:T(8,128)(2,1)S(1)}, bf16[2,3,16,1536]{3,2,1,0:T(8,128)(2,1)S(1)}, u32[]{:S(2)}, u32[]{:S(2)}) collective-permute-start(bf16[2,3,16,1536]{3,2,1,0:T(8,128)(2,1)S(1)} %collective-permute-done.3.c1), channel_id=1, source_target_pairs={{0,8},{1,57},{8,16},{9,1},{16,24},{17,9},{24,32},{25,17},{32,40},{... | collective-permute-start | bytes 884744 | tf_op jit(solution)/shard_map/ppermute | solution.py:162
  53.0 1.9 %collective-permute-start.6 = (bf16[2,3,16,1536]{3,2,1,0:T(8,128)(2,1)S(1)}, bf16[2,3,16,1536]{3,2,1,0:T(8,128)(2,1)S(1)}, u32[]{:S(2)}, u32[]{:S(2)}) collective-permute-start(bf16[2,3,16,1536]{3,2,1,0:T(8,128)(2,1)S(1)} %collective-permute-done.3.c1), channel_id=1, source_target_pairs={{0,1},{1,0},{2,3},{3,2},{4,5},{5,4},{6,7},{7,6},{8,9},{9,8},{10,11... | collective-permute-start | bytes 884744 | tf_op jit(solution)/shard_map/ppermute | solution.py:23
  54.9 1.7 %collective-permute-done.4.c2 = bf16[2,3,16,1536]{3,2,1,0:T(8,128)(2,1)S(1)} collective-permute-done((bf16[2,3,16,1536]{3,2,1,0:T(8,128)(2,1)S(1)}, bf16[2,3,16,1536]{3,2,1,0:T(8,128)(2,1)S(1)}, u32[]{:S(2)}, u32[]{:S(2)}) %collective-permute-start.4) | collective-permute-done | bytes 294944 | tf_op jit(solution)/shard_map/ppermute | solution.py:162
  56.6 5.3 %collective-permute-start.5 = (bf16[2,3,16,1536]{3,2,1,0:T(8,128)(2,1)S(1)}, bf16[2,3,16,1536]{3,2,1,0:T(8,128)(2,1)S(1)}, u32[]{:S(2)}, u32[]{:S(2)}) collective-permute-start(bf16[2,3,16,1536]{3,2,1,0:T(8,128)(2,1)S(1)} %collective-permute-done.4.c2), channel_id=1, source_target_pairs={{0,8},{1,57},{8,16},{9,1},{16,24},{17,9},{24,32},{25,17},{32,40},{... | collective-permute-start | bytes 884744 | tf_op jit(solution)/shard_map/ppermute | solution.py:164
  61.9 1.9 %collective-permute-start.7 = (bf16[2,3,16,1536]{3,2,1,0:T(8,128)(2,1)S(1)}, bf16[2,3,16,1536]{3,2,1,0:T(8,128)(2,1)S(1)}, u32[]{:S(2)}, u32[]{:S(2)}) collective-permute-start(bf16[2,3,16,1536]{3,2,1,0:T(8,128)(2,1)S(1)} %collective-permute-done.4.c2), channel_id=1, source_target_pairs={{0,1},{1,0},{2,3},{3,2},{4,5},{5,4},{6,7},{7,6},{8,9},{9,8},{10,11... | collective-permute-start | bytes 884744 | tf_op jit(solution)/shard_map/ppermute | solution.py:23
  63.9 1.7 %collective-permute-done.5.c3 = bf16[2,3,16,1536]{3,2,1,0:T(8,128)(2,1)S(1)} collective-permute-done((bf16[2,3,16,1536]{3,2,1,0:T(8,128)(2,1)S(1)}, bf16[2,3,16,1536]{3,2,1,0:T(8,128)(2,1)S(1)}, u32[]{:S(2)}, u32[]{:S(2)}) %collective-permute-start.5) | collective-permute-done | bytes 294944 | tf_op jit(solution)/shard_map/ppermute | solution.py:164
  66.3 5.3 %collective-permute-start.9 = (bf16[3,16,1536]{2,1,0:T(8,128)(2,1)S(1)}, bf16[3,16,1536]{2,1,0:T(8,128)(2,1)S(1)}, u32[]{:S(2)}, u32[]{:S(2)}) collective-permute-start(bf16[3,16,1536]{2,1,0:T(8,128)(2,1)S(1)} %slice_bitcast_fusion), channel_id=1, source_target_pairs={{0,8},{1,57},{8,16},{9,1},{16,24},{17,9},{24,32},{25,17},{32,40},{... | collective-permute-start | bytes 442376 | tf_op jit(solution)/shard_map/ppermute | solution.py:167
  71.6 2.2 %collective-permute-start.8 = (bf16[2,3,16,1536]{3,2,1,0:T(8,128)(2,1)S(1)}, bf16[2,3,16,1536]{3,2,1,0:T(8,128)(2,1)}, u32[]{:S(2)}, u32[]{:S(2)}) collective-permute-start(bf16[2,3,16,1536]{3,2,1,0:T(8,128)(2,1)S(1)} %collective-permute-done.5.c3), channel_id=1, source_target_pairs={{0,1},{1,0},{2,3},{3,2},{4,5},{5,4},{6,7},{7,6},{8,9},{9,8},{10,11... | collective-permute-start | bytes 884744 | tf_op jit(solution)/shard_map/ppermute | solution.py:23
  73.9 6.3 %collective-permute-start.10 = (bf16[3,16,1536]{2,1,0:T(8,128)(2,1)S(1)}, bf16[3,16,1536]{2,1,0:T(8,128)(2,1)}, u32[]{:S(2)}, u32[]{:S(2)}) collective-permute-start(bf16[3,16,1536]{2,1,0:T(8,128)(2,1)S(1)} %collective-permute-done.9.c4), channel_id=1, source_target_pairs={{0,1},{1,0},{2,3},{3,2},{4,5},{5,4},{6,7},{7,6},{8,9},{9,8},{10,11... | collective-permute-start | bytes 442376 | tf_op jit(solution)/shard_map/ppermute | solution.py:23
  80.3 0.9 collective-permute-done.10.s4
  81.3 1.0 copy-done.1
  82.2 8.8 %conv.1 = bf16[8,2,128,256]{3,2,1,0:T(8,128)(2,1)S(1)} custom-call(s32[2]{0:T(128)S(1)} %pad_add_fusion.at_ref, bf16[2,2,2,6,2,64,128]{6,5,4,3,2,1,0:T(8,128)(2,1)S(1)} %bitcast.25, bf16[2,3,16,1536]{3,2,1,0:T(8,128)(2,1)S(1)} %pad_maximum_fusion.both, bf16[2,3,16,1536]{3,2,1,0:T(8,128)(2,1)S(1)} %collective-permute-done.3.c1, ...), custom_call_target="tpu_custom_call" | custom-call | flops 4899999744 | bytes 6000000 | tf_op jit(solution)/shard_map/conv/pallas_call | solution.py:127
  91.0 19.4 %all_to_all.15 = bf16[8,2,128,256]{3,2,1,0:T(8,128)(2,1)S(1)} all-to-all(bf16[8,2,128,256]{3,2,1,0:T(8,128)(2,1)S(1)} %conv.1), channel_id=1, replica_groups=mesh['x1'=2,'x0'=2,'zh'=2,'y'=8,'zl1'=2,'zl0'=2,'k'=2] {'zl0','x1','x0'}, dimensions={0} | all-to-all | bytes 2097152 | tf_op jit(solution)/shard_map/all_to_all | solution.py:175
  111.9 1.0 reshape.72
  (40 shorter events, 6.6 us)
Async XLA Ops:
  0.0 15.3 %copy-start.2 = (bf16[2,4,64,128]{3,2,1,0:T(8,128)(2,1)S(1)}, bf16[2,4,64,128]{3,2,1,0:T(8,128)(2,1)}, u32[]{:S(2)}) copy-start(bf16[2,4,64,128]{3,2,1,0:T(8,128)(2,1)} %param.3) | copy-start | bytes 393220
  0.0 21.7 %copy-start.3 = (f32[2048]{0:T(1024)S(1)}, f32[2048]{0:T(1024)}, u32[]{:S(2)}) copy-start(f32[2048]{0:T(1024)} %param.5) | copy-start | bytes 24580
  3.4 19.9 %all-to-all-start = ((bf16[16,3,3,2,2,128]{5,4,3,2,1,0:T(2,128)(2,1)}), bf16[16,3,3,2,2,128]{5,4,3,2,1,0:T(2,128)(2,1)S(1)}, u32[]{:S(2)}, u32[]{:S(2)}) async-start(bf16[16,3,3,2,2,128]{5,4,3,2,1,0:T(2,128)(2,1)} %bitcast.5), calls=%async_computation | async-start | bytes 294912 | tf_op jit(solution)/shard_map/all_to_all | solution.py:37
  15.3 7.9 %collective-permute-start.1 = (bf16[1,2,64,128]{3,2,0,1:T(8,128)(2,1)S(1)}, bf16[1,2,64,128]{3,2,0,1:T(8,128)(2,1)S(1)}, u32[]{:S(2)}, u32[]{:S(2)}) collective-permute-start(bf16[1,2,64,128]{3,2,0,1:T(8,128)(2,1)S(1)} %get-tuple-element.22), channel_id=1, source_target_pairs={{1,0},{2,1},{3,2},{4,3},{5,4},{6,5},{7,6},{8,7},{9,8},{10,9},{11,1... | collective-permute-start | bytes 98312 | tf_op jit(solution)/shard_map/ppermute | solution.py:47
  18.2 5.0 %collective-permute-start = (bf16[1,2,64,128]{3,2,0,1:T(8,128)(2,1)S(1)}, bf16[1,2,64,128]{3,2,0,1:T(8,128)(2,1)S(1)}, u32[]{:S(2)}, u32[]{:S(2)}) collective-permute-start(bf16[1,2,64,128]{3,2,0,1:T(8,128)(2,1)S(1)} %get-tuple-element.21), channel_id=1, source_target_pairs={{0,1},{1,2},{2,3},{3,4},{4,5},{5,6},{6,7},{7,8},{8,9},{9,10},{10,1... | collective-permute-start | bytes 98312 | tf_op jit(solution)/shard_map/ppermute | solution.py:46
  23.5 4.7 %collective-permute-start.2 = (bf16[3,16,1536]{2,1,0:T(8,128)(2,1)S(1)}, bf16[3,16,1536]{2,1,0:T(8,128)(2,1)S(1)}, u32[]{:S(2)}, u32[]{:S(2)}) collective-permute-start(bf16[3,16,1536]{2,1,0:T(8,128)(2,1)S(1)} %reshape.68), channel_id=1, source_target_pairs={{0,1},{1,0},{2,3},{3,2},{4,5},{5,4},{6,7},{7,6},{8,9},{9,8},{10,11... | collective-permute-start | bytes 442376 | tf_op jit(solution)/shard_map/ppermute | solution.py:23
  29.8 51.4 %all-to-all-start.1 = ((bf16[8,6,2,64,128]{4,3,2,1,0:T(8,128)(2,1)}), bf16[8,6,2,64,128]{4,3,2,1,0:T(8,128)(2,1)S(1)}, u32[]{:S(2)}, u32[]{:S(2)}) async-start(bf16[8,6,2,64,128]{4,3,2,1,0:T(8,128)(2,1)} %broadcast_in_dim.25), calls=%async_computation.1 | async-start | bytes 3145728 | tf_op jit(solution)/shard_map/all_to_all | solution.py:160
  35.4 12.2 %collective-permute-start.3 = (bf16[2,3,16,1536]{3,2,1,0:T(8,128)(2,1)S(1)}, bf16[2,3,16,1536]{3,2,1,0:T(8,128)(2,1)S(1)}, u32[]{:S(2)}, u32[]{:S(2)}) collective-permute-start(bf16[2,3,16,1536]{3,2,1,0:T(8,128)(2,1)S(1)} %pad_maximum_fusion.both), channel_id=1, source_target_pairs={{0,8},{1,57},{8,16},{9,1},{16,24},{17,9},{24,32},{25,17},{32,40},{... | collective-permute-start | bytes 884744 | tf_op jit(solution)/shard_map/ppermute | solution.py:159
  47.7 9.0 %collective-permute-start.4 = (bf16[2,3,16,1536]{3,2,1,0:T(8,128)(2,1)S(1)}, bf16[2,3,16,1536]{3,2,1,0:T(8,128)(2,1)S(1)}, u32[]{:S(2)}, u32[]{:S(2)}) collective-permute-start(bf16[2,3,16,1536]{3,2,1,0:T(8,128)(2,1)S(1)} %collective-permute-done.3.c1), channel_id=1, source_target_pairs={{0,8},{1,57},{8,16},{9,1},{16,24},{17,9},{24,32},{25,17},{32,40},{... | collective-permute-start | bytes 884744 | tf_op jit(solution)/shard_map/ppermute | solution.py:162
  53.0 10.9 %collective-permute-start.6 = (bf16[2,3,16,1536]{3,2,1,0:T(8,128)(2,1)S(1)}, bf16[2,3,16,1536]{3,2,1,0:T(8,128)(2,1)S(1)}, u32[]{:S(2)}, u32[]{:S(2)}) collective-permute-start(bf16[2,3,16,1536]{3,2,1,0:T(8,128)(2,1)S(1)} %collective-permute-done.3.c1), channel_id=1, source_target_pairs={{0,1},{1,0},{2,3},{3,2},{4,5},{5,4},{6,7},{7,6},{8,9},{9,8},{10,11... | collective-permute-start | bytes 884744 | tf_op jit(solution)/shard_map/ppermute | solution.py:23
  56.6 9.0 %collective-permute-start.5 = (bf16[2,3,16,1536]{3,2,1,0:T(8,128)(2,1)S(1)}, bf16[2,3,16,1536]{3,2,1,0:T(8,128)(2,1)S(1)}, u32[]{:S(2)}, u32[]{:S(2)}) collective-permute-start(bf16[2,3,16,1536]{3,2,1,0:T(8,128)(2,1)S(1)} %collective-permute-done.4.c2), channel_id=1, source_target_pairs={{0,8},{1,57},{8,16},{9,1},{16,24},{17,9},{24,32},{25,17},{32,40},{... | collective-permute-start | bytes 884744 | tf_op jit(solution)/shard_map/ppermute | solution.py:164
  61.9 3.6 %collective-permute-start.7 = (bf16[2,3,16,1536]{3,2,1,0:T(8,128)(2,1)S(1)}, bf16[2,3,16,1536]{3,2,1,0:T(8,128)(2,1)S(1)}, u32[]{:S(2)}, u32[]{:S(2)}) collective-permute-start(bf16[2,3,16,1536]{3,2,1,0:T(8,128)(2,1)S(1)} %collective-permute-done.4.c2), channel_id=1, source_target_pairs={{0,1},{1,0},{2,3},{3,2},{4,5},{5,4},{6,7},{7,6},{8,9},{9,8},{10,11... | collective-permute-start | bytes 884744 | tf_op jit(solution)/shard_map/ppermute | solution.py:23
  65.6 0.7 copy-start
  66.3 7.5 %collective-permute-start.9 = (bf16[3,16,1536]{2,1,0:T(8,128)(2,1)S(1)}, bf16[3,16,1536]{2,1,0:T(8,128)(2,1)S(1)}, u32[]{:S(2)}, u32[]{:S(2)}) collective-permute-start(bf16[3,16,1536]{2,1,0:T(8,128)(2,1)S(1)} %slice_bitcast_fusion), channel_id=1, source_target_pairs={{0,8},{1,57},{8,16},{9,1},{16,24},{17,9},{24,32},{25,17},{32,40},{... | collective-permute-start | bytes 442376 | tf_op jit(solution)/shard_map/ppermute | solution.py:167
  71.6 9.6 %collective-permute-start.8 = (bf16[2,3,16,1536]{3,2,1,0:T(8,128)(2,1)S(1)}, bf16[2,3,16,1536]{3,2,1,0:T(8,128)(2,1)}, u32[]{:S(2)}, u32[]{:S(2)}) collective-permute-start(bf16[2,3,16,1536]{3,2,1,0:T(8,128)(2,1)S(1)} %collective-permute-done.5.c3), channel_id=1, source_target_pairs={{0,1},{1,0},{2,3},{3,2},{4,5},{5,4},{6,7},{7,6},{8,9},{9,8},{10,11... | collective-permute-start | bytes 884744 | tf_op jit(solution)/shard_map/ppermute | solution.py:23
  73.9 7.4 %collective-permute-start.10 = (bf16[3,16,1536]{2,1,0:T(8,128)(2,1)S(1)}, bf16[3,16,1536]{2,1,0:T(8,128)(2,1)}, u32[]{:S(2)}, u32[]{:S(2)}) collective-permute-start(bf16[3,16,1536]{2,1,0:T(8,128)(2,1)S(1)} %collective-permute-done.9.c4), channel_id=1, source_target_pairs={{0,1},{1,0},{2,3},{3,2},{4,5},{5,4},{6,7},{7,6},{8,9},{9,8},{10,11... | collective-permute-start | bytes 442376 | tf_op jit(solution)/shard_map/ppermute | solution.py:23
  81.3 1.0 copy-start.1

commit v5 on v4

--- a/solution.py
+++ b/solution.py
@@ -13,10 +13,6 @@
 
 def ring(size, step):
     return [(i, (i + step) % size) for i in range(size)]
-
-
-def two_way(size):
-    return [(2 * i + k, 2 * ((i + 1 - 2 * k) % size) + k) for i in range(size) for k in range(2)]
 
 
 def swap(array, axis):
@@ -49,10 +45,10 @@
 
 
 def conv_kernel(
-    at_ref, rows, both, c1, s1, c2, s2, c3, s3, c4, s4, bias_ref, perm_ref, out_ref,
+    at_ref, here, over_x, over_z, over_both, mine, other, bias_ref, perm_ref, out_ref,
     w_ref, x_ref, even_ref, odd_ref, sems,
 ):
-    y, core = at_ref[0], at_ref[1]
+    x0, zh, zl0, core = (at_ref[n] for n in range(4))
     copies = []
 
     def start(src, dst):
@@ -60,17 +56,12 @@
         copy.start()
         copies.append(copy)
 
-    for x in range(2):
-        for h in range(2):
-            for z in range(2):
-                start(rows.at[x, h, z], x_ref.at[z, :, :, 2 * x + h])
-    sign = 1 - 2 * core
-    for half, owner in enumerate((core, 1 - core)):
-        start(both.at[half], w_ref.at[:, y, owner])
-        for n, (chunk, swapped) in enumerate(((c1, s1), (c2, s2), (c3, s3))):
-            start(chunk.at[half], w_ref.at[:, lax.rem(y + 8 - (n + 1) * sign, 8), owner])
-            start(swapped.at[half], w_ref.at[:, lax.rem(y + 8 + (n + 1) * sign, 8), 1 - owner])
-        start((c4, s4)[half], w_ref.at[:, lax.rem(y + 4, 8), owner])
+    for rows, x, z in ((here, x0, zl0), (over_x, 1 - x0, zl0), (over_z, x0, 1 - zl0), (over_both, 1 - x0, 1 - zl0)):
+        for n, h in enumerate((zh, 1 - zh)):
+            start(rows.at[n], x_ref.at[z, :, :, 2 * x + h])
+    for chunks, owner in ((mine, core), (other, 1 - core)):
+        for y in range(NY):
+            start(chunks.at[y], w_ref.at[:, y, owner])
     for copy in copies:
         copy.wait()
 
@@ -128,7 +119,7 @@
         conv_kernel,
         out_shape=jax.ShapeDtypeStruct((8, 2, 128, 256), jnp.bfloat16),
         in_specs=[pl.BlockSpec(memory_space=pltpu.SMEM)]
-        + [pl.BlockSpec(memory_space=pl.ANY)] * 10
+        + [pl.BlockSpec(memory_space=pl.ANY)] * 6
         + [pl.BlockSpec(memory_space=pltpu.VMEM)] * 2,
         out_specs=pl.BlockSpec(memory_space=pltpu.VMEM),
         scratch_shapes=[
@@ -141,12 +132,11 @@
         compiler_params=pltpu.CompilerParams(vmem_limit_bytes=36 * 1024 * 1024),
         cost_estimate=pl.CostEstimate(flops=4_900_000_000, bytes_accessed=6_000_000, transcendentals=0),
         name="conv",
-    )(at, rows, *chunks, bias, perm)
+    )(at, *rows, *chunks, bias, perm)
 
 
 def local(latent, kernel, bias):
-    x1, x0, zh, y, core = (lax.axis_index(a) for a in ("x1", "x0", "zh", "y", "k"))
-    zl0 = lax.axis_index("zl0")
+    x1, x0, zh, zl0, core = (lax.axis_index(a) for a in ("x1", "x0", "zh", "zl0", "k"))
     picked = bias.reshape(NY, 4, 2, 2, 2, 2, 2, 2)[:, :, :, x0, zl0, :, zh, :]
     column = jnp.transpose(picked, (0, 2, 4, 1, 3)).reshape(256, 1)
     column = jnp.broadcast_to(jnp.where(x1 == 0, column, 0.0), (256, 128))
@@ -154,24 +144,17 @@
     own = own_chunk(kernel)
     own, rows, column = lax.optimization_barrier((own, rows, column))
 
-    both = jnp.stack([own, swap(own, "k")])
-    both, rows = lax.optimization_barrier((both, rows))
-    c1 = lax.ppermute(both, ("y", "k"), two_way(NY))
-    rows = lax.all_to_all(jnp.broadcast_to(rows, (8, *rows.shape)), ("x0", "zh", "zl0"), 0, 0, tiled=True)
-    rows = rows.reshape(2, 2, 2, *rows.shape[1:])
-    c2 = lax.ppermute(c1, ("y", "k"), two_way(NY))
-    s1 = swap(c1, "k")
-    c3 = lax.ppermute(c2, ("y", "k"), two_way(NY))
-    s2 = swap(c2, "k")
-    c3, s1, s2 = lax.optimization_barrier((c3, s1, s2))
-    c4 = lax.ppermute(c3[0], ("y", "k"), two_way(NY))
-    s3 = swap(c3, "k")
-    s4 = swap(c4, "k")
+    mine = lax.all_to_all(jnp.broadcast_to(own, (NY, *own.shape)), "y", 0, 0, tiled=True)
+    rows = jnp.stack([rows, swap(rows, "zh")])
+    over_x, over_z = swap(rows, "x0"), swap(rows, "zl0")
+    over_both = lax.ppermute(rows, ("x0", "zl0"), [(i, 3 - i) for i in range(4)])
+    mine, rows, over_x, over_z, over_both = lax.optimization_barrier((mine, rows, over_x, over_z, over_both))
+    other = swap(mine, "k")
 
     place = jnp.arange(256)
     perm = ((2 * (place % 128) + place // 128)[:, None] == place[None, :]).astype(jnp.bfloat16)
-    at = jnp.stack([y, core]).astype(jnp.int32)
-    out = convolve(at, rows, (both, c1, s1, c2, s2, c3, s3, c4, s4), column, perm)
+    at = jnp.stack([x0, zh, zl0, core]).astype(jnp.int32)
+    out = convolve(at, (rows, over_x, over_z, over_both), (mine, other), column, perm)
     got = lax.all_to_all(out, ("zl0", "x1", "x0"), 0, 0, tiled=True).reshape(2, 2, 2, 2, NY, 2, 4, 2, 256)
     total = (got[:, 0].astype(jnp.float32) + got[:, 1].astype(jnp.float32)).astype(jnp.bfloat16)
     return jnp.transpose(total, (2, 3, 5, 4, 1, 0, 6, 7)).reshape(2, 1, 512, 256)

time: 115 us -> 109 us (0.948)
  starting transfers between devices: 64.3 us -> 45.7 us
  waiting for transfers between devices: 9 us -> 22.6 us
  local copies, waits for them, and re-layouts: 8.84 us -> 10.2 us
    ppermute x4 -> x1, starting transfers between devices: 24.5 us -> 5.74 us  [local(): lax.ppermute(rows, ('x0', 'zl0'), [(i, 3 - i) for i in range(4)])]
    ppermute x5 -> x4, waiting for transfers between devices: 1.92 us -> 17.1 us  [swap(): return lax.ppermute(array, axis, ring(2, 1))]
    ppermute x4 -> x1, waiting for transfers between devices: 7.07 us -> 3.7 us  [local(): lax.ppermute(rows, ('x0', 'zl0'), [(i, 3 - i) for i in range(4)])]
    unnamed x8 -> x13, local copies, waits for them, and re-layouts: 1.68 us -> 3.5 us
    ppermute x1, waiting for transfers between devices: 0.01 us -> 1.75 us  [own_rows(): below = lax.ppermute(rows[:1], tile, [(b, a) for a, b in up])]
    all_to_all x1, starting transfers between devices: 5.6 us -> 7.01 us  [local(): lax.all_to_all(jnp.broadcast_to(own, (NY, *own.shape)), 'y', 0, 0, tiled=...]
    ppermute x5 -> x4, starting transfers between devices: 16 us -> 14.7 us  [swap(): return lax.ppermute(array, axis, ring(2, 1))]
  transfers between devices with their start and end apart: 13 -> 9, of which waited for: 5 -> 5; matrix products, arithmetic and copies ran while one was open for 2% -> 2% of each run, Pallas kernels for 0% -> 0%
where the time goes in v5:
time: 109 us; the launch traced here: 108 us
  starting transfers between devices  45.7 us (42%)
  waiting for transfers between devices  22.6 us (21%)
  blocking collectives  18.9 us (17%)
  local copies, waits for them, and re-layouts  10.2 us (9%)
  Pallas kernels  7.99 us (7%)
  other arithmetic  2.23 us (2%)
    all_to_all x1, blocking collectives, local(): lax.all_to_all(out, ('zl0', 'x1', 'x0'), 0, 0, tiled=True)  18.9 us
    ppermute x4, waiting for transfers between devices, swap(): return lax.ppermute(array, axis, ring(2, 1))  17.1 us
    ppermute x4, starting transfers between devices, swap(): return lax.ppermute(array, axis, ring(2, 1))  14.7 us
    all_to_all x1, starting transfers between devices, own_chunk(): got = lax.all_to_all(pieces, ('x0', 'zh', 'zl1', 'zl0'), 0, 0, tiled=True)  11.9 us
    pallas_call x1, Pallas kernels, convolve(): pl.pallas_call(conv_kernel, out_shape=jax.ShapeDtypeStruct((8, 2, 128, 25...  7.99 us
    all_to_all x1, starting transfers between devices, local(): lax.all_to_all(jnp.broadcast_to(own, (NY, *own.shape)), 'y', 0, 0, tiled=...  7.01 us
    ppermute x1, starting transfers between devices, local(): lax.ppermute(rows, ('x0', 'zl0'), [(i, 3 - i) for i in range(4)])  5.74 us
    ppermute x1, starting transfers between devices, own_rows(): above = lax.ppermute(rows[3:], tile, up)  4.39 us
  transfers between devices with their start and end apart: 9, of which 5 were waited for; matrix products, arithmetic and copies ran while one was open for 2% of the time, Pallas kernels for 0%

profile of v5, /device:TPU:1, one launch (start us, length us, event | category | flops | bytes accessed | tf_op | source)
XLA Modules:
  0.0 107.8 jit_solution(16735959360066735469)
XLA Ops:
  0.0 0.9 slice.23
  0.9 1.0 add_convert_fusion.1
  3.4 11.9 %all-to-all-start = ((bf16[16,3,3,2,2,128]{5,4,3,2,1,0:T(2,128)(2,1)}), bf16[16,3,3,2,2,128]{5,4,3,2,1,0:T(2,128)(2,1)S(1)}, u32[]{:S(2)}, u32[]{:S(2)}) async-start(bf16[16,3,3,2,2,128]{5,4,3,2,1,0:T(2,128)(2,1)} %bitcast.7), calls=%async_computation | async-start | bytes 294912 | tf_op jit(solution)/shard_map/all_to_all | solution.py:33
  15.4 4.4 %collective-permute-start = (bf16[1,2,64,128]{3,2,1,0:T(8,128)(2,1)S(1)}, bf16[1,2,64,128]{3,2,1,0:T(8,128)(2,1)S(1)}, u32[]{:S(2)}, u32[]{:S(2)}) collective-permute-start(bf16[1,2,64,128]{3,2,1,0:T(8,128)(2,1)S(1)} %get-tuple-element.21), channel_id=1, source_target_pairs={{0,1},{1,2},{2,3},{3,4},{4,5},{5,6},{6,7},{7,8},{8,9},{9,10},{10,1... | collective-permute-start | bytes 98312 | tf_op jit(solution)/shard_map/ppermute | solution.py:42
  19.8 1.9 %collective-permute-start.1 = (bf16[1,2,64,128]{3,2,1,0:T(8,128)(2,1)S(1)}, bf16[1,2,64,128]{3,2,1,0:T(8,128)(2,1)S(1)}, u32[]{:S(2)}, u32[]{:S(2)}) collective-permute-start(bf16[1,2,64,128]{3,2,1,0:T(8,128)(2,1)S(1)} %get-tuple-element.22), channel_id=1, source_target_pairs={{1,0},{2,1},{3,2},{4,3},{5,4},{6,5},{7,6},{8,7},{9,8},{10,9},{11,1... | collective-permute-start | bytes 98312 | tf_op jit(solution)/shard_map/ppermute | solution.py:43
  21.7 0.8 reshape.66
  23.2 1.8 %collective-permute-done.1 = bf16[1,2,64,128]{3,2,1,0:T(8,128)(2,1)S(1)} collective-permute-done((bf16[1,2,64,128]{3,2,1,0:T(8,128)(2,1)S(1)}, bf16[1,2,64,128]{3,2,1,0:T(8,128)(2,1)S(1)}, u32[]{:S(2)}, u32[]{:S(2)}) %collective-permute-start.1) | collective-permute-done | bytes 32800 | tf_op jit(solution)/shard_map/ppermute | solution.py:43
  25.3 1.2 %broadcast_in_dim.25 = bf16[8,3,16,1536]{3,2,1,0:T(8,128)(2,1)} broadcast(bf16[3,16,1536]{2,1,0:T(8,128)(2,1)S(1)} %reshape.65), dimensions={1,2,3} | broadcast | bytes 1327104 | tf_op jit(solution)/shard_map/broadcast_in_dim | solution.py:147
  26.5 7.0 %all-to-all-start.1 = ((bf16[8,3,16,1536]{3,2,1,0:T(8,128)(2,1)}), bf16[8,3,16,1536]{3,2,1,0:T(8,128)(2,1)S(1)}, u32[]{:S(2)}, u32[]{:S(2)}) async-start(bf16[8,3,16,1536]{3,2,1,0:T(8,128)(2,1)} %broadcast_in_dim.25), calls=%async_computation.1 | async-start | bytes 2359296 | tf_op jit(solution)/shard_map/all_to_all | solution.py:147
  33.5 6.2 %collective-permute-start.2 = (bf16[6,2,64,128]{3,2,1,0:T(8,128)(2,1)S(1)}, bf16[6,2,64,128]{3,2,1,0:T(8,128)(2,1)S(1)}, u32[]{:S(2)}, u32[]{:S(2)}) collective-permute-start(bf16[6,2,64,128]{3,2,1,0:T(8,128)(2,1)S(1)} %pad_maximum_fusion.1), channel_id=1, source_target_pairs={{0,64},{64,0},{1,65},{65,1},{2,66},{66,2},{3,67},{67,3},{4,68},{68... | collective-permute-start | bytes 589832 | tf_op jit(solution)/shard_map/ppermute | solution.py:19
  39.7 6.4 %collective-permute-done.2 = bf16[6,2,64,128]{3,2,1,0:T(8,128)(2,1)S(1)} collective-permute-done((bf16[6,2,64,128]{3,2,1,0:T(8,128)(2,1)S(1)}, bf16[6,2,64,128]{3,2,1,0:T(8,128)(2,1)S(1)}, u32[]{:S(2)}, u32[]{:S(2)}) %collective-permute-start.2) | collective-permute-done | bytes 196640 | tf_op jit(solution)/shard_map/ppermute | solution.py:19
  46.1 5.7 %collective-permute-start.5 = (bf16[2,6,2,64,128]{4,3,2,1,0:T(8,128)(2,1)S(1)}, bf16[2,6,2,64,128]{4,3,2,1,0:T(8,128)(2,1)S(1)}, u32[]{:S(2)}, u32[]{:S(2)}) collective-permute-start(bf16[2,6,2,64,128]{4,3,2,1,0:T(8,128)(2,1)S(1)} %pad_maximum_fusion.here), channel_id=1, source_target_pairs={{0,130},{2,128},{128,2},{130,0},{1,131},{3,129},{129,3},{131,1},{4... | collective-permute-start | bytes 1179656 | tf_op jit(solution)/shard_map/ppermute | solution.py:150
  51.9 2.2 %collective-permute-start.4 = (bf16[2,6,2,64,128]{4,3,2,1,0:T(8,128)(2,1)S(1)}, bf16[2,6,2,64,128]{4,3,2,1,0:T(8,128)(2,1)S(1)}, u32[]{:S(2)}, u32[]{:S(2)}) collective-permute-start(bf16[2,6,2,64,128]{4,3,2,1,0:T(8,128)(2,1)S(1)} %pad_maximum_fusion.here), channel_id=1, source_target_pairs={{0,2},{2,0},{1,3},{3,1},{4,6},{6,4},{5,7},{7,5},{8,10},{10,8},{9,1... | collective-permute-start | bytes 1179656 | tf_op jit(solution)/shard_map/ppermute | solution.py:19
  54.1 1.9 %collective-permute-start.3 = (bf16[2,6,2,64,128]{4,3,2,1,0:T(8,128)(2,1)S(1)}, bf16[2,6,2,64,128]{4,3,2,1,0:T(8,128)(2,1)S(1)}, u32[]{:S(2)}, u32[]{:S(2)}) collective-permute-start(bf16[2,6,2,64,128]{4,3,2,1,0:T(8,128)(2,1)S(1)} %pad_maximum_fusion.here), channel_id=1, source_target_pairs={{0,128},{128,0},{1,129},{129,1},{2,130},{130,2},{3,131},{131,3},{4... | collective-permute-start | bytes 1179656 | tf_op jit(solution)/shard_map/ppermute | solution.py:19
  56.0 3.7 %collective-permute-done.5.over_both = bf16[2,6,2,64,128]{4,3,2,1,0:T(8,128)(2,1)S(1)} collective-permute-done((bf16[2,6,2,64,128]{4,3,2,1,0:T(8,128)(2,1)S(1)}, bf16[2,6,2,64,128]{4,3,2,1,0:T(8,128)(2,1)S(1)}, u32[]{:S(2)}, u32[]{:S(2)}) %collective-permute-start.5) | collective-permute-done | bytes 393248 | tf_op jit(solution)/shard_map/ppermute | solution.py:150
  59.7 8.4 %collective-permute-done.4.over_z = bf16[2,6,2,64,128]{4,3,2,1,0:T(8,128)(2,1)S(1)} collective-permute-done((bf16[2,6,2,64,128]{4,3,2,1,0:T(8,128)(2,1)S(1)}, bf16[2,6,2,64,128]{4,3,2,1,0:T(8,128)(2,1)S(1)}, u32[]{:S(2)}, u32[]{:S(2)}) %collective-permute-start.4) | collective-permute-done | bytes 393248 | tf_op jit(solution)/shard_map/ppermute | solution.py:19
  68.2 0.7 copy-done
  69.7 4.4 %collective-permute-start.6 = (bf16[8,3,16,1536]{3,2,1,0:T(8,128)(2,1)S(1)}, bf16[8,3,16,1536]{3,2,1,0:T(8,128)(2,1)S(1)}, u32[]{:S(2)}, u32[]{:S(2)}) collective-permute-start(bf16[8,3,16,1536]{3,2,1,0:T(8,128)(2,1)S(1)} %all-to-all-done.1.mine), channel_id=1, source_target_pairs={{0,1},{1,0},{2,3},{3,2},{4,5},{5,4},{6,7},{7,6},{8,9},{9,8},{10,11... | collective-permute-start | bytes 3538952 | tf_op jit(solution)/shard_map/ppermute | solution.py:19
  74.3 2.3 %collective-permute-done.6.other = bf16[8,3,16,1536]{3,2,1,0:T(8,128)(2,1)S(1)} collective-permute-done((bf16[8,3,16,1536]{3,2,1,0:T(8,128)(2,1)S(1)}, bf16[8,3,16,1536]{3,2,1,0:T(8,128)(2,1)S(1)}, u32[]{:S(2)}, u32[]{:S(2)}) %collective-permute-start.6) | collective-permute-done | bytes 1179680 | tf_op jit(solution)/shard_map/ppermute | solution.py:19
  76.5 1.0 copy-done.1
  77.5 1.0 copy-done.3
  78.5 8.0 %conv.1 = bf16[8,2,128,256]{3,2,1,0:T(8,128)(2,1)S(1)} custom-call(s32[4]{0:T(128)S(1)} %pad_add_fusion.at_ref, bf16[2,6,2,64,128]{4,3,2,1,0:T(8,128)(2,1)S(1)} %pad_maximum_fusion.here, bf16[2,6,2,64,128]{4,3,2,1,0:T(8,128)(2,1)S(1)} %copy-done.3, bf16[2,6,2,64,128]{4,3,2,1,0:T(8,128)(2,1)S(1)} %copy-done.1, ...), custom_call_target="tpu_custom_call" | custom-call | flops 4899999744 | bytes 6000000 | tf_op jit(solution)/shard_map/conv/pallas_call | solution.py:118
  86.5 18.9 %all_to_all.15 = bf16[8,2,128,256]{3,2,1,0:T(8,128)(2,1)S(1)} all-to-all(bf16[8,2,128,256]{3,2,1,0:T(8,128)(2,1)S(1)} %conv.1), channel_id=1, replica_groups=mesh['x1'=2,'x0'=2,'zh'=2,'y'=8,'zl1'=2,'zl0'=2,'k'=2] {'zl0','x1','x0'}, dimensions={0} | all-to-all | bytes 2097152 | tf_op jit(solution)/shard_map/all_to_all | solution.py:158
  106.8 1.0 reshape.68
  (35 shorter events, 4.9 us)
Async XLA Ops:
  0.0 15.3 %copy-start.4 = (bf16[2,4,64,128]{3,2,1,0:T(8,128)(2,1)S(1)}, bf16[2,4,64,128]{3,2,1,0:T(8,128)(2,1)}, u32[]{:S(2)}) copy-start(bf16[2,4,64,128]{3,2,1,0:T(8,128)(2,1)} %param.3) | copy-start | bytes 393220
  0.9 20.8 %copy-start.5 = (f32[2048]{0:T(1024)S(1)}, f32[2048]{0:T(1024)}, u32[]{:S(2)}) copy-start(f32[2048]{0:T(1024)} %param.5) | copy-start | bytes 24580
  3.4 21.6 %all-to-all-start = ((bf16[16,3,3,2,2,128]{5,4,3,2,1,0:T(2,128)(2,1)}), bf16[16,3,3,2,2,128]{5,4,3,2,1,0:T(2,128)(2,1)S(1)}, u32[]{:S(2)}, u32[]{:S(2)}) async-start(bf16[16,3,3,2,2,128]{5,4,3,2,1,0:T(2,128)(2,1)} %bitcast.7), calls=%async_computation | async-start | bytes 294912 | tf_op jit(solution)/shard_map/all_to_all | solution.py:33
  15.4 7.9 %collective-permute-start = (bf16[1,2,64,128]{3,2,1,0:T(8,128)(2,1)S(1)}, bf16[1,2,64,128]{3,2,1,0:T(8,128)(2,1)S(1)}, u32[]{:S(2)}, u32[]{:S(2)}) collective-permute-start(bf16[1,2,64,128]{3,2,1,0:T(8,128)(2,1)S(1)} %get-tuple-element.21), channel_id=1, source_target_pairs={{0,1},{1,2},{2,3},{3,4},{4,5},{5,6},{6,7},{7,8},{8,9},{9,10},{10,1... | collective-permute-start | bytes 98312 | tf_op jit(solution)/shard_map/ppermute | solution.py:42
  19.8 5.2 %collective-permute-start.1 = (bf16[1,2,64,128]{3,2,1,0:T(8,128)(2,1)S(1)}, bf16[1,2,64,128]{3,2,1,0:T(8,128)(2,1)S(1)}, u32[]{:S(2)}, u32[]{:S(2)}) collective-permute-start(bf16[1,2,64,128]{3,2,1,0:T(8,128)(2,1)S(1)} %get-tuple-element.22), channel_id=1, source_target_pairs={{1,0},{2,1},{3,2},{4,3},{5,4},{6,5},{7,6},{8,7},{9,8},{10,9},{11,1... | collective-permute-start | bytes 98312 | tf_op jit(solution)/shard_map/ppermute | solution.py:43
  26.5 43.2 %all-to-all-start.1 = ((bf16[8,3,16,1536]{3,2,1,0:T(8,128)(2,1)}), bf16[8,3,16,1536]{3,2,1,0:T(8,128)(2,1)S(1)}, u32[]{:S(2)}, u32[]{:S(2)}) async-start(bf16[8,3,16,1536]{3,2,1,0:T(8,128)(2,1)} %broadcast_in_dim.25), calls=%async_computation.1 | async-start | bytes 2359296 | tf_op jit(solution)/shard_map/all_to_all | solution.py:147
  33.5 12.6 %collective-permute-start.2 = (bf16[6,2,64,128]{3,2,1,0:T(8,128)(2,1)S(1)}, bf16[6,2,64,128]{3,2,1,0:T(8,128)(2,1)S(1)}, u32[]{:S(2)}, u32[]{:S(2)}) collective-permute-start(bf16[6,2,64,128]{3,2,1,0:T(8,128)(2,1)S(1)} %pad_maximum_fusion.1), channel_id=1, source_target_pairs={{0,64},{64,0},{1,65},{65,1},{2,66},{66,2},{3,67},{67,3},{4,68},{68... | collective-permute-start | bytes 589832 | tf_op jit(solution)/shard_map/ppermute | solution.py:19
  46.1 13.6 %collective-permute-start.5 = (bf16[2,6,2,64,128]{4,3,2,1,0:T(8,128)(2,1)S(1)}, bf16[2,6,2,64,128]{4,3,2,1,0:T(8,128)(2,1)S(1)}, u32[]{:S(2)}, u32[]{:S(2)}) collective-permute-start(bf16[2,6,2,64,128]{4,3,2,1,0:T(8,128)(2,1)S(1)} %pad_maximum_fusion.here), channel_id=1, source_target_pairs={{0,130},{2,128},{128,2},{130,0},{1,131},{3,129},{129,3},{131,1},{4... | collective-permute-start | bytes 1179656 | tf_op jit(solution)/shard_map/ppermute | solution.py:150
  51.9 16.3 %collective-permute-start.4 = (bf16[2,6,2,64,128]{4,3,2,1,0:T(8,128)(2,1)S(1)}, bf16[2,6,2,64,128]{4,3,2,1,0:T(8,128)(2,1)S(1)}, u32[]{:S(2)}, u32[]{:S(2)}) collective-permute-start(bf16[2,6,2,64,128]{4,3,2,1,0:T(8,128)(2,1)S(1)} %pad_maximum_fusion.here), channel_id=1, source_target_pairs={{0,2},{2,0},{1,3},{3,1},{4,6},{6,4},{5,7},{7,5},{8,10},{10,8},{9,1... | collective-permute-start | bytes 1179656 | tf_op jit(solution)/shard_map/ppermute | solution.py:19
  54.1 14.8 %collective-permute-start.3 = (bf16[2,6,2,64,128]{4,3,2,1,0:T(8,128)(2,1)S(1)}, bf16[2,6,2,64,128]{4,3,2,1,0:T(8,128)(2,1)S(1)}, u32[]{:S(2)}, u32[]{:S(2)}) collective-permute-start(bf16[2,6,2,64,128]{4,3,2,1,0:T(8,128)(2,1)S(1)} %pad_maximum_fusion.here), channel_id=1, source_target_pairs={{0,128},{128,0},{1,129},{129,1},{2,130},{130,2},{3,131},{131,3},{4... | collective-permute-start | bytes 1179656 | tf_op jit(solution)/shard_map/ppermute | solution.py:19
  68.1 0.7 copy-start
  68.9 0.7 copy-start.2
  69.7 6.9 %collective-permute-start.6 = (bf16[8,3,16,1536]{3,2,1,0:T(8,128)(2,1)S(1)}, bf16[8,3,16,1536]{3,2,1,0:T(8,128)(2,1)S(1)}, u32[]{:S(2)}, u32[]{:S(2)}) collective-permute-start(bf16[8,3,16,1536]{3,2,1,0:T(8,128)(2,1)S(1)} %all-to-all-done.1.mine), channel_id=1, source_target_pairs={{0,1},{1,0},{2,3},{3,2},{4,5},{5,4},{6,7},{7,6},{8,9},{9,8},{10,11... | collective-permute-start | bytes 3538952 | tf_op jit(solution)/shard_map/ppermute | solution.py:19
  76.5 1.0 copy-start.1
  77.5 1.0 copy-start.3

commit v6 on v5

--- a/solution.py
+++ b/solution.py
@@ -44,24 +44,41 @@
     return jnp.concatenate([above, rows, below], axis=0)
 
 
-def conv_kernel(
-    at_ref, here, over_x, over_z, over_both, mine, other, bias_ref, perm_ref, out_ref,
-    w_ref, x_ref, even_ref, odd_ref, sems,
-):
-    x0, zh, zl0, core = (at_ref[n] for n in range(4))
+def start_copy(copies, sems, src, dst):
+    copy = pltpu.make_async_copy(src, dst, sems.at[len(copies)])
+    copy.start()
+    copies.append(copy)
+
+
+def pack_kernel(at_ref, here, over_x, over_z, over_both, x_ref, sems):
+    x0, zh, zl0 = (at_ref[n] for n in range(3))
     copies = []
-
-    def start(src, dst):
-        copy = pltpu.make_async_copy(src, dst, sems.at[len(copies)])
-        copy.start()
-        copies.append(copy)
-
     for rows, x, z in ((here, x0, zl0), (over_x, 1 - x0, zl0), (over_z, x0, 1 - zl0), (over_both, 1 - x0, 1 - zl0)):
         for n, h in enumerate((zh, 1 - zh)):
-            start(rows.at[n], x_ref.at[z, :, :, 2 * x + h])
+            start_copy(copies, sems, rows.at[n], x_ref.at[z, :, :, 2 * x + h])
+    for copy in copies:
+        copy.wait()
+
+
+def pack(at, rows):
+    return pl.pallas_call(
+        pack_kernel,
+        out_shape=jax.ShapeDtypeStruct((2, 6, 2, 4, 64, 128), jnp.bfloat16),
+        in_specs=[pl.BlockSpec(memory_space=pltpu.SMEM)] + [pl.BlockSpec(memory_space=pl.ANY)] * 4,
+        out_specs=pl.BlockSpec(memory_space=pltpu.VMEM),
+        scratch_shapes=[pltpu.SemaphoreType.DMA((8,))],
+        compiler_params=pltpu.CompilerParams(vmem_limit_bytes=4 * 1024 * 1024),
+        cost_estimate=pl.CostEstimate(flops=0, bytes_accessed=3_200_000, transcendentals=0),
+        name="pack",
+    )(at, *rows)
+
+
+def conv_kernel(at_ref, x_ref, mine, other, bias_ref, perm_ref, out_ref, w_ref, even_ref, odd_ref, sems):
+    core = at_ref[3]
+    copies = []
     for chunks, owner in ((mine, core), (other, 1 - core)):
         for y in range(NY):
-            start(chunks.at[y], w_ref.at[:, y, owner])
+            start_copy(copies, sems, chunks.at[y], w_ref.at[:, y, owner])
     for copy in copies:
         copy.wait()
 
@@ -119,20 +136,20 @@
         conv_kernel,
         out_shape=jax.ShapeDtypeStruct((8, 2, 128, 256), jnp.bfloat16),
         in_specs=[pl.BlockSpec(memory_space=pltpu.SMEM)]
-        + [pl.BlockSpec(memory_space=pl.ANY)] * 6
+        + [pl.BlockSpec(memory_space=pltpu.VMEM)]
+        + [pl.BlockSpec(memory_space=pl.ANY)] * 2
         + [pl.BlockSpec(memory_space=pltpu.VMEM)] * 2,
         out_specs=pl.BlockSpec(memory_space=pltpu.VMEM),
         scratch_shapes=[
             pltpu.VMEM((3, NY, 2, 16, 1536), jnp.bfloat16),
-            pltpu.VMEM((2, 6, 2, 4, 64, 128), jnp.bfloat16),
             pltpu.VMEM((768, 128 * ROWS), jnp.float32),
             pltpu.VMEM((768, 128 * ROWS), jnp.float32),
             pltpu.SemaphoreType.DMA((24,)),
         ],
-        compiler_params=pltpu.CompilerParams(vmem_limit_bytes=36 * 1024 * 1024),
+        compiler_params=pltpu.CompilerParams(vmem_limit_bytes=18 * 1024 * 1024),
         cost_estimate=pl.CostEstimate(flops=4_900_000_000, bytes_accessed=6_000_000, transcendentals=0),
         name="conv",
-    )(at, *rows, *chunks, bias, perm)
+    )(at, rows, *chunks, bias, perm)
 
 
 def local(latent, kernel, bias):
@@ -149,12 +166,13 @@
     over_x, over_z = swap(rows, "x0"), swap(rows, "zl0")
     over_both = lax.ppermute(rows, ("x0", "zl0"), [(i, 3 - i) for i in range(4)])
     mine, rows, over_x, over_z, over_both = lax.optimization_barrier((mine, rows, over_x, over_z, over_both))
+    at = jnp.stack([x0, zh, zl0, core]).astype(jnp.int32)
+    packed = pack(at, (rows, over_x, over_z, over_both))
     other = swap(mine, "k")
 
     place = jnp.arange(256)
     perm = ((2 * (place % 128) + place // 128)[:, None] == place[None, :]).astype(jnp.bfloat16)
-    at = jnp.stack([x0, zh, zl0, core]).astype(jnp.int32)
-    out = convolve(at, (rows, over_x, over_z, over_both), (mine, other), column, perm)
+    out = convolve(at, packed, (mine, other), column, perm)
     got = lax.all_to_all(out, ("zl0", "x1", "x0"), 0, 0, tiled=True).reshape(2, 2, 2, 2, NY, 2, 4, 2, 256)
     total = (got[:, 0].astype(jnp.float32) + got[:, 1].astype(jnp.float32)).astype(jnp.bfloat16)
     return jnp.transpose(total, (2, 3, 5, 4, 1, 0, 6, 7)).reshape(2, 1, 512, 256)

time: 109 us -> 106 us (0.972)
  local copies, waits for them, and re-layouts: 10.2 us -> 6.74 us
  Pallas kernels: 7.99 us -> 9.5 us
    unnamed x13 -> x5, local copies, waits for them, and re-layouts: 3.5 us -> 0.02 us
  transfers between devices with their start and end apart: 9 -> 9, of which waited for: 5 -> 6; matrix products, arithmetic and copies ran while one was open for 2% -> 2% of each run, Pallas kernels for 0% -> 1%
where the time goes in v6:
time: 106 us; the launch traced here: 105 us
  starting transfers between devices  45.8 us (43%)
  waiting for transfers between devices  21.9 us (21%)
  blocking collectives  18.7 us (18%)
  Pallas kernels  9.5 us (9%)
  local copies, waits for them, and re-layouts  6.74 us (6%)
  other arithmetic  2.23 us (2%)
    all_to_all x1, blocking collectives, local(): lax.all_to_all(out, ('zl0', 'x1', 'x0'), 0, 0, tiled=True)  18.7 us
    ppermute x4, waiting for transfers between devices, swap(): return lax.ppermute(array, axis, ring(2, 1))  16.4 us
    ppermute x4, starting transfers between devices, swap(): return lax.ppermute(array, axis, ring(2, 1))  14.9 us
    all_to_all x1, starting transfers between devices, own_chunk(): got = lax.all_to_all(pieces, ('x0', 'zh', 'zl1', 'zl0'), 0, 0, tiled=True)  11.9 us
    pallas_call x1, Pallas kernels, convolve(): pl.pallas_call(conv_kernel, out_shape=jax.ShapeDtypeStruct((8, 2, 128, 25...  8.62 us
    all_to_all x1, starting transfers between devices, local(): lax.all_to_all(jnp.broadcast_to(own, (NY, *own.shape)), 'y', 0, 0, tiled=...  7.01 us
    ppermute x1, starting transfers between devices, local(): lax.ppermute(rows, ('x0', 'zl0'), [(i, 3 - i) for i in range(4)])  5.74 us
    ppermute x1, starting transfers between devices, own_rows(): above = lax.ppermute(rows[3:], tile, up)  4.39 us
  transfers between devices with their start and end apart: 9, of which 6 were waited for; matrix products, arithmetic and copies ran while one was open for 2% of the time, Pallas kernels for 1%

profile of v6, /device:TPU:1, one launch (start us, length us, event | category | flops | bytes accessed | tf_op | source)
XLA Modules:
  0.0 105.1 jit_solution(15689390944361955018)
XLA Ops:
  0.0 0.9 slice.23
  0.9 1.0 add_convert_fusion.1
  2.7 0.7 broadcast_in_dim.22
  3.4 11.9 %all-to-all-start = ((bf16[16,3,3,2,2,128]{5,4,3,2,1,0:T(2,128)(2,1)}), bf16[16,3,3,2,2,128]{5,4,3,2,1,0:T(2,128)(2,1)S(1)}, u32[]{:S(2)}, u32[]{:S(2)}) async-start(bf16[16,3,3,2,2,128]{5,4,3,2,1,0:T(2,128)(2,1)} %bitcast.7), calls=%async_computation | async-start | bytes 294912 | tf_op jit(solution)/shard_map/all_to_all | solution.py:33
  15.4 4.4 %collective-permute-start = (bf16[1,2,64,128]{3,2,1,0:T(8,128)(2,1)S(1)}, bf16[1,2,64,128]{3,2,1,0:T(8,128)(2,1)S(1)}, u32[]{:S(2)}, u32[]{:S(2)}) collective-permute-start(bf16[1,2,64,128]{3,2,1,0:T(8,128)(2,1)S(1)} %get-tuple-element.21), channel_id=1, source_target_pairs={{0,1},{1,2},{2,3},{3,4},{4,5},{5,6},{6,7},{7,8},{8,9},{9,10},{10,1... | collective-permute-start | bytes 98312 | tf_op jit(solution)/shard_map/ppermute | solution.py:42
  19.8 1.9 %collective-permute-start.1 = (bf16[1,2,64,128]{3,2,1,0:T(8,128)(2,1)S(1)}, bf16[1,2,64,128]{3,2,1,0:T(8,128)(2,1)S(1)}, u32[]{:S(2)}, u32[]{:S(2)}) collective-permute-start(bf16[1,2,64,128]{3,2,1,0:T(8,128)(2,1)S(1)} %get-tuple-element.22), channel_id=1, source_target_pairs={{1,0},{2,1},{3,2},{4,3},{5,4},{6,5},{7,6},{8,7},{9,8},{10,9},{11,1... | collective-permute-start | bytes 98312 | tf_op jit(solution)/shard_map/ppermute | solution.py:43
  21.7 0.8 reshape.66
  23.2 1.8 %collective-permute-done.1 = bf16[1,2,64,128]{3,2,1,0:T(8,128)(2,1)S(1)} collective-permute-done((bf16[1,2,64,128]{3,2,1,0:T(8,128)(2,1)S(1)}, bf16[1,2,64,128]{3,2,1,0:T(8,128)(2,1)S(1)}, u32[]{:S(2)}, u32[]{:S(2)}) %collective-permute-start.1) | collective-permute-done | bytes 32800 | tf_op jit(solution)/shard_map/ppermute | solution.py:43
  25.3 1.2 %broadcast_in_dim.25 = bf16[8,3,16,1536]{3,2,1,0:T(8,128)(2,1)} broadcast(bf16[3,16,1536]{2,1,0:T(8,128)(2,1)S(1)} %reshape.65), dimensions={1,2,3} | broadcast | bytes 1327104 | tf_op jit(solution)/shard_map/broadcast_in_dim | solution.py:164
  26.4 7.0 %all-to-all-start.1 = ((bf16[8,3,16,1536]{3,2,1,0:T(8,128)(2,1)}), bf16[8,3,16,1536]{3,2,1,0:T(8,128)(2,1)S(1)}, u32[]{:S(2)}, u32[]{:S(2)}) async-start(bf16[8,3,16,1536]{3,2,1,0:T(8,128)(2,1)} %broadcast_in_dim.25), calls=%async_computation.1 | async-start | bytes 2359296 | tf_op jit(solution)/shard_map/all_to_all | solution.py:164
  33.5 6.2 %collective-permute-start.2 = (bf16[6,2,64,128]{3,2,1,0:T(8,128)(2,1)S(1)}, bf16[6,2,64,128]{3,2,1,0:T(8,128)(2,1)S(1)}, u32[]{:S(2)}, u32[]{:S(2)}) collective-permute-start(bf16[6,2,64,128]{3,2,1,0:T(8,128)(2,1)S(1)} %pad_maximum_fusion.1), channel_id=1, source_target_pairs={{0,64},{64,0},{1,65},{65,1},{2,66},{66,2},{3,67},{67,3},{4,68},{68... | collective-permute-start | bytes 589832 | tf_op jit(solution)/shard_map/ppermute | solution.py:19
  39.7 6.4 %collective-permute-done.2 = bf16[6,2,64,128]{3,2,1,0:T(8,128)(2,1)S(1)} collective-permute-done((bf16[6,2,64,128]{3,2,1,0:T(8,128)(2,1)S(1)}, bf16[6,2,64,128]{3,2,1,0:T(8,128)(2,1)S(1)}, u32[]{:S(2)}, u32[]{:S(2)}) %collective-permute-start.2) | collective-permute-done | bytes 196640 | tf_op jit(solution)/shard_map/ppermute | solution.py:19
  46.1 5.7 %collective-permute-start.5 = (bf16[2,6,2,64,128]{4,3,2,1,0:T(8,128)(2,1)S(1)}, bf16[2,6,2,64,128]{4,3,2,1,0:T(8,128)(2,1)S(1)}, u32[]{:S(2)}, u32[]{:S(2)}) collective-permute-start(bf16[2,6,2,64,128]{4,3,2,1,0:T(8,128)(2,1)S(1)} %pad_maximum_fusion.here), channel_id=1, source_target_pairs={{0,130},{2,128},{128,2},{130,0},{1,131},{3,129},{129,3},{131,1},{4... | collective-permute-start | bytes 1179656 | tf_op jit(solution)/shard_map/ppermute | solution.py:167
  51.9 2.2 %collective-permute-start.4 = (bf16[2,6,2,64,128]{4,3,2,1,0:T(8,128)(2,1)S(1)}, bf16[2,6,2,64,128]{4,3,2,1,0:T(8,128)(2,1)S(1)}, u32[]{:S(2)}, u32[]{:S(2)}) collective-permute-start(bf16[2,6,2,64,128]{4,3,2,1,0:T(8,128)(2,1)S(1)} %pad_maximum_fusion.here), channel_id=1, source_target_pairs={{0,2},{2,0},{1,3},{3,1},{4,6},{6,4},{5,7},{7,5},{8,10},{10,8},{9,1... | collective-permute-start | bytes 1179656 | tf_op jit(solution)/shard_map/ppermute | solution.py:19
  54.1 1.9 %collective-permute-start.3 = (bf16[2,6,2,64,128]{4,3,2,1,0:T(8,128)(2,1)S(1)}, bf16[2,6,2,64,128]{4,3,2,1,0:T(8,128)(2,1)S(1)}, u32[]{:S(2)}, u32[]{:S(2)}) collective-permute-start(bf16[2,6,2,64,128]{4,3,2,1,0:T(8,128)(2,1)S(1)} %pad_maximum_fusion.here), channel_id=1, source_target_pairs={{0,128},{128,0},{1,129},{129,1},{2,130},{130,2},{3,131},{131,3},{4... | collective-permute-start | bytes 1179656 | tf_op jit(solution)/shard_map/ppermute | solution.py:19
  56.0 3.7 %collective-permute-done.5.over_both = bf16[2,6,2,64,128]{4,3,2,1,0:T(8,128)(2,1)S(1)} collective-permute-done((bf16[2,6,2,64,128]{4,3,2,1,0:T(8,128)(2,1)S(1)}, bf16[2,6,2,64,128]{4,3,2,1,0:T(8,128)(2,1)S(1)}, u32[]{:S(2)}, u32[]{:S(2)}) %collective-permute-start.5) | collective-permute-done | bytes 393248 | tf_op jit(solution)/shard_map/ppermute | solution.py:167
  59.7 8.4 %collective-permute-done.4.over_z = bf16[2,6,2,64,128]{4,3,2,1,0:T(8,128)(2,1)S(1)} collective-permute-done((bf16[2,6,2,64,128]{4,3,2,1,0:T(8,128)(2,1)S(1)}, bf16[2,6,2,64,128]{4,3,2,1,0:T(8,128)(2,1)S(1)}, u32[]{:S(2)}, u32[]{:S(2)}) %collective-permute-start.4) | collective-permute-done | bytes 393248 | tf_op jit(solution)/shard_map/ppermute | solution.py:19
  68.2 4.5 %collective-permute-start.6 = (bf16[8,3,16,1536]{3,2,1,0:T(8,128)(2,1)S(1)}, bf16[8,3,16,1536]{3,2,1,0:T(8,128)(2,1)}, u32[]{:S(2)}, u32[]{:S(2)}) collective-permute-start(bf16[8,3,16,1536]{3,2,1,0:T(8,128)(2,1)S(1)} %all-to-all-done.1.mine), channel_id=1, source_target_pairs={{0,1},{1,0},{2,3},{3,2},{4,5},{5,4},{6,7},{7,6},{8,9},{9,8},{10,11... | collective-permute-start | bytes 3538952 | tf_op jit(solution)/shard_map/ppermute | solution.py:19
  72.9 0.9 pack.1.x_ref
  73.8 1.5 %collective-permute-done.6.other = bf16[8,3,16,1536]{3,2,1,0:T(8,128)(2,1)} collective-permute-done((bf16[8,3,16,1536]{3,2,1,0:T(8,128)(2,1)S(1)}, bf16[8,3,16,1536]{3,2,1,0:T(8,128)(2,1)}, u32[]{:S(2)}, u32[]{:S(2)}) %collective-permute-start.6) | collective-permute-done | bytes 1179680 | tf_op jit(solution)/shard_map/ppermute | solution.py:19
  75.3 8.6 %conv.1 = bf16[8,2,128,256]{3,2,1,0:T(8,128)(2,1)S(1)} custom-call(s32[4]{0:T(128)S(1)} %pad_add_fusion.at_ref, bf16[2,6,2,4,64,128]{5,4,3,2,1,0:T(8,128)(2,1)S(1)} %pack.1.x_ref, bf16[8,3,16,1536]{3,2,1,0:T(8,128)(2,1)S(1)} %all-to-all-done.1.mine, bf16[8,3,16,1536]{3,2,1,0:T(8,128)(2,1)} %collective-permute-done.6.other, ...), custom_call_target="tpu_custom_call" | custom-call | flops 4899999744 | bytes 6000000 | tf_op jit(solution)/shard_map/conv/pallas_call | solution.py:135
  83.9 18.7 %all_to_all.15 = bf16[8,2,128,256]{3,2,1,0:T(8,128)(2,1)S(1)} all-to-all(bf16[8,2,128,256]{3,2,1,0:T(8,128)(2,1)S(1)} %conv.1), channel_id=1, replica_groups=mesh['x1'=2,'x0'=2,'zh'=2,'y'=8,'zl1'=2,'zl0'=2,'k'=2] {'zl0','x1','x0'}, dimensions={0} | all-to-all | bytes 2097152 | tf_op jit(solution)/shard_map/all_to_all | solution.py:176
  103.1 0.5 fusion
  104.1 1.0 reshape.68
  (28 shorter events, 2.9 us)
Async XLA Ops:
  0.0 15.3 %copy-start = (bf16[2,4,64,128]{3,2,1,0:T(8,128)(2,1)S(1)}, bf16[2,4,64,128]{3,2,1,0:T(8,128)(2,1)}, u32[]{:S(2)}) copy-start(bf16[2,4,64,128]{3,2,1,0:T(8,128)(2,1)} %param.3) | copy-start | bytes 393220
  0.9 20.8 %copy-start.1 = (f32[2048]{0:T(1024)S(1)}, f32[2048]{0:T(1024)}, u32[]{:S(2)}) copy-start(f32[2048]{0:T(1024)} %param.5) | copy-start | bytes 24580
  3.4 21.6 %all-to-all-start = ((bf16[16,3,3,2,2,128]{5,4,3,2,1,0:T(2,128)(2,1)}), bf16[16,3,3,2,2,128]{5,4,3,2,1,0:T(2,128)(2,1)S(1)}, u32[]{:S(2)}, u32[]{:S(2)}) async-start(bf16[16,3,3,2,2,128]{5,4,3,2,1,0:T(2,128)(2,1)} %bitcast.7), calls=%async_computation | async-start | bytes 294912 | tf_op jit(solution)/shard_map/all_to_all | solution.py:33
  15.4 7.9 %collective-permute-start = (bf16[1,2,64,128]{3,2,1,0:T(8,128)(2,1)S(1)}, bf16[1,2,64,128]{3,2,1,0:T(8,128)(2,1)S(1)}, u32[]{:S(2)}, u32[]{:S(2)}) collective-permute-start(bf16[1,2,64,128]{3,2,1,0:T(8,128)(2,1)S(1)} %get-tuple-element.21), channel_id=1, source_target_pairs={{0,1},{1,2},{2,3},{3,4},{4,5},{5,6},{6,7},{7,8},{8,9},{9,10},{10,1... | collective-permute-start | bytes 98312 | tf_op jit(solution)/shard_map/ppermute | solution.py:42
  19.8 5.2 %collective-permute-start.1 = (bf16[1,2,64,128]{3,2,1,0:T(8,128)(2,1)S(1)}, bf16[1,2,64,128]{3,2,1,0:T(8,128)(2,1)S(1)}, u32[]{:S(2)}, u32[]{:S(2)}) collective-permute-start(bf16[1,2,64,128]{3,2,1,0:T(8,128)(2,1)S(1)} %get-tuple-element.22), channel_id=1, source_target_pairs={{1,0},{2,1},{3,2},{4,3},{5,4},{6,5},{7,6},{8,7},{9,8},{10,9},{11,1... | collective-permute-start | bytes 98312 | tf_op jit(solution)/shard_map/ppermute | solution.py:43
  26.4 41.7 %all-to-all-start.1 = ((bf16[8,3,16,1536]{3,2,1,0:T(8,128)(2,1)}), bf16[8,3,16,1536]{3,2,1,0:T(8,128)(2,1)S(1)}, u32[]{:S(2)}, u32[]{:S(2)}) async-start(bf16[8,3,16,1536]{3,2,1,0:T(8,128)(2,1)} %broadcast_in_dim.25), calls=%async_computation.1 | async-start | bytes 2359296 | tf_op jit(solution)/shard_map/all_to_all | solution.py:164
  33.5 12.6 %collective-permute-start.2 = (bf16[6,2,64,128]{3,2,1,0:T(8,128)(2,1)S(1)}, bf16[6,2,64,128]{3,2,1,0:T(8,128)(2,1)S(1)}, u32[]{:S(2)}, u32[]{:S(2)}) collective-permute-start(bf16[6,2,64,128]{3,2,1,0:T(8,128)(2,1)S(1)} %pad_maximum_fusion.1), channel_id=1, source_target_pairs={{0,64},{64,0},{1,65},{65,1},{2,66},{66,2},{3,67},{67,3},{4,68},{68... | collective-permute-start | bytes 589832 | tf_op jit(solution)/shard_map/ppermute | solution.py:19
  46.1 13.6 %collective-permute-start.5 = (bf16[2,6,2,64,128]{4,3,2,1,0:T(8,128)(2,1)S(1)}, bf16[2,6,2,64,128]{4,3,2,1,0:T(8,128)(2,1)S(1)}, u32[]{:S(2)}, u32[]{:S(2)}) collective-permute-start(bf16[2,6,2,64,128]{4,3,2,1,0:T(8,128)(2,1)S(1)} %pad_maximum_fusion.here), channel_id=1, source_target_pairs={{0,130},{2,128},{128,2},{130,0},{1,131},{3,129},{129,3},{131,1},{4... | collective-permute-start | bytes 1179656 | tf_op jit(solution)/shard_map/ppermute | solution.py:167
  51.9 16.3 %collective-permute-start.4 = (bf16[2,6,2,64,128]{4,3,2,1,0:T(8,128)(2,1)S(1)}, bf16[2,6,2,64,128]{4,3,2,1,0:T(8,128)(2,1)S(1)}, u32[]{:S(2)}, u32[]{:S(2)}) collective-permute-start(bf16[2,6,2,64,128]{4,3,2,1,0:T(8,128)(2,1)S(1)} %pad_maximum_fusion.here), channel_id=1, source_target_pairs={{0,2},{2,0},{1,3},{3,1},{4,6},{6,4},{5,7},{7,5},{8,10},{10,8},{9,1... | collective-permute-start | bytes 1179656 | tf_op jit(solution)/shard_map/ppermute | solution.py:19
  54.1 14.1 %collective-permute-start.3 = (bf16[2,6,2,64,128]{4,3,2,1,0:T(8,128)(2,1)S(1)}, bf16[2,6,2,64,128]{4,3,2,1,0:T(8,128)(2,1)S(1)}, u32[]{:S(2)}, u32[]{:S(2)}) collective-permute-start(bf16[2,6,2,64,128]{4,3,2,1,0:T(8,128)(2,1)S(1)} %pad_maximum_fusion.here), channel_id=1, source_target_pairs={{0,128},{128,0},{1,129},{129,1},{2,130},{130,2},{3,131},{131,3},{4... | collective-permute-start | bytes 1179656 | tf_op jit(solution)/shard_map/ppermute | solution.py:19
  68.2 7.1 %collective-permute-start.6 = (bf16[8,3,16,1536]{3,2,1,0:T(8,128)(2,1)S(1)}, bf16[8,3,16,1536]{3,2,1,0:T(8,128)(2,1)}, u32[]{:S(2)}, u32[]{:S(2)}) collective-permute-start(bf16[8,3,16,1536]{3,2,1,0:T(8,128)(2,1)S(1)} %all-to-all-done.1.mine), channel_id=1, source_target_pairs={{0,1},{1,0},{2,3},{3,2},{4,5},{5,4},{6,7},{7,6},{8,9},{9,8},{10,11... | collective-permute-start | bytes 3538952 | tf_op jit(solution)/shard_map/ppermute | solution.py:19

commit v7 on v6

--- a/solution.py
+++ b/solution.py
@@ -73,15 +73,8 @@
     )(at, *rows)
 
 
-def conv_kernel(at_ref, x_ref, mine, other, bias_ref, perm_ref, out_ref, w_ref, even_ref, odd_ref, sems):
-    core = at_ref[3]
-    copies = []
-    for chunks, owner in ((mine, core), (other, 1 - core)):
-        for y in range(NY):
-            start_copy(copies, sems, chunks.at[y], w_ref.at[:, y, owner])
-    for copy in copies:
-        copy.wait()
-
+def conv_kernel(at_ref, x_ref, mine, other, bias_ref, perm_ref, out_ref, even_ref, odd_ref):
+    first = at_ref[3] == 0
     lane = lax.broadcasted_iota(jnp.int32, (256, 128), 1)
     count = 8 // ROWS
 
@@ -99,7 +92,8 @@
                     parts.append(x_ref[z, row + q + b, 0, chan])
                     parts.append(x_ref[z, row + q + b, frame, chan])
             sides.append(jnp.concatenate(parts, axis=0))
-        taps = w_ref[...].reshape(768, 1536)
+        taps = [half[y, c] for c in range(3) for y in range(NY) for half in (mine, other)]
+        taps = jnp.concatenate(taps, axis=0)
         return jnp.dot(taps, jnp.concatenate(sides, axis=1), preferred_element_type=jnp.float32)
 
     def finish(total_ref, n):
@@ -110,8 +104,9 @@
             before = jnp.where(lane == 0, 0.0, pltpu.roll(total_ref[:256, lanes], 1, 1))
             after = jnp.where(lane == 127, 0.0, pltpu.roll(total_ref[512:, lanes], 127, 1))
             conv = before + total_ref[256:512, lanes] + after + bias_ref[...]
-            conv = conv.reshape(16, 2, 8, 128)
-            mixed.append(jnp.concatenate([conv[:, 0].reshape(128, 128), conv[:, 1].reshape(128, 128)], axis=1))
+            conv = conv.reshape(NY, 2, 2, 8, 128)
+            conv = jnp.where(first, conv, jnp.concatenate([conv[:, 1:], conv[:, :1]], axis=1))
+            mixed.append(jnp.concatenate([conv[:, :, s].reshape(128, 128) for s in range(2)], axis=1))
         mixed = jnp.concatenate(mixed, axis=0).astype(jnp.bfloat16)
         mixed = jnp.dot(mixed, perm_ref[...], preferred_element_type=jnp.float32).astype(jnp.bfloat16)
         for q in range(ROWS):
@@ -136,15 +131,11 @@
         conv_kernel,
         out_shape=jax.ShapeDtypeStruct((8, 2, 128, 256), jnp.bfloat16),
         in_specs=[pl.BlockSpec(memory_space=pltpu.SMEM)]
-        + [pl.BlockSpec(memory_space=pltpu.VMEM)]
-        + [pl.BlockSpec(memory_space=pl.ANY)] * 2
-        + [pl.BlockSpec(memory_space=pltpu.VMEM)] * 2,
+        + [pl.BlockSpec(memory_space=pltpu.VMEM)] * 5,
         out_specs=pl.BlockSpec(memory_space=pltpu.VMEM),
         scratch_shapes=[
-            pltpu.VMEM((3, NY, 2, 16, 1536), jnp.bfloat16),
             pltpu.VMEM((768, 128 * ROWS), jnp.float32),
             pltpu.VMEM((768, 128 * ROWS), jnp.float32),
-            pltpu.SemaphoreType.DMA((24,)),
         ],
         compiler_params=pltpu.CompilerParams(vmem_limit_bytes=18 * 1024 * 1024),
         cost_estimate=pl.CostEstimate(flops=4_900_000_000, bytes_accessed=6_000_000, transcendentals=0),
@@ -155,6 +146,7 @@
 def local(latent, kernel, bias):
     x1, x0, zh, zl0, core = (lax.axis_index(a) for a in ("x1", "x0", "zh", "zl0", "k"))
     picked = bias.reshape(NY, 4, 2, 2, 2, 2, 2, 2)[:, :, :, x0, zl0, :, zh, :]
+    picked = jnp.where(core == 0, picked, picked[:, :, ::-1])
     column = jnp.transpose(picked, (0, 2, 4, 1, 3)).reshape(256, 1)
     column = jnp.broadcast_to(jnp.where(x1 == 0, column, 0.0), (256, 128))
     rows = own_rows(latent)
@@ -173,8 +165,9 @@
     place = jnp.arange(256)
     perm = ((2 * (place % 128) + place // 128)[:, None] == place[None, :]).astype(jnp.bfloat16)
     out = convolve(at, packed, (mine, other), column, perm)
-    got = lax.all_to_all(out, ("zl0", "x1", "x0"), 0, 0, tiled=True).reshape(2, 2, 2, 2, NY, 2, 4, 2, 256)
+    got = lax.all_to_all(out, ("zl0", "x1", "x0"), 0, 0, tiled=True).reshape(2, 2, 2, 2, 128, 256)
     total = (got[:, 0].astype(jnp.float32) + got[:, 1].astype(jnp.float32)).astype(jnp.bfloat16)
+    total = total.reshape(2, 2, 2, NY, 2, 4, 2, 256)
     return jnp.transpose(total, (2, 3, 5, 4, 1, 0, 6, 7)).reshape(2, 1, 512, 256)
 
 

time: 106 us -> 103 us (0.972)
  Pallas kernels: 9.5 us -> 7.44 us
    pallas_call x1, Pallas kernels: 8.62 us -> 6.57 us  [convolve(): pl.pallas_call(conv_kernel, out_shape=jax.ShapeDtypeStruct((8, 2, 128, 25...]
where the time goes in v7:
time: 103 us; the launch traced here: 102 us
  starting transfers between devices  45.8 us (44%)
  waiting for transfers between devices  21.8 us (21%)
  blocking collectives  18.7 us (18%)
  Pallas kernels  7.44 us (7%)
  local copies, waits for them, and re-layouts  6.47 us (6%)
  other arithmetic  1.74 us (2%)
    all_to_all x1, blocking collectives, local(): lax.all_to_all(out, ('zl0', 'x1', 'x0'), 0, 0, tiled=True)  18.7 us
    ppermute x4, waiting for transfers between devices, swap(): return lax.ppermute(array, axis, ring(2, 1))  16.3 us
    ppermute x4, starting transfers between devices, swap(): return lax.ppermute(array, axis, ring(2, 1))  14.9 us
    all_to_all x1, starting transfers between devices, own_chunk(): got = lax.all_to_all(pieces, ('x0', 'zh', 'zl1', 'zl0'), 0, 0, tiled=True)  11.9 us
    all_to_all x1, starting transfers between devices, local(): lax.all_to_all(jnp.broadcast_to(own, (NY, *own.shape)), 'y', 0, 0, tiled=...  7.01 us
    pallas_call x1, Pallas kernels, convolve(): pl.pallas_call(conv_kernel, out_shape=jax.ShapeDtypeStruct((8, 2, 128, 25...  6.57 us
    ppermute x1, starting transfers between devices, local(): lax.ppermute(rows, ('x0', 'zl0'), [(i, 3 - i) for i in range(4)])  5.74 us
    ppermute x1, starting transfers between devices, own_rows(): above = lax.ppermute(rows[3:], tile, up)  4.39 us
  transfers between devices with their start and end apart: 9, of which 6 were waited for; matrix products, arithmetic and copies ran while one was open for 2% of the time, Pallas kernels for 1%

profile of v7, /device:TPU:1, one launch (start us, length us, event | category | flops | bytes accessed | tf_op | source)
XLA Modules:
  0.0 102.3 jit_solution(13661528799689059986)
XLA Ops:
  0.0 0.9 slice.23
  0.9 1.0 add_convert_fusion.1
  2.7 0.7 broadcast_in_dim.22
  3.4 11.9 %all-to-all-start = ((bf16[16,3,3,2,2,128]{5,4,3,2,1,0:T(2,128)(2,1)}), bf16[16,3,3,2,2,128]{5,4,3,2,1,0:T(2,128)(2,1)S(1)}, u32[]{:S(2)}, u32[]{:S(2)}) async-start(bf16[16,3,3,2,2,128]{5,4,3,2,1,0:T(2,128)(2,1)} %bitcast.7), calls=%async_computation | async-start | bytes 294912 | tf_op jit(solution)/shard_map/all_to_all | solution.py:33
  15.4 4.4 %collective-permute-start = (bf16[1,2,64,128]{3,2,1,0:T(8,128)(2,1)S(1)}, bf16[1,2,64,128]{3,2,1,0:T(8,128)(2,1)S(1)}, u32[]{:S(2)}, u32[]{:S(2)}) collective-permute-start(bf16[1,2,64,128]{3,2,1,0:T(8,128)(2,1)S(1)} %get-tuple-element.21), channel_id=1, source_target_pairs={{0,1},{1,2},{2,3},{3,4},{4,5},{5,6},{6,7},{7,8},{8,9},{9,10},{10,1... | collective-permute-start | bytes 98312 | tf_op jit(solution)/shard_map/ppermute | solution.py:42
  19.8 1.9 %collective-permute-start.1 = (bf16[1,2,64,128]{3,2,1,0:T(8,128)(2,1)S(1)}, bf16[1,2,64,128]{3,2,1,0:T(8,128)(2,1)S(1)}, u32[]{:S(2)}, u32[]{:S(2)}) collective-permute-start(bf16[1,2,64,128]{3,2,1,0:T(8,128)(2,1)S(1)} %get-tuple-element.22), channel_id=1, source_target_pairs={{1,0},{2,1},{3,2},{4,3},{5,4},{6,5},{7,6},{8,7},{9,8},{10,9},{11,1... | collective-permute-start | bytes 98312 | tf_op jit(solution)/shard_map/ppermute | solution.py:43
  21.7 0.8 reshape.66
  23.1 1.9 %collective-permute-done.1 = bf16[1,2,64,128]{3,2,1,0:T(8,128)(2,1)S(1)} collective-permute-done((bf16[1,2,64,128]{3,2,1,0:T(8,128)(2,1)S(1)}, bf16[1,2,64,128]{3,2,1,0:T(8,128)(2,1)S(1)}, u32[]{:S(2)}, u32[]{:S(2)}) %collective-permute-start.1) | collective-permute-done | bytes 32800 | tf_op jit(solution)/shard_map/ppermute | solution.py:43
  25.3 1.2 %broadcast_in_dim.25 = bf16[8,3,16,1536]{3,2,1,0:T(8,128)(2,1)} broadcast(bf16[3,16,1536]{2,1,0:T(8,128)(2,1)S(1)} %reshape.65), dimensions={1,2,3} | broadcast | bytes 1327104 | tf_op jit(solution)/shard_map/broadcast_in_dim | solution.py:156
  26.4 7.0 %all-to-all-start.1 = ((bf16[8,3,16,1536]{3,2,1,0:T(8,128)(2,1)}), bf16[8,3,16,1536]{3,2,1,0:T(8,128)(2,1)S(1)}, u32[]{:S(2)}, u32[]{:S(2)}) async-start(bf16[8,3,16,1536]{3,2,1,0:T(8,128)(2,1)} %broadcast_in_dim.25), calls=%async_computation.1 | async-start | bytes 2359296 | tf_op jit(solution)/shard_map/all_to_all | solution.py:156
  33.5 6.2 %collective-permute-start.2 = (bf16[6,2,64,128]{3,2,1,0:T(8,128)(2,1)S(1)}, bf16[6,2,64,128]{3,2,1,0:T(8,128)(2,1)S(1)}, u32[]{:S(2)}, u32[]{:S(2)}) collective-permute-start(bf16[6,2,64,128]{3,2,1,0:T(8,128)(2,1)S(1)} %pad_maximum_fusion.1), channel_id=1, source_target_pairs={{0,64},{64,0},{1,65},{65,1},{2,66},{66,2},{3,67},{67,3},{4,68},{68... | collective-permute-start | bytes 589832 | tf_op jit(solution)/shard_map/ppermute | solution.py:19
  39.7 6.4 %collective-permute-done.2 = bf16[6,2,64,128]{3,2,1,0:T(8,128)(2,1)S(1)} collective-permute-done((bf16[6,2,64,128]{3,2,1,0:T(8,128)(2,1)S(1)}, bf16[6,2,64,128]{3,2,1,0:T(8,128)(2,1)S(1)}, u32[]{:S(2)}, u32[]{:S(2)}) %collective-permute-start.2) | collective-permute-done | bytes 196640 | tf_op jit(solution)/shard_map/ppermute | solution.py:19
  46.1 5.7 %collective-permute-start.5 = (bf16[2,6,2,64,128]{4,3,2,1,0:T(8,128)(2,1)S(1)}, bf16[2,6,2,64,128]{4,3,2,1,0:T(8,128)(2,1)S(1)}, u32[]{:S(2)}, u32[]{:S(2)}) collective-permute-start(bf16[2,6,2,64,128]{4,3,2,1,0:T(8,128)(2,1)S(1)} %pad_maximum_fusion.here), channel_id=1, source_target_pairs={{0,130},{2,128},{128,2},{130,0},{1,131},{3,129},{129,3},{131,1},{4... | collective-permute-start | bytes 1179656 | tf_op jit(solution)/shard_map/ppermute | solution.py:159
  51.9 2.2 %collective-permute-start.4 = (bf16[2,6,2,64,128]{4,3,2,1,0:T(8,128)(2,1)S(1)}, bf16[2,6,2,64,128]{4,3,2,1,0:T(8,128)(2,1)S(1)}, u32[]{:S(2)}, u32[]{:S(2)}) collective-permute-start(bf16[2,6,2,64,128]{4,3,2,1,0:T(8,128)(2,1)S(1)} %pad_maximum_fusion.here), channel_id=1, source_target_pairs={{0,2},{2,0},{1,3},{3,1},{4,6},{6,4},{5,7},{7,5},{8,10},{10,8},{9,1... | collective-permute-start | bytes 1179656 | tf_op jit(solution)/shard_map/ppermute | solution.py:19
  54.1 1.9 %collective-permute-start.3 = (bf16[2,6,2,64,128]{4,3,2,1,0:T(8,128)(2,1)S(1)}, bf16[2,6,2,64,128]{4,3,2,1,0:T(8,128)(2,1)S(1)}, u32[]{:S(2)}, u32[]{:S(2)}) collective-permute-start(bf16[2,6,2,64,128]{4,3,2,1,0:T(8,128)(2,1)S(1)} %pad_maximum_fusion.here), channel_id=1, source_target_pairs={{0,128},{128,0},{1,129},{129,1},{2,130},{130,2},{3,131},{131,3},{4... | collective-permute-start | bytes 1179656 | tf_op jit(solution)/shard_map/ppermute | solution.py:19
  56.0 3.7 %collective-permute-done.5.over_both = bf16[2,6,2,64,128]{4,3,2,1,0:T(8,128)(2,1)S(1)} collective-permute-done((bf16[2,6,2,64,128]{4,3,2,1,0:T(8,128)(2,1)S(1)}, bf16[2,6,2,64,128]{4,3,2,1,0:T(8,128)(2,1)S(1)}, u32[]{:S(2)}, u32[]{:S(2)}) %collective-permute-start.5) | collective-permute-done | bytes 393248 | tf_op jit(solution)/shard_map/ppermute | solution.py:159
  59.7 8.4 %collective-permute-done.4.over_z = bf16[2,6,2,64,128]{4,3,2,1,0:T(8,128)(2,1)S(1)} collective-permute-done((bf16[2,6,2,64,128]{4,3,2,1,0:T(8,128)(2,1)S(1)}, bf16[2,6,2,64,128]{4,3,2,1,0:T(8,128)(2,1)S(1)}, u32[]{:S(2)}, u32[]{:S(2)}) %collective-permute-start.4) | collective-permute-done | bytes 393248 | tf_op jit(solution)/shard_map/ppermute | solution.py:19
  68.2 4.5 %collective-permute-start.6 = (bf16[8,3,16,1536]{3,2,1,0:T(8,128)(2,1)S(1)}, bf16[8,3,16,1536]{3,2,1,0:T(8,128)(2,1)S(1)}, u32[]{:S(2)}, u32[]{:S(2)}) collective-permute-start(bf16[8,3,16,1536]{3,2,1,0:T(8,128)(2,1)S(1)} %all-to-all-done.1.mine), channel_id=1, source_target_pairs={{0,1},{1,0},{2,3},{3,2},{4,5},{5,4},{6,7},{7,6},{8,9},{9,8},{10,11... | collective-permute-start | bytes 3538952 | tf_op jit(solution)/shard_map/ppermute | solution.py:19
  72.9 0.9 pack.1.x_ref
  73.8 1.4 %collective-permute-done.6.other = bf16[8,3,16,1536]{3,2,1,0:T(8,128)(2,1)S(1)} collective-permute-done((bf16[8,3,16,1536]{3,2,1,0:T(8,128)(2,1)S(1)}, bf16[8,3,16,1536]{3,2,1,0:T(8,128)(2,1)S(1)}, u32[]{:S(2)}, u32[]{:S(2)}) %collective-permute-start.6) | collective-permute-done | bytes 1179680 | tf_op jit(solution)/shard_map/ppermute | solution.py:19
  75.2 6.6 %conv.1 = bf16[8,2,128,256]{3,2,1,0:T(8,128)(2,1)S(1)} custom-call(s32[4]{0:T(128)S(1)} %pad_add_fusion.at_ref, bf16[2,6,2,4,64,128]{5,4,3,2,1,0:T(8,128)(2,1)S(1)} %pack.1.x_ref, bf16[8,3,16,1536]{3,2,1,0:T(8,128)(2,1)S(1)} %all-to-all-done.1.mine, bf16[8,3,16,1536]{3,2,1,0:T(8,128)(2,1)S(1)} %collective-permute-done.6.other, ...), custom_call_target="tpu_custom_call" | custom-call | flops 4899999744 | bytes 6000000 | tf_op jit(solution)/shard_map/conv/pallas_call | solution.py:130
  81.8 18.7 %all_to_all.15 = bf16[8,2,128,256]{3,2,1,0:T(8,128)(2,1)S(1)} all-to-all(bf16[8,2,128,256]{3,2,1,0:T(8,128)(2,1)S(1)} %conv.1), channel_id=1, replica_groups=mesh['x1'=2,'x0'=2,'zh'=2,'y'=8,'zl1'=2,'zl0'=2,'k'=2] {'zl0','x1','x0'}, dimensions={0} | all-to-all | bytes 2097152 | tf_op jit(solution)/shard_map/all_to_all | solution.py:168
  100.8 0.5 copy.29
  101.3 1.0 reshape.68
  (30 shorter events, 2.2 us)
Async XLA Ops:
  0.0 15.3 %copy-start = (bf16[2,4,64,128]{3,2,1,0:T(8,128)(2,1)S(1)}, bf16[2,4,64,128]{3,2,1,0:T(8,128)(2,1)}, u32[]{:S(2)}) copy-start(bf16[2,4,64,128]{3,2,1,0:T(8,128)(2,1)} %param.3) | copy-start | bytes 393220
  0.9 20.8 %copy-start.1 = (f32[2048]{0:T(1024)S(1)}, f32[2048]{0:T(1024)}, u32[]{:S(2)}) copy-start(f32[2048]{0:T(1024)} %param.5) | copy-start | bytes 24580
  3.4 21.6 %all-to-all-start = ((bf16[16,3,3,2,2,128]{5,4,3,2,1,0:T(2,128)(2,1)}), bf16[16,3,3,2,2,128]{5,4,3,2,1,0:T(2,128)(2,1)S(1)}, u32[]{:S(2)}, u32[]{:S(2)}) async-start(bf16[16,3,3,2,2,128]{5,4,3,2,1,0:T(2,128)(2,1)} %bitcast.7), calls=%async_computation | async-start | bytes 294912 | tf_op jit(solution)/shard_map/all_to_all | solution.py:33
  15.4 7.7 %collective-permute-start = (bf16[1,2,64,128]{3,2,1,0:T(8,128)(2,1)S(1)}, bf16[1,2,64,128]{3,2,1,0:T(8,128)(2,1)S(1)}, u32[]{:S(2)}, u32[]{:S(2)}) collective-permute-start(bf16[1,2,64,128]{3,2,1,0:T(8,128)(2,1)S(1)} %get-tuple-element.21), channel_id=1, source_target_pairs={{0,1},{1,2},{2,3},{3,4},{4,5},{5,6},{6,7},{7,8},{8,9},{9,10},{10,1... | collective-permute-start | bytes 98312 | tf_op jit(solution)/shard_map/ppermute | solution.py:42
  19.8 5.2 %collective-permute-start.1 = (bf16[1,2,64,128]{3,2,1,0:T(8,128)(2,1)S(1)}, bf16[1,2,64,128]{3,2,1,0:T(8,128)(2,1)S(1)}, u32[]{:S(2)}, u32[]{:S(2)}) collective-permute-start(bf16[1,2,64,128]{3,2,1,0:T(8,128)(2,1)S(1)} %get-tuple-element.22), channel_id=1, source_target_pairs={{1,0},{2,1},{3,2},{4,3},{5,4},{6,5},{7,6},{8,7},{9,8},{10,9},{11,1... | collective-permute-start | bytes 98312 | tf_op jit(solution)/shard_map/ppermute | solution.py:43
  26.4 41.7 %all-to-all-start.1 = ((bf16[8,3,16,1536]{3,2,1,0:T(8,128)(2,1)}), bf16[8,3,16,1536]{3,2,1,0:T(8,128)(2,1)S(1)}, u32[]{:S(2)}, u32[]{:S(2)}) async-start(bf16[8,3,16,1536]{3,2,1,0:T(8,128)(2,1)} %broadcast_in_dim.25), calls=%async_computation.1 | async-start | bytes 2359296 | tf_op jit(solution)/shard_map/all_to_all | solution.py:156
  33.5 12.6 %collective-permute-start.2 = (bf16[6,2,64,128]{3,2,1,0:T(8,128)(2,1)S(1)}, bf16[6,2,64,128]{3,2,1,0:T(8,128)(2,1)S(1)}, u32[]{:S(2)}, u32[]{:S(2)}) collective-permute-start(bf16[6,2,64,128]{3,2,1,0:T(8,128)(2,1)S(1)} %pad_maximum_fusion.1), channel_id=1, source_target_pairs={{0,64},{64,0},{1,65},{65,1},{2,66},{66,2},{3,67},{67,3},{4,68},{68... | collective-permute-start | bytes 589832 | tf_op jit(solution)/shard_map/ppermute | solution.py:19
  46.1 13.6 %collective-permute-start.5 = (bf16[2,6,2,64,128]{4,3,2,1,0:T(8,128)(2,1)S(1)}, bf16[2,6,2,64,128]{4,3,2,1,0:T(8,128)(2,1)S(1)}, u32[]{:S(2)}, u32[]{:S(2)}) collective-permute-start(bf16[2,6,2,64,128]{4,3,2,1,0:T(8,128)(2,1)S(1)} %pad_maximum_fusion.here), channel_id=1, source_target_pairs={{0,130},{2,128},{128,2},{130,0},{1,131},{3,129},{129,3},{131,1},{4... | collective-permute-start | bytes 1179656 | tf_op jit(solution)/shard_map/ppermute | solution.py:159
  51.9 16.3 %collective-permute-start.4 = (bf16[2,6,2,64,128]{4,3,2,1,0:T(8,128)(2,1)S(1)}, bf16[2,6,2,64,128]{4,3,2,1,0:T(8,128)(2,1)S(1)}, u32[]{:S(2)}, u32[]{:S(2)}) collective-permute-start(bf16[2,6,2,64,128]{4,3,2,1,0:T(8,128)(2,1)S(1)} %pad_maximum_fusion.here), channel_id=1, source_target_pairs={{0,2},{2,0},{1,3},{3,1},{4,6},{6,4},{5,7},{7,5},{8,10},{10,8},{9,1... | collective-permute-start | bytes 1179656 | tf_op jit(solution)/shard_map/ppermute | solution.py:19
  54.1 14.1 %collective-permute-start.3 = (bf16[2,6,2,64,128]{4,3,2,1,0:T(8,128)(2,1)S(1)}, bf16[2,6,2,64,128]{4,3,2,1,0:T(8,128)(2,1)S(1)}, u32[]{:S(2)}, u32[]{:S(2)}) collective-permute-start(bf16[2,6,2,64,128]{4,3,2,1,0:T(8,128)(2,1)S(1)} %pad_maximum_fusion.here), channel_id=1, source_target_pairs={{0,128},{128,0},{1,129},{129,1},{2,130},{130,2},{3,131},{131,3},{4... | collective-permute-start | bytes 1179656 | tf_op jit(solution)/shard_map/ppermute | solution.py:19
  68.2 7.0 %collective-permute-start.6 = (bf16[8,3,16,1536]{3,2,1,0:T(8,128)(2,1)S(1)}, bf16[8,3,16,1536]{3,2,1,0:T(8,128)(2,1)S(1)}, u32[]{:S(2)}, u32[]{:S(2)}) collective-permute-start(bf16[8,3,16,1536]{3,2,1,0:T(8,128)(2,1)S(1)} %all-to-all-done.1.mine), channel_id=1, source_target_pairs={{0,1},{1,0},{2,3},{3,2},{4,5},{5,4},{6,7},{7,6},{8,9},{9,8},{10,11... | collective-permute-start | bytes 3538952 | tf_op jit(solution)/shard_map/ppermute | solution.py:19

commit v8 on v7

--- a/solution.py
+++ b/solution.py
@@ -19,11 +19,29 @@
     return lax.ppermute(array, axis, ring(2, 1))
 
 
+def sum_kernel(taps_ref, out_ref):
+    for b in range(3):
+        for c in range(3):
+            k01 = taps_ref[0, b, c].astype(jnp.float32) + taps_ref[1, b, c].astype(jnp.float32)
+            k2 = taps_ref[2, b, c].astype(jnp.float32)
+            out_ref[b, c] = jnp.concatenate([k01, k2], axis=1).astype(jnp.bfloat16)
+
+
+def sum_taps(taps):
+    return pl.pallas_call(
+        sum_kernel,
+        out_shape=jax.ShapeDtypeStruct((3, 3, 32, 128), jnp.bfloat16),
+        in_specs=[pl.BlockSpec(memory_space=pltpu.VMEM)],
+        out_specs=pl.BlockSpec(memory_space=pltpu.VMEM),
+        compiler_params=pltpu.CompilerParams(vmem_limit_bytes=4 * 1024 * 1024),
+        name="sum_taps",
+    )(taps)
+
+
 def spread_kernel(kernel):
-    k01 = (kernel[0].astype(jnp.float32) + kernel[1].astype(jnp.float32)).astype(kernel.dtype)
-    both = jnp.stack([k01, kernel[2]])
-    split = both.reshape(2, 3, 3, 64, 2, 2, 2, 2, 2)
-    moved = jnp.transpose(split, (4, 7, 5, 1, 2, 8, 6, 0, 3))
+    both = sum_taps(jnp.swapaxes(kernel, 3, 4))
+    split = both.reshape(3, 3, 2, 2, 2, 2, 2, 128)
+    moved = jnp.transpose(split, (2, 5, 3, 0, 1, 6, 4, 7))
     flat = moved.reshape(2, 2, 1, 2, 3, 3, 2, 2, 128)
     return jnp.broadcast_to(flat, (2, 2, 2, 2, 3, 3, 2, 2, 128))
 

time: 103 us -> 102 us (level)
  waiting for transfers between devices: 21.8 us -> 19.2 us
  starting transfers between devices: 45.8 us -> 48.3 us
  other arithmetic: 1.74 us -> 0.39 us
    ppermute x4, waiting for transfers between devices: 16.3 us -> 13.9 us  [swap(): return lax.ppermute(array, axis, ring(2, 1))]
    unnamed x5, local copies, waits for them, and re-layouts: 0.02 us -> 1.85 us
    ppermute x1, starting transfers between devices: 5.74 us -> 7.37 us  [local(): lax.ppermute(rows, ('x0', 'zl0'), [(i, 3 - i) for i in range(4)])]
  transfers between devices with their start and end apart: 9 -> 9, of which waited for: 6 -> 5; matrix products, arithmetic and copies ran while one was open for 2% -> 3% of each run, Pallas kernels for 1% -> 1%
where the time goes in v8:
time: 102 us; the launch traced here: 101 us
  starting transfers between devices  48.3 us (47%)
  waiting for transfers between devices  19.2 us (19%)
  blocking collectives  18.5 us (18%)
  Pallas kernels  7.52 us (7%)
  local copies, waits for them, and re-layouts  7.09 us (7%)
    all_to_all x1, blocking collectives, local(): lax.all_to_all(out, ('zl0', 'x1', 'x0'), 0, 0, tiled=True)  18.5 us
    ppermute x4, starting transfers between devices, swap(): return lax.ppermute(array, axis, ring(2, 1))  15.7 us
    ppermute x4, waiting for transfers between devices, swap(): return lax.ppermute(array, axis, ring(2, 1))  13.9 us
    all_to_all x1, starting transfers between devices, own_chunk(): got = lax.all_to_all(pieces, ('x0', 'zh', 'zl1', 'zl0'), 0, 0, tiled=True)  11.9 us
    ppermute x1, starting transfers between devices, local(): lax.ppermute(rows, ('x0', 'zl0'), [(i, 3 - i) for i in range(4)])  7.37 us
    all_to_all x1, starting transfers between devices, local(): lax.all_to_all(jnp.broadcast_to(own, (NY, *own.shape)), 'y', 0, 0, tiled=...  6.95 us
    pallas_call x1, Pallas kernels, convolve(): pl.pallas_call(conv_kernel, out_shape=jax.ShapeDtypeStruct((8, 2, 128, 25...  6.56 us
    ppermute x1, starting transfers between devices, own_rows(): above = lax.ppermute(rows[3:], tile, up)  4.39 us
  transfers between devices with their start and end apart: 9, of which 5 were waited for; matrix products, arithmetic and copies ran while one was open for 3% of the time, Pallas kernels for 1%

profile of v8, /device:TPU:1, one launch (start us, length us, event | category | flops | bytes accessed | tf_op | source)
XLA Modules:
  0.0 101.2 jit_solution(6011078717922983605)
XLA Ops:
  0.0 0.9 copy-done
  1.1 0.7 broadcast_in_dim.10
  1.8 11.9 %all-to-all-start = ((bf16[16,3,3,2,2,128]{5,4,3,2,1,0:T(2,128)(2,1)}), bf16[16,3,3,2,2,128]{5,4,3,2,1,0:T(2,128)(2,1)S(1)}, u32[]{:S(2)}, u32[]{:S(2)}) async-start(bf16[16,3,3,2,2,128]{5,4,3,2,1,0:T(2,128)(2,1)} %bitcast.7), calls=%async_computation | async-start | bytes 294912 | tf_op jit(solution)/shard_map/all_to_all | solution.py:51
  13.7 0.9 copy.26
  14.7 4.4 %collective-permute-start = (bf16[1,2,64,128]{3,2,1,0:T(8,128)(2,1)S(1)}, bf16[1,2,64,128]{3,2,1,0:T(8,128)(2,1)S(1)}, u32[]{:S(2)}, u32[]{:S(2)}) collective-permute-start(bf16[1,2,64,128]{3,2,1,0:T(8,128)(2,1)S(1)} %get-tuple-element.21), channel_id=1, source_target_pairs={{0,1},{1,2},{2,3},{3,4},{4,5},{5,6},{6,7},{7,8},{8,9},{9,10},{10,1... | collective-permute-start | bytes 98312 | tf_op jit(solution)/shard_map/ppermute | solution.py:60
  19.1 1.9 %collective-permute-start.1 = (bf16[1,2,64,128]{3,2,1,0:T(8,128)(2,1)S(1)}, bf16[1,2,64,128]{3,2,1,0:T(8,128)(2,1)S(1)}, u32[]{:S(2)}, u32[]{:S(2)}) collective-permute-start(bf16[1,2,64,128]{3,2,1,0:T(8,128)(2,1)S(1)} %get-tuple-element.22), channel_id=1, source_target_pairs={{1,0},{2,1},{3,2},{4,3},{5,4},{6,5},{7,6},{8,7},{9,8},{10,9},{11,1... | collective-permute-start | bytes 98312 | tf_op jit(solution)/shard_map/ppermute | solution.py:61
  21.0 0.8 reshape.67
  22.4 1.9 %collective-permute-done.1 = bf16[1,2,64,128]{3,2,1,0:T(8,128)(2,1)S(1)} collective-permute-done((bf16[1,2,64,128]{3,2,1,0:T(8,128)(2,1)S(1)}, bf16[1,2,64,128]{3,2,1,0:T(8,128)(2,1)S(1)}, u32[]{:S(2)}, u32[]{:S(2)}) %collective-permute-start.1) | collective-permute-done | bytes 32800 | tf_op jit(solution)/shard_map/ppermute | solution.py:61
  24.6 1.2 %broadcast_in_dim.22 = bf16[8,3,16,1536]{3,2,1,0:T(8,128)(2,1)} broadcast(bf16[3,16,1536]{2,1,0:T(8,128)(2,1)S(1)} %reshape.66), dimensions={1,2,3} | broadcast | bytes 1327104 | tf_op jit(solution)/shard_map/broadcast_in_dim | solution.py:174
  25.8 6.9 %all-to-all-start.1 = ((bf16[8,3,16,1536]{3,2,1,0:T(8,128)(2,1)}), bf16[8,3,16,1536]{3,2,1,0:T(8,128)(2,1)S(1)}, u32[]{:S(2)}, u32[]{:S(2)}) async-start(bf16[8,3,16,1536]{3,2,1,0:T(8,128)(2,1)} %broadcast_in_dim.22), calls=%async_computation.1 | async-start | bytes 2359296 | tf_op jit(solution)/shard_map/all_to_all | solution.py:174
  32.7 6.3 %collective-permute-start.2 = (bf16[6,2,64,128]{3,2,1,0:T(8,128)(2,1)S(1)}, bf16[6,2,64,128]{3,2,1,0:T(8,128)(2,1)S(1)}, u32[]{:S(2)}, u32[]{:S(2)}) collective-permute-start(bf16[6,2,64,128]{3,2,1,0:T(8,128)(2,1)S(1)} %pad_maximum_fusion.1), channel_id=1, source_target_pairs={{0,64},{64,0},{1,65},{65,1},{2,66},{66,2},{3,67},{67,3},{4,68},{68... | collective-permute-start | bytes 589832 | tf_op jit(solution)/shard_map/ppermute | solution.py:19
  39.0 4.1 %collective-permute-done.2 = bf16[6,2,64,128]{3,2,1,0:T(8,128)(2,1)S(1)} collective-permute-done((bf16[6,2,64,128]{3,2,1,0:T(8,128)(2,1)S(1)}, bf16[6,2,64,128]{3,2,1,0:T(8,128)(2,1)S(1)}, u32[]{:S(2)}, u32[]{:S(2)}) %collective-permute-start.2) | collective-permute-done | bytes 196640 | tf_op jit(solution)/shard_map/ppermute | solution.py:19
  43.2 7.4 %collective-permute-start.5 = (bf16[2,6,2,64,128]{4,3,2,1,0:T(8,128)(2,1)S(1)}, bf16[2,6,2,64,128]{4,3,2,1,0:T(8,128)(2,1)S(1)}, u32[]{:S(2)}, u32[]{:S(2)}) collective-permute-start(bf16[2,6,2,64,128]{4,3,2,1,0:T(8,128)(2,1)S(1)} %pad_maximum_fusion.here), channel_id=1, source_target_pairs={{0,130},{2,128},{128,2},{130,0},{1,131},{3,129},{129,3},{131,1},{4... | collective-permute-start | bytes 1179656 | tf_op jit(solution)/shard_map/ppermute | solution.py:177
  50.6 2.8 %collective-permute-start.4 = (bf16[2,6,2,64,128]{4,3,2,1,0:T(8,128)(2,1)S(1)}, bf16[2,6,2,64,128]{4,3,2,1,0:T(8,128)(2,1)S(1)}, u32[]{:S(2)}, u32[]{:S(2)}) collective-permute-start(bf16[2,6,2,64,128]{4,3,2,1,0:T(8,128)(2,1)S(1)} %pad_maximum_fusion.here), channel_id=1, source_target_pairs={{0,2},{2,0},{1,3},{3,1},{4,6},{6,4},{5,7},{7,5},{8,10},{10,8},{9,1... | collective-permute-start | bytes 1179656 | tf_op jit(solution)/shard_map/ppermute | solution.py:19
  53.4 1.9 %collective-permute-start.3 = (bf16[2,6,2,64,128]{4,3,2,1,0:T(8,128)(2,1)S(1)}, bf16[2,6,2,64,128]{4,3,2,1,0:T(8,128)(2,1)S(1)}, u32[]{:S(2)}, u32[]{:S(2)}) collective-permute-start(bf16[2,6,2,64,128]{4,3,2,1,0:T(8,128)(2,1)S(1)} %pad_maximum_fusion.here), channel_id=1, source_target_pairs={{0,128},{128,0},{1,129},{129,1},{2,130},{130,2},{3,131},{131,3},{4... | collective-permute-start | bytes 1179656 | tf_op jit(solution)/shard_map/ppermute | solution.py:19
  55.3 3.4 %collective-permute-done.5.over_both = bf16[2,6,2,64,128]{4,3,2,1,0:T(8,128)(2,1)S(1)} collective-permute-done((bf16[2,6,2,64,128]{4,3,2,1,0:T(8,128)(2,1)S(1)}, bf16[2,6,2,64,128]{4,3,2,1,0:T(8,128)(2,1)S(1)}, u32[]{:S(2)}, u32[]{:S(2)}) %collective-permute-start.5) | collective-permute-done | bytes 393248 | tf_op jit(solution)/shard_map/ppermute | solution.py:177
  58.7 8.4 %collective-permute-done.4.over_z = bf16[2,6,2,64,128]{4,3,2,1,0:T(8,128)(2,1)S(1)} collective-permute-done((bf16[2,6,2,64,128]{4,3,2,1,0:T(8,128)(2,1)S(1)}, bf16[2,6,2,64,128]{4,3,2,1,0:T(8,128)(2,1)S(1)}, u32[]{:S(2)}, u32[]{:S(2)}) %collective-permute-start.4) | collective-permute-done | bytes 393248 | tf_op jit(solution)/shard_map/ppermute | solution.py:19
  67.1 4.7 %collective-permute-start.6 = (bf16[8,3,16,1536]{3,2,1,0:T(8,128)(2,1)S(1)}, bf16[8,3,16,1536]{3,2,1,0:T(8,128)(2,1)S(1)}, u32[]{:S(2)}, u32[]{:S(2)}) collective-permute-start(bf16[8,3,16,1536]{3,2,1,0:T(8,128)(2,1)S(1)} %all-to-all-done.1.mine), channel_id=1, source_target_pairs={{0,1},{1,0},{2,3},{3,2},{4,5},{5,4},{6,7},{7,6},{8,9},{9,8},{10,11... | collective-permute-start | bytes 3538952 | tf_op jit(solution)/shard_map/ppermute | solution.py:19
  72.1 0.9 pack.1.x_ref
  72.9 1.4 %collective-permute-done.6.other = bf16[8,3,16,1536]{3,2,1,0:T(8,128)(2,1)S(1)} collective-permute-done((bf16[8,3,16,1536]{3,2,1,0:T(8,128)(2,1)S(1)}, bf16[8,3,16,1536]{3,2,1,0:T(8,128)(2,1)S(1)}, u32[]{:S(2)}, u32[]{:S(2)}) %collective-permute-start.6) | collective-permute-done | bytes 1179680 | tf_op jit(solution)/shard_map/ppermute | solution.py:19
  74.3 6.6 %conv.1 = bf16[8,2,128,256]{3,2,1,0:T(8,128)(2,1)S(1)} custom-call(s32[4]{0:T(128)S(1)} %pad_add_fusion.at_ref, bf16[2,6,2,4,64,128]{5,4,3,2,1,0:T(8,128)(2,1)S(1)} %pack.1.x_ref, bf16[8,3,16,1536]{3,2,1,0:T(8,128)(2,1)S(1)} %all-to-all-done.1.mine, bf16[8,3,16,1536]{3,2,1,0:T(8,128)(2,1)S(1)} %collective-permute-done.6.other, ...), custom_call_target="tpu_custom_call" | custom-call | flops 4899999744 | bytes 6000000 | tf_op jit(solution)/shard_map/conv/pallas_call | solution.py:148
  80.9 18.5 %all_to_all.15 = bf16[8,2,128,256]{3,2,1,0:T(8,128)(2,1)S(1)} all-to-all(bf16[8,2,128,256]{3,2,1,0:T(8,128)(2,1)S(1)} %conv.1), channel_id=1, replica_groups=mesh['x1'=2,'x0'=2,'zh'=2,'y'=8,'zl1'=2,'zl0'=2,'k'=2] {'zl0','x1','x0'}, dimensions={0} | all-to-all | bytes 2097152 | tf_op jit(solution)/shard_map/all_to_all | solution.py:186
  99.7 0.5 copy.25
  100.2 1.0 reshape.69
  (26 shorter events, 1.6 us)
Async XLA Ops:
  0.0 0.9 copy-start
  0.9 20.1 %copy-start.1 = (f32[2048]{0:T(1024)S(1)}, f32[2048]{0:T(1024)}, u32[]{:S(2)}) copy-start(f32[2048]{0:T(1024)} %param.5) | copy-start | bytes 24580
  1.8 22.5 %all-to-all-start = ((bf16[16,3,3,2,2,128]{5,4,3,2,1,0:T(2,128)(2,1)}), bf16[16,3,3,2,2,128]{5,4,3,2,1,0:T(2,128)(2,1)S(1)}, u32[]{:S(2)}, u32[]{:S(2)}) async-start(bf16[16,3,3,2,2,128]{5,4,3,2,1,0:T(2,128)(2,1)} %bitcast.7), calls=%async_computation | async-start | bytes 294912 | tf_op jit(solution)/shard_map/all_to_all | solution.py:51
  14.7 7.7 %collective-permute-start = (bf16[1,2,64,128]{3,2,1,0:T(8,128)(2,1)S(1)}, bf16[1,2,64,128]{3,2,1,0:T(8,128)(2,1)S(1)}, u32[]{:S(2)}, u32[]{:S(2)}) collective-permute-start(bf16[1,2,64,128]{3,2,1,0:T(8,128)(2,1)S(1)} %get-tuple-element.21), channel_id=1, source_target_pairs={{0,1},{1,2},{2,3},{3,4},{4,5},{5,6},{6,7},{7,8},{8,9},{9,10},{10,1... | collective-permute-start | bytes 98312 | tf_op jit(solution)/shard_map/ppermute | solution.py:60
  19.1 5.2 %collective-permute-start.1 = (bf16[1,2,64,128]{3,2,1,0:T(8,128)(2,1)S(1)}, bf16[1,2,64,128]{3,2,1,0:T(8,128)(2,1)S(1)}, u32[]{:S(2)}, u32[]{:S(2)}) collective-permute-start(bf16[1,2,64,128]{3,2,1,0:T(8,128)(2,1)S(1)} %get-tuple-element.22), channel_id=1, source_target_pairs={{1,0},{2,1},{3,2},{4,3},{5,4},{6,5},{7,6},{8,7},{9,8},{10,9},{11,1... | collective-permute-start | bytes 98312 | tf_op jit(solution)/shard_map/ppermute | solution.py:61
  25.8 41.4 %all-to-all-start.1 = ((bf16[8,3,16,1536]{3,2,1,0:T(8,128)(2,1)}), bf16[8,3,16,1536]{3,2,1,0:T(8,128)(2,1)S(1)}, u32[]{:S(2)}, u32[]{:S(2)}) async-start(bf16[8,3,16,1536]{3,2,1,0:T(8,128)(2,1)} %broadcast_in_dim.22), calls=%async_computation.1 | async-start | bytes 2359296 | tf_op jit(solution)/shard_map/all_to_all | solution.py:174
  32.7 10.4 %collective-permute-start.2 = (bf16[6,2,64,128]{3,2,1,0:T(8,128)(2,1)S(1)}, bf16[6,2,64,128]{3,2,1,0:T(8,128)(2,1)S(1)}, u32[]{:S(2)}, u32[]{:S(2)}) collective-permute-start(bf16[6,2,64,128]{3,2,1,0:T(8,128)(2,1)S(1)} %pad_maximum_fusion.1), channel_id=1, source_target_pairs={{0,64},{64,0},{1,65},{65,1},{2,66},{66,2},{3,67},{67,3},{4,68},{68... | collective-permute-start | bytes 589832 | tf_op jit(solution)/shard_map/ppermute | solution.py:19
  43.2 15.5 %collective-permute-start.5 = (bf16[2,6,2,64,128]{4,3,2,1,0:T(8,128)(2,1)S(1)}, bf16[2,6,2,64,128]{4,3,2,1,0:T(8,128)(2,1)S(1)}, u32[]{:S(2)}, u32[]{:S(2)}) collective-permute-start(bf16[2,6,2,64,128]{4,3,2,1,0:T(8,128)(2,1)S(1)} %pad_maximum_fusion.here), channel_id=1, source_target_pairs={{0,130},{2,128},{128,2},{130,0},{1,131},{3,129},{129,3},{131,1},{4... | collective-permute-start | bytes 1179656 | tf_op jit(solution)/shard_map/ppermute | solution.py:177
  50.6 16.6 %collective-permute-start.4 = (bf16[2,6,2,64,128]{4,3,2,1,0:T(8,128)(2,1)S(1)}, bf16[2,6,2,64,128]{4,3,2,1,0:T(8,128)(2,1)S(1)}, u32[]{:S(2)}, u32[]{:S(2)}) collective-permute-start(bf16[2,6,2,64,128]{4,3,2,1,0:T(8,128)(2,1)S(1)} %pad_maximum_fusion.here), channel_id=1, source_target_pairs={{0,2},{2,0},{1,3},{3,1},{4,6},{6,4},{5,7},{7,5},{8,10},{10,8},{9,1... | collective-permute-start | bytes 1179656 | tf_op jit(solution)/shard_map/ppermute | solution.py:19
  53.4 13.7 %collective-permute-start.3 = (bf16[2,6,2,64,128]{4,3,2,1,0:T(8,128)(2,1)S(1)}, bf16[2,6,2,64,128]{4,3,2,1,0:T(8,128)(2,1)S(1)}, u32[]{:S(2)}, u32[]{:S(2)}) collective-permute-start(bf16[2,6,2,64,128]{4,3,2,1,0:T(8,128)(2,1)S(1)} %pad_maximum_fusion.here), channel_id=1, source_target_pairs={{0,128},{128,0},{1,129},{129,1},{2,130},{130,2},{3,131},{131,3},{4... | collective-permute-start | bytes 1179656 | tf_op jit(solution)/shard_map/ppermute | solution.py:19
  67.1 7.2 %collective-permute-start.6 = (bf16[8,3,16,1536]{3,2,1,0:T(8,128)(2,1)S(1)}, bf16[8,3,16,1536]{3,2,1,0:T(8,128)(2,1)S(1)}, u32[]{:S(2)}, u32[]{:S(2)}) collective-permute-start(bf16[8,3,16,1536]{3,2,1,0:T(8,128)(2,1)S(1)} %all-to-all-done.1.mine), channel_id=1, source_target_pairs={{0,1},{1,0},{2,3},{3,2},{4,5},{5,4},{6,7},{7,6},{8,9},{9,8},{10,11... | collective-permute-start | bytes 3538952 | tf_op jit(solution)/shard_map/ppermute | solution.py:19

commit v9 on v8

--- a/solution.py
+++ b/solution.py
@@ -128,7 +128,7 @@
         mixed = jnp.concatenate(mixed, axis=0).astype(jnp.bfloat16)
         mixed = jnp.dot(mixed, perm_ref[...], preferred_element_type=jnp.float32).astype(jnp.bfloat16)
         for q in range(ROWS):
-            out_ref[4 * z + row + q, frame] = mixed[128 * q : 128 * q + 128]
+            out_ref[2 * (row + q) + z, frame] = mixed[128 * q : 128 * q + 128]
 
     def step(i, carry):
         n = 2 * i
@@ -183,10 +183,10 @@
     place = jnp.arange(256)
     perm = ((2 * (place % 128) + place // 128)[:, None] == place[None, :]).astype(jnp.bfloat16)
     out = convolve(at, packed, (mine, other), column, perm)
-    got = lax.all_to_all(out, ("zl0", "x1", "x0"), 0, 0, tiled=True).reshape(2, 2, 2, 2, 128, 256)
-    total = (got[:, 0].astype(jnp.float32) + got[:, 1].astype(jnp.float32)).astype(jnp.bfloat16)
+    got = lax.all_to_all(out, ("x1", "x0", "zl0"), 0, 0, tiled=True).reshape(2, 2, 2, 2, 128, 256)
+    total = (got[0].astype(jnp.float32) + got[1].astype(jnp.float32)).astype(jnp.bfloat16)
     total = total.reshape(2, 2, 2, NY, 2, 4, 2, 256)
-    return jnp.transpose(total, (2, 3, 5, 4, 1, 0, 6, 7)).reshape(2, 1, 512, 256)
+    return jnp.transpose(total, (2, 3, 5, 4, 0, 1, 6, 7)).reshape(2, 1, 512, 256)
 
 
 def solution(mesh):

time: 102 us -> 102 us (level)
  no operation moved by 1% of the time
where the time goes in v9:
time: 102 us
  starting transfers between devices  48.3 us (47%)
  waiting for transfers between devices  19.2 us (19%)
  blocking collectives  18.9 us (19%)
  Pallas kernels  7.53 us (7%)
  local copies, waits for them, and re-layouts  7.09 us (7%)
    all_to_all x1, blocking collectives, local(): lax.all_to_all(out, ('x1', 'x0', 'zl0'), 0, 0, tiled=True)  18.9 us
    ppermute x4, starting transfers between devices, swap(): return lax.ppermute(array, axis, ring(2, 1))  15.7 us
    ppermute x4, waiting for transfers between devices, swap(): return lax.ppermute(array, axis, ring(2, 1))  13.9 us
    all_to_all x1, starting transfers between devices, own_chunk(): got = lax.all_to_all(pieces, ('x0', 'zh', 'zl1', 'zl0'), 0, 0, tiled=True)  11.9 us
    ppermute x1, starting transfers between devices, local(): lax.ppermute(rows, ('x0', 'zl0'), [(i, 3 - i) for i in range(4)])  7.37 us
    all_to_all x1, starting transfers between devices, local(): lax.all_to_all(jnp.broadcast_to(own, (NY, *own.shape)), 'y', 0, 0, tiled=...  6.95 us
    pallas_call x1, Pallas kernels, convolve(): pl.pallas_call(conv_kernel, out_shape=jax.ShapeDtypeStruct((8, 2, 128, 25...  6.57 us
    ppermute x1, starting transfers between devices, own_rows(): above = lax.ppermute(rows[3:], tile, up)  4.39 us
  transfers between devices with their start and end apart: 9, of which 5 were waited for; matrix products, arithmetic and copies ran while one was open for 3% of the time, Pallas kernels for 1%

profile of v9, /device:TPU:1, one launch (start us, length us, event | category | flops | bytes accessed | tf_op | source)
XLA Modules:
  0.0 101.6 jit_solution(3669759320854685667)
XLA Ops:
  0.0 0.9 copy-done
  1.1 0.7 broadcast_in_dim.10
  1.8 11.9 %all-to-all-start = ((bf16[16,3,3,2,2,128]{5,4,3,2,1,0:T(2,128)(2,1)}), bf16[16,3,3,2,2,128]{5,4,3,2,1,0:T(2,128)(2,1)S(1)}, u32[]{:S(2)}, u32[]{:S(2)}) async-start(bf16[16,3,3,2,2,128]{5,4,3,2,1,0:T(2,128)(2,1)} %bitcast.7), calls=%async_computation | async-start | bytes 294912 | tf_op jit(solution)/shard_map/all_to_all | solution.py:51
  13.7 0.9 copy.24
  14.7 4.4 %collective-permute-start = (bf16[1,2,64,128]{3,2,1,0:T(8,128)(2,1)S(1)}, bf16[1,2,64,128]{3,2,1,0:T(8,128)(2,1)S(1)}, u32[]{:S(2)}, u32[]{:S(2)}) collective-permute-start(bf16[1,2,64,128]{3,2,1,0:T(8,128)(2,1)S(1)} %get-tuple-element.21), channel_id=1, source_target_pairs={{0,1},{1,2},{2,3},{3,4},{4,5},{5,6},{6,7},{7,8},{8,9},{9,10},{10,1... | collective-permute-start | bytes 98312 | tf_op jit(solution)/shard_map/ppermute | solution.py:60
  19.1 1.9 %collective-permute-start.1 = (bf16[1,2,64,128]{3,2,1,0:T(8,128)(2,1)S(1)}, bf16[1,2,64,128]{3,2,1,0:T(8,128)(2,1)S(1)}, u32[]{:S(2)}, u32[]{:S(2)}) collective-permute-start(bf16[1,2,64,128]{3,2,1,0:T(8,128)(2,1)S(1)} %get-tuple-element.22), channel_id=1, source_target_pairs={{1,0},{2,1},{3,2},{4,3},{5,4},{6,5},{7,6},{8,7},{9,8},{10,9},{11,1... | collective-permute-start | bytes 98312 | tf_op jit(solution)/shard_map/ppermute | solution.py:61
  21.0 0.8 reshape.69
  22.4 1.9 %collective-permute-done.1 = bf16[1,2,64,128]{3,2,1,0:T(8,128)(2,1)S(1)} collective-permute-done((bf16[1,2,64,128]{3,2,1,0:T(8,128)(2,1)S(1)}, bf16[1,2,64,128]{3,2,1,0:T(8,128)(2,1)S(1)}, u32[]{:S(2)}, u32[]{:S(2)}) %collective-permute-start.1) | collective-permute-done | bytes 32800 | tf_op jit(solution)/shard_map/ppermute | solution.py:61
  24.6 1.2 %broadcast_in_dim.22 = bf16[8,3,16,1536]{3,2,1,0:T(8,128)(2,1)} broadcast(bf16[3,16,1536]{2,1,0:T(8,128)(2,1)S(1)} %reshape.68), dimensions={1,2,3} | broadcast | bytes 1327104 | tf_op jit(solution)/shard_map/broadcast_in_dim | solution.py:174
  25.8 6.9 %all-to-all-start.1 = ((bf16[8,3,16,1536]{3,2,1,0:T(8,128)(2,1)}), bf16[8,3,16,1536]{3,2,1,0:T(8,128)(2,1)S(1)}, u32[]{:S(2)}, u32[]{:S(2)}) async-start(bf16[8,3,16,1536]{3,2,1,0:T(8,128)(2,1)} %broadcast_in_dim.22), calls=%async_computation.1 | async-start | bytes 2359296 | tf_op jit(solution)/shard_map/all_to_all | solution.py:174
  32.7 6.3 %collective-permute-start.2 = (bf16[6,2,64,128]{3,2,1,0:T(8,128)(2,1)S(1)}, bf16[6,2,64,128]{3,2,1,0:T(8,128)(2,1)S(1)}, u32[]{:S(2)}, u32[]{:S(2)}) collective-permute-start(bf16[6,2,64,128]{3,2,1,0:T(8,128)(2,1)S(1)} %pad_maximum_fusion.1), channel_id=1, source_target_pairs={{0,64},{64,0},{1,65},{65,1},{2,66},{66,2},{3,67},{67,3},{4,68},{68... | collective-permute-start | bytes 589832 | tf_op jit(solution)/shard_map/ppermute | solution.py:19
  39.0 4.1 %collective-permute-done.2 = bf16[6,2,64,128]{3,2,1,0:T(8,128)(2,1)S(1)} collective-permute-done((bf16[6,2,64,128]{3,2,1,0:T(8,128)(2,1)S(1)}, bf16[6,2,64,128]{3,2,1,0:T(8,128)(2,1)S(1)}, u32[]{:S(2)}, u32[]{:S(2)}) %collective-permute-start.2) | collective-permute-done | bytes 196640 | tf_op jit(solution)/shard_map/ppermute | solution.py:19
  43.2 7.4 %collective-permute-start.5 = (bf16[2,6,2,64,128]{4,3,2,1,0:T(8,128)(2,1)S(1)}, bf16[2,6,2,64,128]{4,3,2,1,0:T(8,128)(2,1)S(1)}, u32[]{:S(2)}, u32[]{:S(2)}) collective-permute-start(bf16[2,6,2,64,128]{4,3,2,1,0:T(8,128)(2,1)S(1)} %pad_maximum_fusion.here), channel_id=1, source_target_pairs={{0,130},{2,128},{128,2},{130,0},{1,131},{3,129},{129,3},{131,1},{4... | collective-permute-start | bytes 1179656 | tf_op jit(solution)/shard_map/ppermute | solution.py:177
  50.6 2.8 %collective-permute-start.4 = (bf16[2,6,2,64,128]{4,3,2,1,0:T(8,128)(2,1)S(1)}, bf16[2,6,2,64,128]{4,3,2,1,0:T(8,128)(2,1)S(1)}, u32[]{:S(2)}, u32[]{:S(2)}) collective-permute-start(bf16[2,6,2,64,128]{4,3,2,1,0:T(8,128)(2,1)S(1)} %pad_maximum_fusion.here), channel_id=1, source_target_pairs={{0,2},{2,0},{1,3},{3,1},{4,6},{6,4},{5,7},{7,5},{8,10},{10,8},{9,1... | collective-permute-start | bytes 1179656 | tf_op jit(solution)/shard_map/ppermute | solution.py:19
  53.4 1.9 %collective-permute-start.3 = (bf16[2,6,2,64,128]{4,3,2,1,0:T(8,128)(2,1)S(1)}, bf16[2,6,2,64,128]{4,3,2,1,0:T(8,128)(2,1)S(1)}, u32[]{:S(2)}, u32[]{:S(2)}) collective-permute-start(bf16[2,6,2,64,128]{4,3,2,1,0:T(8,128)(2,1)S(1)} %pad_maximum_fusion.here), channel_id=1, source_target_pairs={{0,128},{128,0},{1,129},{129,1},{2,130},{130,2},{3,131},{131,3},{4... | collective-permute-start | bytes 1179656 | tf_op jit(solution)/shard_map/ppermute | solution.py:19
  55.3 3.4 %collective-permute-done.5.over_both = bf16[2,6,2,64,128]{4,3,2,1,0:T(8,128)(2,1)S(1)} collective-permute-done((bf16[2,6,2,64,128]{4,3,2,1,0:T(8,128)(2,1)S(1)}, bf16[2,6,2,64,128]{4,3,2,1,0:T(8,128)(2,1)S(1)}, u32[]{:S(2)}, u32[]{:S(2)}) %collective-permute-start.5) | collective-permute-done | bytes 393248 | tf_op jit(solution)/shard_map/ppermute | solution.py:177
  58.7 8.4 %collective-permute-done.4.over_z = bf16[2,6,2,64,128]{4,3,2,1,0:T(8,128)(2,1)S(1)} collective-permute-done((bf16[2,6,2,64,128]{4,3,2,1,0:T(8,128)(2,1)S(1)}, bf16[2,6,2,64,128]{4,3,2,1,0:T(8,128)(2,1)S(1)}, u32[]{:S(2)}, u32[]{:S(2)}) %collective-permute-start.4) | collective-permute-done | bytes 393248 | tf_op jit(solution)/shard_map/ppermute | solution.py:19
  67.1 4.7 %collective-permute-start.6 = (bf16[8,3,16,1536]{3,2,1,0:T(8,128)(2,1)S(1)}, bf16[8,3,16,1536]{3,2,1,0:T(8,128)(2,1)S(1)}, u32[]{:S(2)}, u32[]{:S(2)}) collective-permute-start(bf16[8,3,16,1536]{3,2,1,0:T(8,128)(2,1)S(1)} %all-to-all-done.1.mine), channel_id=1, source_target_pairs={{0,1},{1,0},{2,3},{3,2},{4,5},{5,4},{6,7},{7,6},{8,9},{9,8},{10,11... | collective-permute-start | bytes 3538952 | tf_op jit(solution)/shard_map/ppermute | solution.py:19
  72.1 0.9 pack.1.x_ref
  72.9 1.4 %collective-permute-done.6.other = bf16[8,3,16,1536]{3,2,1,0:T(8,128)(2,1)S(1)} collective-permute-done((bf16[8,3,16,1536]{3,2,1,0:T(8,128)(2,1)S(1)}, bf16[8,3,16,1536]{3,2,1,0:T(8,128)(2,1)S(1)}, u32[]{:S(2)}, u32[]{:S(2)}) %collective-permute-start.6) | collective-permute-done | bytes 1179680 | tf_op jit(solution)/shard_map/ppermute | solution.py:19
  74.3 6.6 %conv.1 = bf16[8,2,128,256]{3,2,1,0:T(8,128)(2,1)S(1)} custom-call(s32[4]{0:T(128)S(1)} %pad_add_fusion.at_ref, bf16[2,6,2,4,64,128]{5,4,3,2,1,0:T(8,128)(2,1)S(1)} %pack.1.x_ref, bf16[8,3,16,1536]{3,2,1,0:T(8,128)(2,1)S(1)} %all-to-all-done.1.mine, bf16[8,3,16,1536]{3,2,1,0:T(8,128)(2,1)S(1)} %collective-permute-done.6.other, ...), custom_call_target="tpu_custom_call" | custom-call | flops 4899999744 | bytes 6000000 | tf_op jit(solution)/shard_map/conv/pallas_call | solution.py:148
  80.9 18.9 %all_to_all.15 = bf16[8,2,128,256]{3,2,1,0:T(8,128)(2,1)S(1)} all-to-all(bf16[8,2,128,256]{3,2,1,0:T(8,128)(2,1)S(1)} %conv.1), channel_id=1, replica_groups=mesh['x1'=2,'x0'=2,'zh'=2,'y'=8,'zl1'=2,'zl0'=2,'k'=2] {'x1','x0','zl0'}, dimensions={0} | all-to-all | bytes 2097152 | tf_op jit(solution)/shard_map/all_to_all | solution.py:186
  100.1 0.5 copy.22
  100.6 1.0 reshape.70
  (26 shorter events, 1.6 us)
Async XLA Ops:
  0.0 0.9 copy-start
  0.9 20.1 %copy-start.1 = (f32[2048]{0:T(1024)S(1)}, f32[2048]{0:T(1024)}, u32[]{:S(2)}) copy-start(f32[2048]{0:T(1024)} %param.5) | copy-start | bytes 24580
  1.8 22.5 %all-to-all-start = ((bf16[16,3,3,2,2,128]{5,4,3,2,1,0:T(2,128)(2,1)}), bf16[16,3,3,2,2,128]{5,4,3,2,1,0:T(2,128)(2,1)S(1)}, u32[]{:S(2)}, u32[]{:S(2)}) async-start(bf16[16,3,3,2,2,128]{5,4,3,2,1,0:T(2,128)(2,1)} %bitcast.7), calls=%async_computation | async-start | bytes 294912 | tf_op jit(solution)/shard_map/all_to_all | solution.py:51
  14.7 7.7 %collective-permute-start = (bf16[1,2,64,128]{3,2,1,0:T(8,128)(2,1)S(1)}, bf16[1,2,64,128]{3,2,1,0:T(8,128)(2,1)S(1)}, u32[]{:S(2)}, u32[]{:S(2)}) collective-permute-start(bf16[1,2,64,128]{3,2,1,0:T(8,128)(2,1)S(1)} %get-tuple-element.21), channel_id=1, source_target_pairs={{0,1},{1,2},{2,3},{3,4},{4,5},{5,6},{6,7},{7,8},{8,9},{9,10},{10,1... | collective-permute-start | bytes 98312 | tf_op jit(solution)/shard_map/ppermute | solution.py:60
  19.1 5.2 %collective-permute-start.1 = (bf16[1,2,64,128]{3,2,1,0:T(8,128)(2,1)S(1)}, bf16[1,2,64,128]{3,2,1,0:T(8,128)(2,1)S(1)}, u32[]{:S(2)}, u32[]{:S(2)}) collective-permute-start(bf16[1,2,64,128]{3,2,1,0:T(8,128)(2,1)S(1)} %get-tuple-element.22), channel_id=1, source_target_pairs={{1,0},{2,1},{3,2},{4,3},{5,4},{6,5},{7,6},{8,7},{9,8},{10,9},{11,1... | collective-permute-start | bytes 98312 | tf_op jit(solution)/shard_map/ppermute | solution.py:61
  25.8 41.4 %all-to-all-start.1 = ((bf16[8,3,16,1536]{3,2,1,0:T(8,128)(2,1)}), bf16[8,3,16,1536]{3,2,1,0:T(8,128)(2,1)S(1)}, u32[]{:S(2)}, u32[]{:S(2)}) async-start(bf16[8,3,16,1536]{3,2,1,0:T(8,128)(2,1)} %broadcast_in_dim.22), calls=%async_computation.1 | async-start | bytes 2359296 | tf_op jit(solution)/shard_map/all_to_all | solution.py:174
  32.7 10.4 %collective-permute-start.2 = (bf16[6,2,64,128]{3,2,1,0:T(8,128)(2,1)S(1)}, bf16[6,2,64,128]{3,2,1,0:T(8,128)(2,1)S(1)}, u32[]{:S(2)}, u32[]{:S(2)}) collective-permute-start(bf16[6,2,64,128]{3,2,1,0:T(8,128)(2,1)S(1)} %pad_maximum_fusion.1), channel_id=1, source_target_pairs={{0,64},{64,0},{1,65},{65,1},{2,66},{66,2},{3,67},{67,3},{4,68},{68... | collective-permute-start | bytes 589832 | tf_op jit(solution)/shard_map/ppermute | solution.py:19
  43.2 15.5 %collective-permute-start.5 = (bf16[2,6,2,64,128]{4,3,2,1,0:T(8,128)(2,1)S(1)}, bf16[2,6,2,64,128]{4,3,2,1,0:T(8,128)(2,1)S(1)}, u32[]{:S(2)}, u32[]{:S(2)}) collective-permute-start(bf16[2,6,2,64,128]{4,3,2,1,0:T(8,128)(2,1)S(1)} %pad_maximum_fusion.here), channel_id=1, source_target_pairs={{0,130},{2,128},{128,2},{130,0},{1,131},{3,129},{129,3},{131,1},{4... | collective-permute-start | bytes 1179656 | tf_op jit(solution)/shard_map/ppermute | solution.py:177
  50.6 16.6 %collective-permute-start.4 = (bf16[2,6,2,64,128]{4,3,2,1,0:T(8,128)(2,1)S(1)}, bf16[2,6,2,64,128]{4,3,2,1,0:T(8,128)(2,1)S(1)}, u32[]{:S(2)}, u32[]{:S(2)}) collective-permute-start(bf16[2,6,2,64,128]{4,3,2,1,0:T(8,128)(2,1)S(1)} %pad_maximum_fusion.here), channel_id=1, source_target_pairs={{0,2},{2,0},{1,3},{3,1},{4,6},{6,4},{5,7},{7,5},{8,10},{10,8},{9,1... | collective-permute-start | bytes 1179656 | tf_op jit(solution)/shard_map/ppermute | solution.py:19
  53.4 13.7 %collective-permute-start.3 = (bf16[2,6,2,64,128]{4,3,2,1,0:T(8,128)(2,1)S(1)}, bf16[2,6,2,64,128]{4,3,2,1,0:T(8,128)(2,1)S(1)}, u32[]{:S(2)}, u32[]{:S(2)}) collective-permute-start(bf16[2,6,2,64,128]{4,3,2,1,0:T(8,128)(2,1)S(1)} %pad_maximum_fusion.here), channel_id=1, source_target_pairs={{0,128},{128,0},{1,129},{129,1},{2,130},{130,2},{3,131},{131,3},{4... | collective-permute-start | bytes 1179656 | tf_op jit(solution)/shard_map/ppermute | solution.py:19
  67.1 7.2 %collective-permute-start.6 = (bf16[8,3,16,1536]{3,2,1,0:T(8,128)(2,1)S(1)}, bf16[8,3,16,1536]{3,2,1,0:T(8,128)(2,1)S(1)}, u32[]{:S(2)}, u32[]{:S(2)}) collective-permute-start(bf16[8,3,16,1536]{3,2,1,0:T(8,128)(2,1)S(1)} %all-to-all-done.1.mine), channel_id=1, source_target_pairs={{0,1},{1,0},{2,3},{3,2},{4,5},{5,4},{6,7},{7,6},{8,9},{9,8},{10,11... | collective-permute-start | bytes 3538952 | tf_op jit(solution)/shard_map/ppermute | solution.py:19
